TPU v7x, 256 devices: a whole 4x4x8 slice. The times are simulated.
256 devices in a mesh: layer: 64 (over z, x, core), dp: 4 (over y).
Axes of the slice: x: 4, y: 4, z: 8, core: 2. Of those that a mesh axis runs over, the one named last changes fastest.
Arguments:
- states: bfloat16 [128, 4, 16, 16, 256], P('layer', 'dp'), may hold values from -6 to 6
- kernels: bfloat16 [128, 3, 3, 256, 256], P('layer'), may hold values from -0.125 to 0.125
- adjoint_guess: float32 [64, 4, 16, 16, 256], P('layer', 'dp'), may hold values from -6 to 6
- coarse_gain: float32 [64, 16, 16, 256], P('layer'), may hold values from 0 to 1, as said below
- terminal: float32 [4, 16, 16, 256], P('dp'), may hold values from -6 to 6
Outputs:
- adjoint: float32 [128, 4, 16, 16, 256], P('layer', 'dp')
- weight_grad: float32 [128, 3, 3, 256, 256], P('layer', None, None, None, 'dp')
Inputs may be any that keep to these rules, and one draw needn't show every extreme that they name: `coarse_gain`: strictly positive.
All inputs are finite; a program needn't handle non-finite values.
Results may differ from a plain program's by a relative error of at most 0.015.
Values may be sent and summed in bfloat16 or wider, within the bound.
No kernel may reach another device: no remote copies, remote signals or barrier semaphores. Data moves between devices by JAX's collectives and lax.ppermute only.
A program may use at most 128 MiB of HBM per device.

v0:
```python
import jax
import jax.numpy as jnp
from jax import lax
from jax.sharding import PartitionSpec as P

STEP = 0.5
DAMPING = 0.5


def shifted(block, axis, distance):
    devices = range(lax.axis_size(axis))
    route = [(i - distance, i) for i in devices if i - distance in devices]
    return lax.ppermute(block, axis, route)


def entering(shard, axis, combine, identity):
    count, here = (lax.axis_size(axis), lax.axis_index(axis))
    everything = jax.tree.map(lambda part: lax.all_gather(part, axis), shard)
    start = jax.tree.map(
        lambda part, zero: jnp.broadcast_to(jnp.asarray(zero, part.dtype), part.shape),
        shard,
        identity,
    )

    def turn(k, before):
        at = count - 1 - k
        reached = at > here
        new = combine(before, jax.tree.map(lambda part: part[at], everything))
        return jax.tree.map(lambda a, b: jnp.where(reached, a, b), new, before)

    return lax.fori_loop(0, count, turn, start)


def forward_conv(layer_state, kernel):
    return lax.conv_general_dilated(
        layer_state,
        kernel,
        (1, 1),
        "SAME",
        dimension_numbers=("NHWC", "HWIO", "NHWC"),
        preferred_element_type=jnp.float32,
    )


def adjoint_conv(signal, kernel):
    return lax.conv_general_dilated(
        signal,
        kernel[::-1, ::-1],
        (1, 1),
        "SAME",
        dimension_numbers=("NHWC", "HWOI", "NHWC"),
        preferred_element_type=jnp.float32,
    )


def sensitivity(layer_state, kernel):
    activation = jnp.tanh(forward_conv(layer_state, kernel))
    return 1.0 - activation * activation


def adjoint_step(carried, slopes, kernel):
    signal = (slopes * carried).astype(jnp.bfloat16)
    return carried + STEP * adjoint_conv(signal, kernel)


def relax(right_value, slopes, kernels, lowest):
    values = []
    carried = right_value
    for block_index in range(slopes.shape[0] - 1, lowest - 1, -1):
        carried = adjoint_step(carried, slopes[block_index], kernels[block_index])
        values.append(carried)
    return jnp.stack(values[::-1])


def tap_products(layer_state, signal):
    height = layer_state.shape[1]
    width = layer_state.shape[2]
    channels = layer_state.shape[3]
    padded = jnp.pad(layer_state, ((0, 0), (1, 1), (1, 1), (0, 0)))
    signal_rows = signal.reshape(-1, signal.shape[-1])
    tap_list = []
    for row_tap in range(3):
        for col_tap in range(3):
            patch_rows = padded[
                :, row_tap : row_tap + height, col_tap : col_tap + width, :
            ].reshape(-1, channels)
            tap_list.append(
                lax.dot_general(
                    patch_rows,
                    signal_rows,
                    (((0,), (0,)), ((), ())),
                    preferred_element_type=jnp.float32,
                )
            )
    return jnp.stack(tap_list).reshape(3, 3, channels, signal_rows.shape[-1])


def from_right(points, last_value, is_last):
    arriving = shifted(points, "layer", -1)
    return arriving + jnp.where(is_last, last_value, jnp.zeros_like(last_value))


def compose(earlier, later):
    return (later[0] * earlier[0], later[0][None] * earlier[1] + later[1])


def on_device(states, kernels, adjoint_guess, coarse_gain, terminal):
    is_last = lax.axis_index("layer") == lax.axis_size("layer") - 1
    per_slab = states.shape[0]
    slopes = jnp.stack(
        [sensitivity(states[index_block], kernels[index_block]) for index_block in range(per_slab)]
    )
    points = adjoint_guess[0]
    for sweep_index in range(2):
        points = points + DAMPING * (
            relax(from_right(points, terminal, is_last), slopes, kernels, 0)[0] - points
        )
    neighbours = from_right(points, terminal, is_last)
    residual = relax(neighbours, slopes, kernels, 0)[0] - points
    coupling_gain = coarse_gain[0]
    prefix = entering(
        (coupling_gain, residual),
        "layer",
        compose,
        (jnp.ones_like(coupling_gain), jnp.zeros_like(residual)),
    )
    corrected = points + (coupling_gain[None] * prefix[1] + residual)
    right_value = neighbours + prefix[1]
    inner_points = relax(right_value, slopes, kernels, 1)
    adjoint = jnp.concatenate([corrected[None], inner_points], 0)
    following = jnp.concatenate([adjoint[1:], right_value[None]], 0)
    signals = (slopes * following).astype(jnp.bfloat16)
    partial_grads = jnp.stack(
        [tap_products(states[index_block], signals[index_block]) for index_block in range(per_slab)]
    )
    grads = lax.psum_scatter(
        partial_grads.astype(jnp.bfloat16), "dp", scatter_dimension=4, tiled=True
    ).astype(jnp.float32)
    return (adjoint, STEP * grads)


def solution(mesh):
    in_specs = (
        P("layer", "dp", None, None, None),
        P("layer", None, None, None, None),
        P("layer", "dp", None, None, None),
        P("layer", None, None, None),
        P("dp", None, None, None),
    )
    out_specs = (P("layer", "dp", None, None, None), P("layer", None, None, None, "dp"))
    return jax.shard_map(
        on_device, mesh=mesh, in_specs=in_specs, out_specs=out_specs, check_vma=False
    )
```

profile of v0, /device:TPU:1, one launch (start us, length us, event | category | flops | bytes accessed | tf_op | source)
XLA Modules:
  0.0 352.3 jit_solution(17270119978672052012)
XLA Ops:
  8.0 5.2 %collective-permute-start = (f32[1,16,16,256]{3,2,1,0:T(8,128)}, f32[1,16,16,256]{3,2,1,0:T(8,128)S(1)}, u32[]{:S(2)}, u32[]{:S(2)}) collective-permute-start(f32[1,16,16,256]{3,2,1,0:T(8,128)} %bitcast.407), channel_id=1, source_target_pairs={{4,0},{8,4},{12,8},{16,12},{20,16},{24,20},{28,24},{32,28},{36,32}... | collective-permute-start | bytes 786440 | tf_op jit(solution)/shard_map/ppermute | solution.py:13
  14.3 1.9 fusion.5
  16.6 1.3 copy-done.16
  23.7 1.9 collective-permute-start.1
  25.7 7.6 %collective-permute-done.1 = f32[1,16,16,256]{3,2,1,0:T(8,128)S(1)} collective-permute-done((f32[1,16,16,256]{3,2,1,0:T(8,128)S(1)}, f32[1,16,16,256]{3,2,1,0:T(8,128)S(1)}, u32[]{:S(2)}, u32[]{:S(2)}) %collective-permute-start.1) | collective-permute-done | bytes 262176 | tf_op jit(solution)/shard_map/ppermute | solution.py:13
  36.1 1.9 collective-permute-start.2
  38.0 7.0 %collective-permute-done.2 = f32[1,16,16,256]{3,2,1,0:T(8,128)S(1)} collective-permute-done((f32[1,16,16,256]{3,2,1,0:T(8,128)S(1)}, f32[1,16,16,256]{3,2,1,0:T(8,128)S(1)}, u32[]{:S(2)}, u32[]{:S(2)}) %collective-permute-start.2) | collective-permute-done | bytes 262176 | tf_op jit(solution)/shard_map/ppermute | solution.py:13
  50.4 64.5 %all-gather.4.cloned.1.call-done = f32[64,16,16,256]{3,2,1,0:T(8,128)} async-done(((f32[1,16,16,256]{3,2,1,0:T(8,128)}), f32[64,16,16,256]{3,2,1,0:T(8,128)}) %all-gather.4.cloned.1.call-update) | async-done | bytes 16777232 | tf_op jit(solution)/shard_map/all_gather | solution.py:18
  114.8 100.1 %all-gather.6.cloned.1.call-done = f32[64,16,16,256]{3,2,1,0:T(8,128)} async-done(((f32[1,16,16,256]{3,2,1,0:T(8,128)}), f32[64,16,16,256]{3,2,1,0:T(8,128)}) %all-gather.6.cloned.1.call-update) | async-done | bytes 16777232 | tf_op jit(solution)/shard_map/all_gather | solution.py:18
  214.9 82.3 %while.16 = (s32[]{:T(128)}, f32[1,16,16,256]{3,2,1,0:T(8,128)S(1)}, s32[]{:T(128)}, f32[64,16,16,256]{3,2,1,0:T(8,128)}, f32[64,1,16,16,256]{4,3,2,1,0:T(8,128)...) while((s32[]{:T(128)}, f32[1,16,16,256]{3,2,1,0:T(8,128)S(1)}, s32[]{:T(128)}, ...), condition=%wide.region_1.2_spmd.clone, body=%wide.region_0.1_spmd.clone.sunk | while | flops 262152 | bytes 1048747 | solution.py:31
  214.9 1.3 fusion.241
  216.3 1.3 fusion.241
  217.6 1.3 fusion.241
  218.8 1.3 fusion.241
  220.1 1.3 fusion.241
  221.4 1.3 fusion.241
  222.7 1.3 fusion.241
  224.0 1.3 fusion.241
  225.3 1.3 fusion.241
  226.6 1.3 fusion.241
  227.8 1.3 fusion.241
  229.1 1.3 fusion.241
  230.4 1.3 fusion.241
  231.7 1.3 fusion.241
  233.0 1.3 fusion.241
  234.3 1.3 fusion.241
  235.5 1.3 fusion.241
  236.8 1.3 fusion.241
  240.7 1.3 fusion.241
  242.0 1.3 fusion.241
  243.3 1.3 fusion.241
  244.5 1.3 fusion.241
  248.4 1.3 fusion.241
  249.7 1.3 fusion.241
  251.0 1.3 fusion.241
  252.2 1.3 fusion.241
  253.5 1.3 fusion.241
  256.1 1.3 fusion.241
  257.4 1.3 fusion.241
  258.7 1.3 fusion.241
  260.0 1.3 fusion.241
  261.2 1.3 fusion.241
  265.1 1.3 fusion.241
  266.4 1.3 fusion.241
  267.7 1.3 fusion.241
  269.0 1.3 fusion.241
  272.8 1.3 fusion.241
  274.1 1.3 fusion.241
  275.4 1.3 fusion.241
  276.7 1.3 fusion.241
  277.9 1.3 fusion.241
  280.5 1.3 fusion.241
  281.8 1.3 fusion.241
  283.1 1.3 fusion.241
  284.4 1.3 fusion.241
  285.7 1.3 fusion.241
  289.5 1.3 fusion.241
  290.8 1.3 fusion.241
  292.1 1.3 fusion.241
  293.4 1.3 fusion.241
  309.1 1.6 copy.110
  310.7 1.6 pad_maximum_fusion
  312.3 31.2 %reduce-scatter.2.cloned.1.call-done = bf16[2,3,3,256,64]{3,4,2,1,0:T(8,128)(2,1)} async-done(((bf16[2,3,3,256,256]{3,4,2,1,0:T(8,128)(2,1)}), bf16[2,3,3,256,64]{3,4,2,1,0:T(8,128)(2,1)}) %reduce-scatter.2.cloned.1.call-update) | async-done | bytes 589840 | tf_op jit(solution)/shard_map/reduce_scatter | solution.py:136
  343.5 2.2 convert_multiply_fusion
  (158 shorter events, 44.9 us)
Async XLA Ops:
  7.2 7.2 %copy-start.19 = (pred[8,3]{0,1:T(4,128)(4,1)S(1)}, pred[8,3]{0,1:T(4,128)(4,1)}, u32[]{:S(2)}) copy-start(pred[8,3]{0,1:T(4,128)(4,1)} %constant.106) | copy-start | bytes 76
  7.2 107.7 %all-gather.4.cloned.1.call-start = ((), (), s32[]{:S(2)}) async-start(), calls=%async_computation.1 | async-start | bytes 17039360 | tf_op jit(solution)/shard_map/all_gather | solution.py:18
  7.9 207.0 %all-gather.6.cloned.1.call-start = ((), (), s32[]{:S(2)}) async-start(), calls=%async_computation.3 | async-start | bytes 17039360 | tf_op jit(solution)/shard_map/all_gather | solution.py:18
  8.0 10.8 %collective-permute-start = (f32[1,16,16,256]{3,2,1,0:T(8,128)}, f32[1,16,16,256]{3,2,1,0:T(8,128)S(1)}, u32[]{:S(2)}, u32[]{:S(2)}) collective-permute-start(f32[1,16,16,256]{3,2,1,0:T(8,128)} %bitcast.407), channel_id=1, source_target_pairs={{4,0},{8,4},{12,8},{16,12},{20,16},{24,20},{28,24},{32,28},{36,32}... | collective-permute-start | bytes 786440 | tf_op jit(solution)/shard_map/ppermute | solution.py:13
  16.2 1.7 copy-start.16
  18.6 1.0 copy-start.1
  18.7 1.7 copy-start.17
  22.4 1.0 copy-start.12
  23.7 9.5 %collective-permute-start.1 = (f32[1,16,16,256]{3,2,1,0:T(8,128)S(1)}, f32[1,16,16,256]{3,2,1,0:T(8,128)S(1)}, u32[]{:S(2)}, u32[]{:S(2)}) collective-permute-start(f32[1,16,16,256]{3,2,1,0:T(8,128)S(1)} %fusion.147), channel_id=1, source_target_pairs={{4,0},{8,4},{12,8},{16,12},{20,16},{24,20},{28,24},{32,28},{36,32}... | collective-permute-start | bytes 786440 | tf_op jit(solution)/shard_map/ppermute | solution.py:13
  36.1 9.0 %collective-permute-start.2 = (f32[1,16,16,256]{3,2,1,0:T(8,128)S(1)}, f32[1,16,16,256]{3,2,1,0:T(8,128)S(1)}, u32[]{:S(2)}, u32[]{:S(2)}) collective-permute-start(f32[1,16,16,256]{3,2,1,0:T(8,128)S(1)} %fusion.142), channel_id=1, source_target_pairs={{4,0},{8,4},{12,8},{16,12},{20,16},{24,20},{28,24},{32,28},{36,32}... | collective-permute-start | bytes 786440 | tf_op jit(solution)/shard_map/ppermute | solution.py:13
  48.7 294.8 %reduce-scatter.2.cloned.1.call-start = ((), (), s32[]{:S(2)}) async-start(), calls=%async_computation.2 | async-start | bytes 2949120 | tf_op jit(solution)/shard_map/reduce_scatter | solution.py:136
  214.9 82.3 %copy-start = (f32[1,16,16,256]{3,2,1,0:T(8,128)S(1)}, f32[1,16,16,256]{3,2,1,0:T(8,128)}, u32[]{:S(2)}) copy-start(f32[1,16,16,256]{3,2,1,0:T(8,128)} %fusion.137) | copy-start | bytes 786436
  214.9 82.3 %copy-start.3 = (f32[1,16,16,256]{3,2,1,0:T(8,128)S(1)}, f32[1,16,16,256]{3,2,1,0:T(8,128)}, u32[]{:S(2)}) copy-start(f32[1,16,16,256]{3,2,1,0:T(8,128)} %param.10) | copy-start | bytes 786436
  297.2 1.7 copy-start.18
  299.9 0.9 copy-start.15
  299.9 1.2 copy-start.11
  300.8 0.9 copy-start.10
  300.8 1.1 copy-start.9
  300.8 1.4 copy-start.13
  300.8 1.6 copy-start.8
  300.8 1.8 copy-start.7
  301.1 1.8 copy-start.6
  301.7 1.4 copy-start.5
  303.4 3.1 copy-start.4
  304.1 2.8 copy-start.14
  308.1 1.0 copy-start.2
Sparse Core Ops, SparseCore 0:
  10.8 104.0 all-gather.3
  118.2 96.7 all-gather.5
  312.4 31.0 reduce-scatter.1
where the time goes:
time: 354 us; the launch traced here: 352 us
  waiting for transfers between devices  211 us (60%)
  other arithmetic  88.9 us (25%)
  between operations  14.7 us (4%)
  local copies, waits for them, and re-layouts  13.5 us (4%)
  matrix products  13 us (4%)
  starting transfers between devices  9.29 us (3%)
    all_gather x2, waiting for transfers between devices, entering(): everything = jax.tree.map(lambda part: lax.all_gather(part, axis), shard)  165 us
    select_n x64, other arithmetic, turn(): return jax.tree.map(lambda a, b: jnp.where(reached, a, b), new, before)  80.6 us
    reduce_scatter x1, waiting for transfers between devices, on_device(): lax.psum_scatter(partial_grads.astype(jnp.bfloat16), 'dp', scatter_dimens...  31.2 us
    ppermute x3, waiting for transfers between devices, shifted(): return lax.ppermute(block, axis, route)  14.6 us
    ppermute x3, starting transfers between devices, shifted(): return lax.ppermute(block, axis, route)  8.99 us
  transfers between devices with their start and end apart: 6, of which 5 were waited for; matrix products, arithmetic and copies ran while one was open for 4% of the time, Pallas kernels for 0%

commit v1 on v0

v1 whole, which is shorter than its diff:
```python
import functools

import jax
import jax.numpy as jnp
from jax import lax
from jax.experimental import pallas as pl
from jax.experimental.pallas import tpu as pltpu
from jax.sharding import PartitionSpec as P

STEP = 0.5
DAMPING = 0.5
BF = jnp.bfloat16
F32 = jnp.float32
VMEM_LIMIT = 24 * 1024 * 1024


def call(body, outs, n_in, smem=(), flops=0, name=None):
    return pl.pallas_call(
        body,
        out_shape=outs,
        in_specs=[
            pl.BlockSpec(memory_space=pltpu.SMEM if k in smem else pltpu.VMEM)
            for k in range(n_in)
        ],
        out_specs=jax.tree.map(lambda _: pl.BlockSpec(memory_space=pltpu.VMEM), outs),
        compiler_params=pltpu.CompilerParams(vmem_limit_bytes=VMEM_LIMIT),
        cost_estimate=pl.CostEstimate(flops=flops, bytes_accessed=2_000_000, transcendentals=0),
        name=name,
    )


def columns(value, width):
    cells = value.shape[0]
    col = lax.broadcasted_iota(jnp.int32, value.shape, 0) % width
    ahead = jnp.where(col == width - 1, 0.0, pltpu.roll(value, cells - 1, 0))
    behind = jnp.where(col == 0, 0.0, pltpu.roll(value, 1, 0))
    return ahead, value, behind


def rows(value, width):
    edge = jnp.zeros((width, value.shape[1]), value.dtype)
    return jnp.concatenate([edge, value, edge], 0)


def forward_patches(value, width):
    cells = value.shape[0]
    ahead, here, behind = columns(value, width)
    padded = [rows(part.astype(BF), width) for part in (behind, here, ahead)]
    return [padded[j][i * width : i * width + cells] for i in range(3) for j in range(3)]


def adjoint_patches(value, width):
    cells = value.shape[0]
    ahead, here, behind = columns(value, width)
    padded = [rows(part.astype(BF), width) for part in (ahead, here, behind)]
    return [padded[j][(2 - i) * width : (2 - i) * width + cells] for i in range(3) for j in range(3)]


def adjoint_conv(signal, turned_ref, block, width):
    patches = jnp.concatenate(adjoint_patches(signal, width), 1)
    return jnp.dot(patches, turned_ref[block], preferred_element_type=F32)


def block_map(value, slope, turned_ref, block, width):
    signal = (slope * value).astype(BF).astype(F32)
    return value + STEP * adjoint_conv(signal, turned_ref, block, width)


def relaxed(right, slope_ref, turned_ref, width):
    for block in range(slope_ref.shape[0] - 1, -1, -1):
        right = block_map(right, slope_ref[block], turned_ref, block, width)
    return right


def slope_body(width, states_ref, kernels_ref, slope_ref, turned_ref):
    blocks, _, height, _, channels = states_ref.shape
    for block in range(blocks):
        value = states_ref[block, 0].reshape(height * width, channels).astype(F32)
        patches = jnp.concatenate(forward_patches(value, width), 1)
        taps = kernels_ref[block].reshape(9 * channels, channels)
        act = jnp.tanh(jnp.dot(patches, taps, preferred_element_type=F32))
        slope_ref[block] = 1.0 - act * act
        for i in range(3):
            for j in range(3):
                at = (i * 3 + j) * channels
                turned_ref[block, at : at + channels, :] = kernels_ref[block, i, j].T


def entering(flag_ref, arriving_ref, terminal_ref):
    return jnp.where(flag_ref[0] == 1, terminal_ref[...], arriving_ref[...].astype(F32))


def sweep_body(width, flag_ref, arriving_ref, terminal_ref, points_ref, slope_ref, turned_ref, out_ref, send_ref):
    right = entering(flag_ref, arriving_ref, terminal_ref)
    points = points_ref[...]
    points = points + DAMPING * (relaxed(right, slope_ref, turned_ref, width) - points)
    out_ref[...] = points
    send_ref[...] = points.astype(BF)


def residual_body(width, flag_ref, arriving_ref, terminal_ref, points_ref, slope_ref, turned_ref, gain_ref, relax_ref, send_ref):
    right = entering(flag_ref, arriving_ref, terminal_ref)
    relax = relaxed(right, slope_ref, turned_ref, width)
    relax_ref[...] = relax
    residual = (relax - points_ref[...]).reshape(32, 8, 256)
    decay = (1.0 - gain_ref[...]).reshape(32, 8, 256)
    for half in range(2):
        lanes = slice(128 * half, 128 * half + 128)
        send_ref[:, half] = jnp.concatenate([residual[:, :, lanes], decay[:, :, lanes]], 1).astype(BF)


def scan_body(given_ref, out_ref):
    count = given_ref.shape[0]
    error = jnp.zeros((8, 128), F32)
    for at in range(count - 1, -1, -1):
        out_ref[at] = error.astype(BF)
        term = given_ref[at].astype(F32)
        error = error - term[8:] * error + term[:8]


def final_body(width, flag_ref, arriving_ref, terminal_ref, error_ref, gain_ref, relax_ref, slope_ref, turned_ref, adjoint_ref, signal_ref):
    error = error_ref[...].astype(F32).reshape(32, 2, 8, 128)
    error = jnp.concatenate([error[:, 0], error[:, 1]], 2).reshape(256, 256)
    right = entering(flag_ref, arriving_ref, terminal_ref) + error
    adjoint_ref[0] = gain_ref[...] * error + relax_ref[...]
    slope = slope_ref[1]
    last = (slope * right).astype(BF).astype(F32)
    inner = right + STEP * adjoint_conv(last, turned_ref, 1, width)
    adjoint_ref[1] = inner
    first = (slope_ref[0] * inner).astype(BF).astype(F32)
    low = lax.broadcasted_iota(jnp.int32, (128, 128), 1) < 64
    for block, signal in ((0, first), (1, last)):
        for half in range(2):
            top = signal[:128, 128 * half : 128 * half + 128]
            bottom = signal[128:, 128 * half : 128 * half + 128]
            signal_ref[2 * half, block] = jnp.where(low, top, pltpu.roll(bottom, 64, 1)).astype(BF)
            signal_ref[2 * half + 1, block] = jnp.where(low, pltpu.roll(top, 64, 1), bottom).astype(BF)


def turn_body(states_ref, out_ref):
    images, blocks = states_ref.shape[:2]
    for block in range(blocks):
        for image in range(images):
            out_ref[block, :, 256 * image : 256 * image + 256] = states_ref[image, block].T


def taps_body(width, images, *refs):
    states_ref, signal_refs, out_ref = refs[0], refs[1 : 1 + images], refs[1 + images]
    low = lax.broadcasted_iota(jnp.int32, (128, 128), 1) < 64
    wide = lax.broadcasted_iota(jnp.int32, (256, 128), 1) < 64
    for block in range(out_ref.shape[0]):
        parts = []
        for image in range(images):
            packed = signal_refs[image][block].astype(F32)
            other = pltpu.roll(packed, 64, 1)
            both = jnp.concatenate([jnp.where(low, packed, other), jnp.where(low, other, packed)], 0)
            patches = adjoint_patches(both, width)
            patches.append(patches[-1])
            parts.append(
                jnp.concatenate([jnp.where(wide, patches[2 * k], patches[2 * k + 1]) for k in range(5)], 1)
            )
        moved = jnp.concatenate(parts, 0)
        grads = STEP * jnp.dot(states_ref[block], moved, preferred_element_type=F32)
        for tap in range(9):
            out_ref[block, tap // 3, tap % 3] = grads[:, 64 * tap : 64 * tap + 64]


def on_device(states, kernels, adjoint_guess, coarse_gain, terminal):
    blocks, _, height, width, channels = states.shape
    cells = height * width
    slabs = lax.axis_size("layer")
    images = lax.axis_size("dp")
    here = lax.axis_index("dp")
    flag = (lax.axis_index("layer") == slabs - 1).astype(jnp.int32).reshape(1)
    conv_flops = 2 * cells * 9 * channels * channels
    shape = jax.ShapeDtypeStruct

    def from_right(points):
        return lax.ppermute(points, "layer", [((i + 1) % slabs, i) for i in range(slabs)])

    points = adjoint_guess.reshape(cells, channels)
    last_value = terminal.reshape(cells, channels)
    gain = coarse_gain.reshape(cells, channels)
    arriving = from_right(points.astype(BF))
    gathered = lax.all_gather(states.reshape(blocks, cells, channels), "dp")
    slopes, turned = call(
        functools.partial(slope_body, width),
        (shape((blocks, cells, channels), F32), shape((blocks, 9 * channels, channels), BF)),
        2,
        flops=blocks * conv_flops,
        name="slopes",
    )(states, kernels)
    for sweep_index in range(2):
        points, send = call(
            functools.partial(sweep_body, width),
            (shape((cells, channels), F32), shape((cells, channels), BF)),
            6,
            smem=(0,),
            flops=blocks * conv_flops,
            name="sweep",
        )(flag, arriving, last_value, points, slopes, turned)
        arriving = from_right(send)
    relax, send = call(
        functools.partial(residual_body, width),
        (shape((cells, channels), F32), shape((32, 2, 16, 128), BF)),
        7,
        smem=(0,),
        flops=blocks * conv_flops,
        name="residual",
    )(flag, arriving, last_value, points, slopes, turned, gain)
    spread = lax.all_to_all(send.reshape(slabs, 16, 128), "layer", 0, 0, tiled=True)
    errors = call(scan_body, shape((slabs, 8, 128), BF), 1, name="scan")(spread)
    error = lax.all_to_all(errors, "layer", 0, 0, tiled=True)
    adjoint, signals = call(
        functools.partial(final_body, width),
        (shape((blocks, cells, channels), F32), shape((images, blocks, 128, 128), BF)),
        8,
        smem=(0,),
        flops=conv_flops,
        name="final",
    )(flag, arriving, last_value, error, gain, relax, slopes, turned)

    received = [lax.dynamic_index_in_dim(signals, here, 0, keepdims=False)]
    for k in range(1, images):
        part = lax.dynamic_index_in_dim(signals, (here + k) % images, 0, keepdims=False)
        received.append(lax.ppermute(part, "dp", [(i, (i + k) % images) for i in range(images)]))
    order = jnp.stack([(here - k) % images for k in range(images)])
    ordered = jnp.take(gathered, order, axis=0)
    states_turned = call(turn_body, shape((blocks, channels, images * cells), BF), 1, name="turn")(ordered)
    grads = call(
        functools.partial(taps_body, width, images),
        shape((blocks, 3, 3, channels, channels // images), F32),
        1 + images,
        flops=blocks * conv_flops,
        name="taps",
    )(states_turned, *received)
    return adjoint.reshape(blocks, 1, height, width, channels), grads


def solution(mesh):
    in_specs = (
        P("layer", "dp", None, None, None),
        P("layer", None, None, None, None),
        P("layer", "dp", None, None, None),
        P("layer", None, None, None),
        P("dp", None, None, None),
    )
    out_specs = (P("layer", "dp", None, None, None), P("layer", None, None, None, "dp"))
    return jax.shard_map(
        on_device, mesh=mesh, in_specs=in_specs, out_specs=out_specs, check_vma=False
    )
```

time: 354 us -> 106 us (0.30)
  waiting for transfers between devices: 211 us -> 26.8 us
  other arithmetic: 88.9 us -> 1.95 us
  starting transfers between devices: 9.29 us -> 39.2 us
  matrix products: 13 us -> 0 us
  Pallas kernels: 0 us -> 10.1 us
    all_gather x2 -> x1, waiting for transfers between devices: 165 us -> 0.01 us  [on_device(): gathered = lax.all_gather(states.reshape(blocks, cells, channels), 'dp')]
    select_n x64 -> x2, other arithmetic: 80.6 us -> 0.24 us  [on_device(): ordered = jnp.take(gathered, order, axis=0)]
    reduce_scatter x1 -> x0, waiting for transfers between devices: 31.2 us -> none  [on_device(): lax.psum_scatter(partial_grads.astype(jnp.bfloat16), 'dp', scatter_dimens...]
    all_to_all x0 -> x2, waiting for transfers between devices: none -> 24.1 us  [the longest x1 13 us: on_device(): lax.all_to_all(send.reshape(slabs, 16, 128), 'layer', 0, 0, tiled=True)]
    all_to_all x0 -> x2, starting transfers between devices: none -> 19 us  [the longest x1 13.9 us: on_device(): lax.all_to_all(send.reshape(slabs, 16, 128), 'layer', 0, 0, tiled=True)]
    ppermute x3 -> x6, waiting for transfers between devices: 14.6 us -> 1.98 us  [the longest x3 1.98 us: from_right(): lax.ppermute(points, 'layer', [((i + 1) % slabs, i) for i in range(slabs)])]
    ppermute x3 -> x6, starting transfers between devices: 8.99 us -> 20.2 us  [the longest x3 15.1 us: from_right(): lax.ppermute(points, 'layer', [((i + 1) % slabs, i) for i in range(slabs)])]
    pallas_call x0 -> x8, Pallas kernels: none -> 10.1 us  [the longest x2 2.89 us: on_device(): call(functools.partial(sweep_body, width), (shape((cells, channels), F32)...]
  transfers between devices with their start and end apart: 6 -> 9, of which waited for: 5 -> 4; matrix products, arithmetic and copies ran while one was open for 4% -> 4% of each run, Pallas kernels for 0% -> 8%
where the time goes in v1:
time: 106 us
  starting transfers between devices  39.2 us (37%)
  waiting for transfers between devices  26.8 us (25%)
  between operations  14.3 us (13%)
  local copies, waits for them, and re-layouts  13.6 us (13%)
  Pallas kernels  10.1 us (10%)
  other arithmetic  1.95 us (2%)
    ppermute x3, starting transfers between devices, from_right(): lax.ppermute(points, 'layer', [((i + 1) % slabs, i) for i in range(slabs)])  15.1 us
    all_to_all x1, starting transfers between devices, on_device(): lax.all_to_all(send.reshape(slabs, 16, 128), 'layer', 0, 0, tiled=True)  13.9 us
    all_to_all x1, waiting for transfers between devices, on_device(): lax.all_to_all(send.reshape(slabs, 16, 128), 'layer', 0, 0, tiled=True)  13 us
    unnamed x31, local copies, waits for them, and re-layouts  11.7 us
    all_to_all x1, waiting for transfers between devices, on_device(): error = lax.all_to_all(errors, 'layer', 0, 0, tiled=True)  11.1 us
    all_to_all x1, starting transfers between devices, on_device(): error = lax.all_to_all(errors, 'layer', 0, 0, tiled=True)  5.06 us
    ppermute x3, starting transfers between devices, on_device(): lax.ppermute(part, 'dp', [(i, (i + k) % images) for i in range(images)])  5.06 us
    pallas_call x2, Pallas kernels, on_device(): call(functools.partial(sweep_body, width), (shape((cells, channels), F32)...  2.89 us
  transfers between devices with their start and end apart: 9, of which 4 were waited for; matrix products, arithmetic and copies ran while one was open for 4% of the time, Pallas kernels for 8%

profile of v1, /device:TPU:1, one launch (start us, length us, event | category | flops | bytes accessed | tf_op | source)
XLA Modules:
  0.0 105.9 jit_solution(3022992391431635348)
XLA Ops:
  7.2 0.0 copy-start.4
  7.2 0.0 copy-start
  7.2 0.0 all-gather.2.cloned.1.call-start
  7.2 0.7 all-gather.2.cloned.1.call-update
  7.9 1.6 %bitcast_convert_fusion = bf16[256,256]{1,0:T(8,128)(2,1)} fusion(f32[1,1,16,16,256]{4,3,2,1,0:T(8,128)} %param.7), kind=kLoop, calls=%fused_computation.11 | loop fusion | flops 65536 | bytes 393216 | tf_op jit(solution)/shard_map/convert_element_type | solution.py:184
  9.5 3.2 %collective-permute-start = (bf16[256,256]{1,0:T(8,128)(2,1)}, bf16[256,256]{1,0:T(8,128)(2,1)S(1)}, u32[]{:S(2)}, u32[]{:S(2)}) collective-permute-start(bf16[256,256]{1,0:T(8,128)(2,1)} %bitcast_convert_fusion), channel_id=1, source_target_pairs={{4,0},{8,4},{12,8},{16,12},{20,16},{24,20},{28,24},{32,28},{36,32}... | collective-permute-start | bytes 393224 | tf_op jit(solution)/shard_map/ppermute | solution.py:179
  12.8 0.0 copy-start.1
  12.8 1.7 %copy-done.1 = bf16[2,3,3,256,256]{4,3,2,1,0:T(8,128)(2,1)S(1)} copy-done((bf16[2,3,3,256,256]{4,3,2,1,0:T(8,128)(2,1)S(1)}, bf16[2,3,3,256,256]{4,3,2,1,0:T(8,128)(2,1)}, u32[]{:S(2)}) %copy-start.1) | copy-done | bytes 2359320
  14.4 0.0 copy-start.3
  14.4 0.9 copy-done.3
  15.4 0.8 slopes.1
  16.2 0.0 collective-permute-done.arriving_ref
  16.2 0.0 copy-done.4
  16.2 0.0 copy-done
  16.2 1.4 %sweep.2 = (f32[256,256]{1,0:T(8,128)S(1)}, bf16[256,256]{1,0:T(8,128)(2,1)S(1)}) custom-call(s32[1]{0:T(128)} %bitcast.flag_ref, bf16[256,256]{1,0:T(8,128)(2,1)S(1)} %collective-permute-done.arriving_ref, f32[256,256]{1,0:T(8,128)S(1)} %bitcast.28, f32[256,256]{1,0:T(8,128)S(1)} %bitcast.35, f32[2,256,256]{2,1,0:T(8,128)S(1)} %get-tuple-element.12.slope_ref, ...), custom_call_target="tpu_custom_call" | custom-call | flops 603979776 | bytes 2000000 | tf_op jit(solution)/shard_map/sweep/pallas_call | solution.py:194
  17.7 0.0 copy-start.2
  17.7 5.8 %collective-permute-start.1 = (bf16[256,256]{1,0:T(8,128)(2,1)S(1)}, bf16[256,256]{1,0:T(8,128)(2,1)S(1)}, u32[]{:S(2)}, u32[]{:S(2)}) collective-permute-start(bf16[256,256]{1,0:T(8,128)(2,1)S(1)} %get-tuple-element.14), channel_id=1, source_target_pairs={{4,0},{8,4},{12,8},{16,12},{20,16},{24,20},{28,24},{32,28},{36,32}... | collective-permute-start | bytes 393224 | tf_op jit(solution)/shard_map/ppermute | solution.py:179
  23.5 1.0 collective-permute-done.1.arriving_ref
  24.5 1.4 %sweep.3 = (f32[256,256]{1,0:T(8,128)S(1)}, bf16[256,256]{1,0:T(8,128)(2,1)S(1)}) custom-call(s32[1]{0:T(128)} %bitcast.flag_ref, bf16[256,256]{1,0:T(8,128)(2,1)S(1)} %collective-permute-done.1.arriving_ref, f32[256,256]{1,0:T(8,128)S(1)} %bitcast.29, f32[256,256]{1,0:T(8,128)S(1)} %get-tuple-element.15.points_ref, ...), custom_call_target="tpu_custom_call" | custom-call | flops 603979776 | bytes 2000000 | tf_op jit(solution)/shard_map/sweep/pallas_call | solution.py:194
  26.0 6.1 %collective-permute-start.2 = (bf16[256,256]{1,0:T(8,128)(2,1)S(1)}, bf16[256,256]{1,0:T(8,128)(2,1)S(1)}, u32[]{:S(2)}, u32[]{:S(2)}) collective-permute-start(bf16[256,256]{1,0:T(8,128)(2,1)S(1)} %get-tuple-element.16), channel_id=1, source_target_pairs={{4,0},{8,4},{12,8},{16,12},{20,16},{24,20},{28,24},{32,28},{36,32}... | collective-permute-start | bytes 393224 | tf_op jit(solution)/shard_map/ppermute | solution.py:179
  32.1 1.0 collective-permute-done.2.arriving_ref
  33.0 0.0 copy-done.2
  33.0 1.4 %residual.1 = (f32[256,256]{1,0:T(8,128)S(1)}, bf16[32,2,16,128]{3,2,1,0:T(8,128)(2,1)S(1)}) custom-call(s32[1]{0:T(128)} %bitcast.flag_ref, bf16[256,256]{1,0:T(8,128)(2,1)S(1)} %collective-permute-done.2.arriving_ref, f32[256,256]{1,0:T(8,128)S(1)} %bitcast.30, f32[256,256]{1,0:T(8,128)S(1)} %get-tuple-element.17.points_ref, ...), custom_call_target="tpu_custom_call" | custom-call | flops 603979776 | bytes 2000000 | tf_op jit(solution)/shard_map/residual/pallas_call | solution.py:203
  34.5 0.0 copy-start.6
  34.5 0.7 copy-done.6
  35.2 0.0 copy-start.8
  35.2 0.7 copy-done.8
  35.9 13.9 %all-to-all-start = ((bf16[64,16,128]{2,1,0:T(8,128)(2,1)}), bf16[64,16,128]{2,1,0:T(8,128)(2,1)}, u32[]{:S(2)}, u32[]{:S(2)}) async-start(bf16[64,16,128]{2,1,0:T(8,128)(2,1)} %bitcast.36), calls=%async_computation | async-start | bytes 524288 | tf_op jit(solution)/shard_map/all_to_all | solution.py:211
  49.9 13.0 %all-to-all-done.given_ref = bf16[64,16,128]{2,1,0:T(8,128)(2,1)} async-done(((bf16[64,16,128]{2,1,0:T(8,128)(2,1)}), bf16[64,16,128]{2,1,0:T(8,128)(2,1)}, u32[]{:S(2)}, u32[]{:S(2)}) %all-to-all-start) | async-done | bytes 262176 | tf_op jit(solution)/shard_map/all_to_all | solution.py:211
  62.9 1.2 %scan.1 = bf16[64,8,128]{2,1,0:T(8,128)(2,1)S(1)} custom-call(bf16[64,16,128]{2,1,0:T(8,128)(2,1)} %all-to-all-done.given_ref), custom_call_target="tpu_custom_call" | custom-call | bytes 2000000 | tf_op jit(solution)/shard_map/scan/pallas_call | solution.py:212
  64.1 0.0 copy-start.5
  64.1 0.6 copy-done.5
  64.7 5.1 %all-to-all-start.1 = ((bf16[64,8,128]{2,1,0:T(8,128)(2,1)}), bf16[64,8,128]{2,1,0:T(8,128)(2,1)}, u32[]{:S(2)}, u32[]{:S(2)}) async-start(bf16[64,8,128]{2,1,0:T(8,128)(2,1)} %copy-done.5), calls=%async_computation.1 | async-start | bytes 262144 | tf_op jit(solution)/shard_map/all_to_all | solution.py:213
  69.8 0.1 fusion
  69.9 0.1 compare_and_fusion
  70.0 11.1 %all-to-all-done.1.error_ref = bf16[64,8,128]{2,1,0:T(8,128)(2,1)} async-done(((bf16[64,8,128]{2,1,0:T(8,128)(2,1)}), bf16[64,8,128]{2,1,0:T(8,128)(2,1)}, u32[]{:S(2)}, u32[]{:S(2)}) %all-to-all-start.1) | async-done | bytes 131104 | tf_op jit(solution)/shard_map/all_to_all | solution.py:213
  81.1 0.0 copy-start.7
  81.1 0.9 copy-done.7
  82.0 2.2 %final.1 = (f32[2,256,256]{2,1,0:T(8,128)}, bf16[4,2,128,128]{3,2,1,0:T(8,128)(2,1)S(1)}) custom-call(s32[1]{0:T(128)} %bitcast.flag_ref, bf16[256,256]{1,0:T(8,128)(2,1)S(1)} %collective-permute-done.2.arriving_ref, f32[256,256]{1,0:T(8,128)S(1)} %bitcast.31, bf16[64,8,128]{2,1,0:T(8,128)(2,1)} %all-to-all-done.1.error_ref, f32[256,256]{1,0:T(8,128)S(1)} %bitcast.33, ...), custom_call_target="tpu_custom_call" | custom-call | flops 301989888 | bytes 2000000 | tf_op jit(solution)/shard_map/final/pallas_call | solution.py:214
  84.3 1.4 %collective-permute-start.3 = (bf16[2,128,128]{2,1,0:T(8,128)(2,1)S(1)}, bf16[2,128,128]{2,1,0:T(8,128)(2,1)S(1)}, u32[]{:S(2)}, u32[]{:S(2)}) collective-permute-start(bf16[2,128,128]{2,1,0:T(8,128)(2,1)S(1)} %get-tuple-element.28), channel_id=1, source_target_pairs={{0,1},{1,2},{2,3},{3,0},{4,5},{5,6},{6,7},{7,4},{8,9},{9,10},{10,1... | collective-permute-start | bytes 196616 | tf_op jit(solution)/shard_map/ppermute | solution.py:226
  85.6 2.6 %collective-permute-start.4 = (bf16[2,128,128]{2,1,0:T(8,128)(2,1)S(1)}, bf16[2,128,128]{2,1,0:T(8,128)(2,1)S(1)}, u32[]{:S(2)}, u32[]{:S(2)}) collective-permute-start(bf16[2,128,128]{2,1,0:T(8,128)(2,1)S(1)} %get-tuple-element.27), channel_id=1, source_target_pairs={{0,2},{1,3},{2,0},{3,1},{4,6},{5,7},{6,4},{7,5},{8,10},{9,11},{10,... | collective-permute-start | bytes 196616 | tf_op jit(solution)/shard_map/ppermute | solution.py:226
  88.2 1.1 %collective-permute-start.5 = (bf16[2,128,128]{2,1,0:T(8,128)(2,1)S(1)}, bf16[2,128,128]{2,1,0:T(8,128)(2,1)S(1)}, u32[]{:S(2)}, u32[]{:S(2)}) collective-permute-start(bf16[2,128,128]{2,1,0:T(8,128)(2,1)S(1)} %get-tuple-element.26), channel_id=1, source_target_pairs={{0,3},{1,0},{2,1},{3,2},{4,7},{5,4},{6,5},{7,6},{8,11},{9,8},{10,9... | collective-permute-start | bytes 196616 | tf_op jit(solution)/shard_map/ppermute | solution.py:226
  89.3 0.0 all-gather.2.cloned.1.call-done
  89.3 1.8 %gather_fusion = bf16[4,2,256,256]{3,2,1,0:T(8,128)(2,1)S(1)} fusion(bf16[4,2,256,256]{3,2,1,0:T(8,128)(2,1)} %all-gather.2.cloned.1.call-done, s32[1024]{0:T(1024)S(1)} %pad_clamp_fusion), kind=kCustom, calls=%fused_computation | custom fusion | bytes 2097168 | tf_op jit(solution)/shard_map/jit(_take)/gather | solution.py:228
  91.2 0.2 broadcast_select_fusion.states_ref
  91.3 0.3 turn.1.refs_0_
  91.7 0.0 collective-permute-done.3.refs_2_
  91.7 0.0 copy-start.9
  91.7 0.6 copy-done.9
  92.3 0.0 collective-permute-done.4.refs_3_
  92.3 0.0 copy-start.11
  92.3 0.6 copy-done.11
  92.9 0.0 collective-permute-done.5.refs_4_
  92.9 0.0 copy-start.13
  92.9 0.6 copy-done.13
  93.6 0.0 copy-start.10
  93.6 0.8 copy-done.10
  94.4 0.0 copy-start.12
  94.4 0.8 copy-done.12
  95.2 0.0 copy-start.14
  95.2 0.8 copy-done.14
  96.1 1.2 %taps.1 = f32[2,3,3,256,64]{4,3,2,1,0:T(8,128)S(1)} custom-call(bf16[2,256,1024]{2,1,0:T(8,128)(2,1)S(1)} %turn.1.refs_0_, bf16[2,128,128]{2,1,0:T(8,128)(2,1)S(1)} %get-tuple-element.29.refs_1_, bf16[2,128,128]{2,1,0:T(8,128)(2,1)S(1)} %copy-done.10, bf16[2,128,128]{2,1,0:T(8,128)(2,1)S(1)} %copy-done.12, bf16[2,128,128]{2,1,0:T(8,128)(2,1)S(1)} %copy-done.14), custom_call_target="tpu_custom_call" | custom-call | flops 603979776 | bytes 2000000 | tf_op jit(solution)/shard_map/taps/pallas_call | solution.py:230
  97.3 1.7 %copy.10 = f32[2,3,3,256,64]{3,4,2,1,0:T(8,128)} copy(f32[2,3,3,256,64]{4,3,2,1,0:T(8,128)S(1)} %taps.1) | data formatting | bytes 2359296
  (2 shorter events, 0.0 us)
Async XLA Ops:
  7.2 9.1 %copy-start.4 = (f32[1,1,16,16,256]{4,3,2,1,0:T(8,128)S(1)}, f32[1,1,16,16,256]{4,3,2,1,0:T(8,128)}, u32[]{:S(2)}) copy-start(f32[1,1,16,16,256]{4,3,2,1,0:T(8,128)} %param.7) | copy-start | bytes 786436
  7.2 9.1 %copy-start = (f32[1,16,16,256]{3,2,1,0:T(8,128)S(1)}, f32[1,16,16,256]{3,2,1,0:T(8,128)}, u32[]{:S(2)}) copy-start(f32[1,16,16,256]{3,2,1,0:T(8,128)} %param.9) | copy-start | bytes 786436
  7.2 82.1 %all-gather.2.cloned.1.call-start = ((), (), s32[]{:S(2)}) async-start(), calls=%async_computation.2 | async-start | bytes 1310720 | tf_op jit(solution)/shard_map/all_gather | solution.py:185
  9.5 6.7 %collective-permute-start = (bf16[256,256]{1,0:T(8,128)(2,1)}, bf16[256,256]{1,0:T(8,128)(2,1)S(1)}, u32[]{:S(2)}, u32[]{:S(2)}) collective-permute-start(bf16[256,256]{1,0:T(8,128)(2,1)} %bitcast_convert_fusion), channel_id=1, source_target_pairs={{4,0},{8,4},{12,8},{16,12},{20,16},{24,20},{28,24},{32,28},{36,32}... | collective-permute-start | bytes 393224 | tf_op jit(solution)/shard_map/ppermute | solution.py:179
  12.8 1.7 %copy-start.1 = (bf16[2,3,3,256,256]{4,3,2,1,0:T(8,128)(2,1)S(1)}, bf16[2,3,3,256,256]{4,3,2,1,0:T(8,128)(2,1)}, u32[]{:S(2)}) copy-start(bf16[2,3,3,256,256]{4,3,2,1,0:T(8,128)(2,1)} %kernels_ref.1) | copy-start | bytes 7077892
  14.4 0.9 copy-start.3
  17.7 15.3 %copy-start.2 = (f32[1,16,16,256]{3,2,1,0:T(8,128)S(1)}, f32[1,16,16,256]{3,2,1,0:T(8,128)}, u32[]{:S(2)}) copy-start(f32[1,16,16,256]{3,2,1,0:T(8,128)} %param.8) | copy-start | bytes 786436
  17.7 6.8 %collective-permute-start.1 = (bf16[256,256]{1,0:T(8,128)(2,1)S(1)}, bf16[256,256]{1,0:T(8,128)(2,1)S(1)}, u32[]{:S(2)}, u32[]{:S(2)}) collective-permute-start(bf16[256,256]{1,0:T(8,128)(2,1)S(1)} %get-tuple-element.14), channel_id=1, source_target_pairs={{4,0},{8,4},{12,8},{16,12},{20,16},{24,20},{28,24},{32,28},{36,32}... | collective-permute-start | bytes 393224 | tf_op jit(solution)/shard_map/ppermute | solution.py:179
  26.0 7.1 %collective-permute-start.2 = (bf16[256,256]{1,0:T(8,128)(2,1)S(1)}, bf16[256,256]{1,0:T(8,128)(2,1)S(1)}, u32[]{:S(2)}, u32[]{:S(2)}) collective-permute-start(bf16[256,256]{1,0:T(8,128)(2,1)S(1)} %get-tuple-element.16), channel_id=1, source_target_pairs={{4,0},{8,4},{12,8},{16,12},{20,16},{24,20},{28,24},{32,28},{36,32}... | collective-permute-start | bytes 393224 | tf_op jit(solution)/shard_map/ppermute | solution.py:179
  34.5 0.7 copy-start.6
  35.2 0.7 copy-start.8
  35.9 27.0 %all-to-all-start = ((bf16[64,16,128]{2,1,0:T(8,128)(2,1)}), bf16[64,16,128]{2,1,0:T(8,128)(2,1)}, u32[]{:S(2)}, u32[]{:S(2)}) async-start(bf16[64,16,128]{2,1,0:T(8,128)(2,1)} %bitcast.36), calls=%async_computation | async-start | bytes 524288 | tf_op jit(solution)/shard_map/all_to_all | solution.py:211
  64.1 0.7 copy-start.5
  64.7 16.3 %all-to-all-start.1 = ((bf16[64,8,128]{2,1,0:T(8,128)(2,1)}), bf16[64,8,128]{2,1,0:T(8,128)(2,1)}, u32[]{:S(2)}, u32[]{:S(2)}) async-start(bf16[64,8,128]{2,1,0:T(8,128)(2,1)} %copy-done.5), calls=%async_computation.1 | async-start | bytes 262144 | tf_op jit(solution)/shard_map/all_to_all | solution.py:213
  81.1 1.0 copy-start.7
  84.3 7.4 %collective-permute-start.3 = (bf16[2,128,128]{2,1,0:T(8,128)(2,1)S(1)}, bf16[2,128,128]{2,1,0:T(8,128)(2,1)S(1)}, u32[]{:S(2)}, u32[]{:S(2)}) collective-permute-start(bf16[2,128,128]{2,1,0:T(8,128)(2,1)S(1)} %get-tuple-element.28), channel_id=1, source_target_pairs={{0,1},{1,2},{2,3},{3,0},{4,5},{5,6},{6,7},{7,4},{8,9},{9,10},{10,1... | collective-permute-start | bytes 196616 | tf_op jit(solution)/shard_map/ppermute | solution.py:226
  85.6 6.7 %collective-permute-start.4 = (bf16[2,128,128]{2,1,0:T(8,128)(2,1)S(1)}, bf16[2,128,128]{2,1,0:T(8,128)(2,1)S(1)}, u32[]{:S(2)}, u32[]{:S(2)}) collective-permute-start(bf16[2,128,128]{2,1,0:T(8,128)(2,1)S(1)} %get-tuple-element.27), channel_id=1, source_target_pairs={{0,2},{1,3},{2,0},{3,1},{4,6},{5,7},{6,4},{7,5},{8,10},{9,11},{10,... | collective-permute-start | bytes 196616 | tf_op jit(solution)/shard_map/ppermute | solution.py:226
  88.2 4.7 %collective-permute-start.5 = (bf16[2,128,128]{2,1,0:T(8,128)(2,1)S(1)}, bf16[2,128,128]{2,1,0:T(8,128)(2,1)S(1)}, u32[]{:S(2)}, u32[]{:S(2)}) collective-permute-start(bf16[2,128,128]{2,1,0:T(8,128)(2,1)S(1)} %get-tuple-element.26), channel_id=1, source_target_pairs={{0,3},{1,0},{2,1},{3,2},{4,7},{5,4},{6,5},{7,6},{8,11},{9,8},{10,9... | collective-permute-start | bytes 196616 | tf_op jit(solution)/shard_map/ppermute | solution.py:226
  91.7 0.6 copy-start.9
  92.3 0.6 copy-start.11
  92.9 0.6 copy-start.13
  93.6 0.8 copy-start.10
  94.4 0.8 copy-start.12
  95.2 0.8 copy-start.14
Sparse Core Ops, SparseCore 0:
  9.8 29.4 all-gather.1

commit v2 on v1

--- a/solution.py
+++ b/solution.py
@@ -137,11 +137,11 @@
             signal_ref[2 * half + 1, block] = jnp.where(low, pltpu.roll(top, 64, 1), bottom).astype(BF)
 
 
-def turn_body(states_ref, out_ref):
-    images, blocks = states_ref.shape[:2]
-    for block in range(blocks):
-        for image in range(images):
-            out_ref[block, :, 256 * image : 256 * image + 256] = states_ref[image, block].T
+def turn_body(*refs):
+    out_ref = refs[-1]
+    for image, states_ref in enumerate(refs[:-1]):
+        for block in range(states_ref.shape[0]):
+            out_ref[block, :, 256 * image : 256 * image + 256] = states_ref[block].T
 
 
 def taps_body(width, images, *refs):
@@ -160,9 +160,9 @@
                 jnp.concatenate([jnp.where(wide, patches[2 * k], patches[2 * k + 1]) for k in range(5)], 1)
             )
         moved = jnp.concatenate(parts, 0)
-        grads = STEP * jnp.dot(states_ref[block], moved, preferred_element_type=F32)
+        grads = (STEP * jnp.dot(states_ref[block], moved, preferred_element_type=F32)).T
         for tap in range(9):
-            out_ref[block, tap // 3, tap % 3] = grads[:, 64 * tap : 64 * tap + 64]
+            out_ref[block, tap // 3, tap % 3] = grads[64 * tap : 64 * tap + 64]
 
 
 def on_device(states, kernels, adjoint_guess, coarse_gain, terminal):
@@ -181,8 +181,7 @@
     points = adjoint_guess.reshape(cells, channels)
     last_value = terminal.reshape(cells, channels)
     gain = coarse_gain.reshape(cells, channels)
-    arriving = from_right(points.astype(BF))
-    gathered = lax.all_gather(states.reshape(blocks, cells, channels), "dp")
+    arriving = from_right(points)
     slopes, turned = call(
         functools.partial(slope_body, width),
         (shape((blocks, cells, channels), F32), shape((blocks, 9 * channels, channels), BF)),
@@ -208,6 +207,7 @@
         flops=blocks * conv_flops,
         name="residual",
     )(flag, arriving, last_value, points, slopes, turned, gain)
+    own_states, send = lax.optimization_barrier((states.reshape(blocks, cells, channels), send))
     spread = lax.all_to_all(send.reshape(slabs, 16, 128), "layer", 0, 0, tiled=True)
     errors = call(scan_body, shape((slabs, 8, 128), BF), 1, name="scan")(spread)
     error = lax.all_to_all(errors, "layer", 0, 0, tiled=True)
@@ -220,21 +220,23 @@
         name="final",
     )(flag, arriving, last_value, error, gain, relax, slopes, turned)
 
-    received = [lax.dynamic_index_in_dim(signals, here, 0, keepdims=False)]
+    all_states, received = [own_states], [lax.dynamic_index_in_dim(signals, here, 0, keepdims=False)]
     for k in range(1, images):
+        route = [(i, (i + k) % images) for i in range(images)]
+        all_states.append(lax.ppermute(own_states, "dp", route))
         part = lax.dynamic_index_in_dim(signals, (here + k) % images, 0, keepdims=False)
-        received.append(lax.ppermute(part, "dp", [(i, (i + k) % images) for i in range(images)]))
-    order = jnp.stack([(here - k) % images for k in range(images)])
-    ordered = jnp.take(gathered, order, axis=0)
-    states_turned = call(turn_body, shape((blocks, channels, images * cells), BF), 1, name="turn")(ordered)
+        received.append(lax.ppermute(part, "dp", route))
+    states_turned = call(
+        turn_body, shape((blocks, channels, images * cells), BF), images, name="turn"
+    )(*all_states)
     grads = call(
         functools.partial(taps_body, width, images),
-        shape((blocks, 3, 3, channels, channels // images), F32),
+        shape((blocks, 3, 3, channels // images, channels), F32),
         1 + images,
         flops=blocks * conv_flops,
         name="taps",
     )(states_turned, *received)
-    return adjoint.reshape(blocks, 1, height, width, channels), grads
+    return adjoint.reshape(blocks, 1, height, width, channels), jnp.swapaxes(grads, 3, 4)
 
 
 def solution(mesh):

time: 106 us -> 86 us (0.81)
  blocking collectives: 0 us -> 26.7 us
  waiting for transfers between devices: 26.8 us -> 9.34 us
  between operations: 14.3 us -> 0.74 us
  local copies, waits for them, and re-layouts: 13.6 us -> 4.99 us
  starting transfers between devices: 39.2 us -> 31.6 us
  Pallas kernels: 10.1 us -> 12.2 us
  other arithmetic: 1.95 us -> 0 us
    all_to_all x0 -> x1, blocking collectives: none -> 26.7 us  [on_device(): lax.all_to_all(send.reshape(slabs, 16, 128), 'layer', 0, 0, tiled=True)]
    all_to_all x1 -> x0, starting transfers between devices: 13.9 us -> none  [on_device(): lax.all_to_all(send.reshape(slabs, 16, 128), 'layer', 0, 0, tiled=True)]
    all_to_all x1 -> x0, waiting for transfers between devices: 13 us -> none  [on_device(): lax.all_to_all(send.reshape(slabs, 16, 128), 'layer', 0, 0, tiled=True)]
    unnamed x31 -> x18, local copies, waits for them, and re-layouts: 11.7 us -> 4.97 us
    ppermute x3 -> x6, starting transfers between devices: 5.06 us -> 10.1 us  [the longest x3 5.06 us: on_device(): received.append(lax.ppermute(part, 'dp', route))]
    all_to_all x1, waiting for transfers between devices: 11.1 us -> 6.19 us  [on_device(): error = lax.all_to_all(errors, 'layer', 0, 0, tiled=True)]
    gather x1 -> x0, local copies, waits for them, and re-layouts: 1.84 us -> none  [on_device(): ordered = jnp.take(gathered, order, axis=0)]
    convert_element_type x1 -> x0, other arithmetic: 1.62 us -> none  [on_device(): arriving = from_right(points.astype(BF))]
  transfers between devices with their start and end apart: 9 -> 10, of which waited for: 4 -> 6; matrix products, arithmetic and copies ran while one was open for 4% -> 0% of each run, Pallas kernels for 8% -> 5%
where the time goes in v2:
time: 86 us; the launch traced here: 85.6 us
  starting transfers between devices  31.6 us (37%)
  blocking collectives  26.7 us (31%)
  Pallas kernels  12.2 us (14%)
  waiting for transfers between devices  9.34 us (11%)
  local copies, waits for them, and re-layouts  4.99 us (6%)
    all_to_all x1, blocking collectives, on_device(): lax.all_to_all(send.reshape(slabs, 16, 128), 'layer', 0, 0, tiled=True)  26.7 us
    ppermute x3, starting transfers between devices, from_right(): lax.ppermute(points, 'layer', [((i + 1) % slabs, i) for i in range(slabs)])  16.5 us
    all_to_all x1, waiting for transfers between devices, on_device(): error = lax.all_to_all(errors, 'layer', 0, 0, tiled=True)  6.19 us
    all_to_all x1, starting transfers between devices, on_device(): error = lax.all_to_all(errors, 'layer', 0, 0, tiled=True)  5.06 us
    ppermute x3, starting transfers between devices, on_device(): received.append(lax.ppermute(part, 'dp', route))  5.06 us
    ppermute x3, starting transfers between devices, on_device(): all_states.append(lax.ppermute(own_states, 'dp', route))  5.06 us
    unnamed x18, local copies, waits for them, and re-layouts  4.97 us
    pallas_call x2, Pallas kernels, on_device(): call(functools.partial(sweep_body, width), (shape((cells, channels), F32)...  3.84 us
  transfers between devices with their start and end apart: 10, of which 6 were waited for; matrix products, arithmetic and copies ran while one was open for 0% of the time, Pallas kernels for 5%

profile of v2, /device:TPU:1, one launch (start us, length us, event | category | flops | bytes accessed | tf_op | source)
XLA Modules:
  0.0 85.6 jit_solution(7377909567629247973)
XLA Ops:
  0.6 0.0 copy-start
  0.6 3.3 %collective-permute-start = (f32[256,256]{1,0:T(8,128)}, f32[256,256]{1,0:T(8,128)}, u32[]{:S(2)}, u32[]{:S(2)}) collective-permute-start(f32[256,256]{1,0:T(8,128)} %bitcast.29), channel_id=1, source_target_pairs={{4,0},{8,4},{12,8},{16,12},{20,16},{24,20},{28,24},{32,28},{36,32}... | collective-permute-start | bytes 786440 | tf_op jit(solution)/shard_map/ppermute | solution.py:179
  4.0 0.0 copy-start.1
  4.0 1.7 %copy-done.1 = bf16[2,3,3,256,256]{4,3,2,1,0:T(8,128)(2,1)S(1)} copy-done((bf16[2,3,3,256,256]{4,3,2,1,0:T(8,128)(2,1)S(1)}, bf16[2,3,3,256,256]{4,3,2,1,0:T(8,128)(2,1)}, u32[]{:S(2)}) %copy-start.1) | copy-done | bytes 2359320
  5.6 0.0 copy-start.3
  5.6 0.9 %copy-done.3 = bf16[2,1,16,16,256]{4,3,2,1,0:T(8,128)(2,1)S(1)} copy-done((bf16[2,1,16,16,256]{4,3,2,1,0:T(8,128)(2,1)S(1)}, bf16[2,1,16,16,256]{4,3,2,1,0:T(8,128)(2,1)}, u32[]{:S(2)}) %copy-start.3) | copy-done | bytes 262168
  6.6 0.0 copy-start.8
  6.6 0.8 slopes.1
  7.4 0.3 collective-permute-done.arriving_ref
  7.7 0.0 copy-done
  7.7 0.0 copy-done.8
  7.7 2.4 %sweep.2 = (f32[256,256]{1,0:T(8,128)S(1)}, bf16[256,256]{1,0:T(8,128)(2,1)S(1)}) custom-call(s32[1]{0:T(128)} %bitcast.flag_ref, f32[256,256]{1,0:T(8,128)} %collective-permute-done.arriving_ref, f32[256,256]{1,0:T(8,128)S(1)} %bitcast.18, f32[256,256]{1,0:T(8,128)S(1)} %bitcast.30, f32[2,256,256]{2,1,0:T(8,128)S(1)} %get-tuple-element.14.slope_ref, ...), custom_call_target="tpu_custom_call" | custom-call | flops 603979776 | bytes 2000000 | tf_op jit(solution)/shard_map/sweep/pallas_call | solution.py:193
  10.1 0.0 copy-start.2
  10.1 6.3 %collective-permute-start.1 = (bf16[256,256]{1,0:T(8,128)(2,1)S(1)}, bf16[256,256]{1,0:T(8,128)(2,1)S(1)}, u32[]{:S(2)}, u32[]{:S(2)}) collective-permute-start(bf16[256,256]{1,0:T(8,128)(2,1)S(1)} %get-tuple-element.16), channel_id=1, source_target_pairs={{4,0},{8,4},{12,8},{16,12},{20,16},{24,20},{28,24},{32,28},{36,32}... | collective-permute-start | bytes 393224 | tf_op jit(solution)/shard_map/ppermute | solution.py:179
  16.4 1.0 %collective-permute-done.1.arriving_ref = bf16[256,256]{1,0:T(8,128)(2,1)S(1)} collective-permute-done((bf16[256,256]{1,0:T(8,128)(2,1)S(1)}, bf16[256,256]{1,0:T(8,128)(2,1)S(1)}, u32[]{:S(2)}, u32[]{:S(2)}) %collective-permute-start.1) | collective-permute-done | bytes 131104 | tf_op jit(solution)/shard_map/ppermute | solution.py:179
  17.4 1.4 %sweep.3 = (f32[256,256]{1,0:T(8,128)S(1)}, bf16[256,256]{1,0:T(8,128)(2,1)S(1)}) custom-call(s32[1]{0:T(128)} %bitcast.flag_ref, bf16[256,256]{1,0:T(8,128)(2,1)S(1)} %collective-permute-done.1.arriving_ref, f32[256,256]{1,0:T(8,128)S(1)} %bitcast.19, f32[256,256]{1,0:T(8,128)S(1)} %get-tuple-element.17.points_ref, ...), custom_call_target="tpu_custom_call" | custom-call | flops 603979776 | bytes 2000000 | tf_op jit(solution)/shard_map/sweep/pallas_call | solution.py:193
  18.9 6.8 %collective-permute-start.2 = (bf16[256,256]{1,0:T(8,128)(2,1)S(1)}, bf16[256,256]{1,0:T(8,128)(2,1)S(1)}, u32[]{:S(2)}, u32[]{:S(2)}) collective-permute-start(bf16[256,256]{1,0:T(8,128)(2,1)S(1)} %get-tuple-element.18), channel_id=1, source_target_pairs={{4,0},{8,4},{12,8},{16,12},{20,16},{24,20},{28,24},{32,28},{36,32}... | collective-permute-start | bytes 393224 | tf_op jit(solution)/shard_map/ppermute | solution.py:179
  25.7 1.0 %collective-permute-done.2.arriving_ref = bf16[256,256]{1,0:T(8,128)(2,1)S(1)} collective-permute-done((bf16[256,256]{1,0:T(8,128)(2,1)S(1)}, bf16[256,256]{1,0:T(8,128)(2,1)S(1)}, u32[]{:S(2)}, u32[]{:S(2)}) %collective-permute-start.2) | collective-permute-done | bytes 131104 | tf_op jit(solution)/shard_map/ppermute | solution.py:179
  26.7 0.0 copy-done.2
  26.7 1.4 %residual.1 = (f32[256,256]{1,0:T(8,128)S(1)}, bf16[32,2,16,128]{3,2,1,0:T(8,128)(2,1)S(1)}) custom-call(s32[1]{0:T(128)} %bitcast.flag_ref, bf16[256,256]{1,0:T(8,128)(2,1)S(1)} %collective-permute-done.2.arriving_ref, f32[256,256]{1,0:T(8,128)S(1)} %bitcast.20, f32[256,256]{1,0:T(8,128)S(1)} %get-tuple-element.19.points_ref, ...), custom_call_target="tpu_custom_call" | custom-call | flops 603979776 | bytes 2000000 | tf_op jit(solution)/shard_map/residual/pallas_call | solution.py:202
  28.1 0.0 copy-start.6
  28.1 0.7 copy-done.6
  28.8 26.7 %all_to_all.10.given_ref = bf16[64,16,128]{2,1,0:T(8,128)(2,1)S(1)} all-to-all(bf16[64,16,128]{2,1,0:T(8,128)(2,1)S(1)} %bitcast.28), channel_id=1, replica_groups=mesh['layer'=64,'dp'=4] {'layer'}, dimensions={0} | all-to-all | bytes 524288 | tf_op jit(solution)/shard_map/all_to_all | solution.py:211
  55.5 0.2 scan.1
  55.7 0.0 copy-start.5
  55.7 0.6 copy-done.5
  56.4 5.1 %all-to-all-start.1 = ((bf16[64,8,128]{2,1,0:T(8,128)(2,1)}), bf16[64,8,128]{2,1,0:T(8,128)(2,1)}, u32[]{:S(2)}, u32[]{:S(2)}) async-start(bf16[64,8,128]{2,1,0:T(8,128)(2,1)} %copy-done.5), calls=%async_computation.1 | async-start | bytes 262144 | tf_op jit(solution)/shard_map/all_to_all | solution.py:213
  61.5 1.4 %collective-permute-start.3 = (bf16[2,256,256]{2,1,0:T(8,128)(2,1)}, bf16[2,256,256]{2,1,0:T(8,128)(2,1)}, u32[]{:S(2)}, u32[]{:S(2)}) collective-permute-start(bf16[2,256,256]{2,1,0:T(8,128)(2,1)} %bitcast.24), channel_id=1, source_target_pairs={{0,1},{1,2},{2,3},{3,0},{4,5},{5,6},{6,7},{7,4},{8,9},{9,10},{10,1... | collective-permute-start | bytes 786440 | tf_op jit(solution)/shard_map/ppermute | solution.py:226
  62.8 2.6 %collective-permute-start.4 = (bf16[2,256,256]{2,1,0:T(8,128)(2,1)}, bf16[2,256,256]{2,1,0:T(8,128)(2,1)}, u32[]{:S(2)}, u32[]{:S(2)}) collective-permute-start(bf16[2,256,256]{2,1,0:T(8,128)(2,1)} %bitcast.25), channel_id=1, source_target_pairs={{0,2},{1,3},{2,0},{3,1},{4,6},{5,7},{6,4},{7,5},{8,10},{9,11},{10,... | collective-permute-start | bytes 786440 | tf_op jit(solution)/shard_map/ppermute | solution.py:226
  65.5 1.1 %collective-permute-start.5 = (bf16[2,256,256]{2,1,0:T(8,128)(2,1)}, bf16[2,256,256]{2,1,0:T(8,128)(2,1)}, u32[]{:S(2)}, u32[]{:S(2)}) collective-permute-start(bf16[2,256,256]{2,1,0:T(8,128)(2,1)} %bitcast.26), channel_id=1, source_target_pairs={{0,3},{1,0},{2,1},{3,2},{4,7},{5,4},{6,5},{7,6},{8,11},{9,8},{10,9... | collective-permute-start | bytes 786440 | tf_op jit(solution)/shard_map/ppermute | solution.py:226
  66.5 6.2 %all-to-all-done.1.error_ref = bf16[64,8,128]{2,1,0:T(8,128)(2,1)} async-done(((bf16[64,8,128]{2,1,0:T(8,128)(2,1)}), bf16[64,8,128]{2,1,0:T(8,128)(2,1)}, u32[]{:S(2)}, u32[]{:S(2)}) %all-to-all-start.1) | async-done | bytes 131104 | tf_op jit(solution)/shard_map/all_to_all | solution.py:213
  72.7 0.0 copy-start.4
  72.7 0.0 copy-start.7
  72.7 1.0 %copy-done.7 = f32[256,256]{1,0:T(8,128)S(1)} copy-done((f32[256,256]{1,0:T(8,128)S(1)}, f32[256,256]{1,0:T(8,128)}, u32[]{:S(2)}) %copy-start.7) | copy-done | bytes 262168
  73.7 2.2 %final.1 = (f32[2,256,256]{2,1,0:T(8,128)}, bf16[4,2,128,128]{3,2,1,0:T(8,128)(2,1)S(1)}) custom-call(s32[1]{0:T(128)} %bitcast.flag_ref, bf16[256,256]{1,0:T(8,128)(2,1)S(1)} %collective-permute-done.2.arriving_ref, f32[256,256]{1,0:T(8,128)S(1)} %bitcast.21, bf16[64,8,128]{2,1,0:T(8,128)(2,1)} %all-to-all-done.1.error_ref, f32[256,256]{1,0:T(8,128)S(1)} %bitcast.23, ...), custom_call_target="tpu_custom_call" | custom-call | flops 301989888 | bytes 2000000 | tf_op jit(solution)/shard_map/final/pallas_call | solution.py:214
  76.0 1.4 %collective-permute-start.6 = (bf16[2,128,128]{2,1,0:T(8,128)(2,1)S(1)}, bf16[2,128,128]{2,1,0:T(8,128)(2,1)S(1)}, u32[]{:S(2)}, u32[]{:S(2)}) collective-permute-start(bf16[2,128,128]{2,1,0:T(8,128)(2,1)S(1)} %get-tuple-element.30), channel_id=1, source_target_pairs={{0,1},{1,2},{2,3},{3,0},{4,5},{5,6},{6,7},{7,4},{8,9},{9,10},{10,1... | collective-permute-start | bytes 196616 | tf_op jit(solution)/shard_map/ppermute | solution.py:228
  77.3 2.6 %collective-permute-start.7 = (bf16[2,128,128]{2,1,0:T(8,128)(2,1)S(1)}, bf16[2,128,128]{2,1,0:T(8,128)(2,1)S(1)}, u32[]{:S(2)}, u32[]{:S(2)}) collective-permute-start(bf16[2,128,128]{2,1,0:T(8,128)(2,1)S(1)} %get-tuple-element.29), channel_id=1, source_target_pairs={{0,2},{1,3},{2,0},{3,1},{4,6},{5,7},{6,4},{7,5},{8,10},{9,11},{10,... | collective-permute-start | bytes 196616 | tf_op jit(solution)/shard_map/ppermute | solution.py:228
  80.0 0.0 collective-permute-done.3.refs_1_
  80.0 1.1 %collective-permute-start.8 = (bf16[2,128,128]{2,1,0:T(8,128)(2,1)S(1)}, bf16[2,128,128]{2,1,0:T(8,128)(2,1)S(1)}, u32[]{:S(2)}, u32[]{:S(2)}) collective-permute-start(bf16[2,128,128]{2,1,0:T(8,128)(2,1)S(1)} %get-tuple-element.28), channel_id=1, source_target_pairs={{0,3},{1,0},{2,1},{3,2},{4,7},{5,4},{6,5},{7,6},{8,11},{9,8},{10,9... | collective-permute-start | bytes 196616 | tf_op jit(solution)/shard_map/ppermute | solution.py:228
  81.0 0.0 collective-permute-done.4.refs_2_
  81.0 0.0 collective-permute-done.5.refs_3_
  81.0 0.0 copy-done.4
  81.0 1.4 %turn.1.refs_0_ = bf16[2,256,1024]{2,1,0:T(8,128)(2,1)S(1)} custom-call(bf16[2,256,256]{2,1,0:T(8,128)(2,1)S(1)} %bitcast.27, bf16[2,256,256]{2,1,0:T(8,128)(2,1)} %collective-permute-done.3.refs_1_, bf16[2,256,256]{2,1,0:T(8,128)(2,1)} %collective-permute-done.4.refs_2_, bf16[2,256,256]{2,1,0:T(8,128)(2,1)} %collective-permute-done.5.refs_3_), custom_call_target="tpu_custom_call" | custom-call | bytes 2000000 | tf_op jit(solution)/shard_map/turn/pallas_call | solution.py:229
  82.5 0.0 collective-permute-done.6.refs_2_
  82.5 0.4 collective-permute-done.7.refs_3_
  82.9 0.5 collective-permute-done.8.refs_4_
  83.4 2.3 %taps.1 = f32[2,3,3,64,256]{4,3,2,1,0:T(8,128)} custom-call(bf16[2,256,1024]{2,1,0:T(8,128)(2,1)S(1)} %turn.1.refs_0_, bf16[2,128,128]{2,1,0:T(8,128)(2,1)S(1)} %get-tuple-element.31.refs_1_, bf16[2,128,128]{2,1,0:T(8,128)(2,1)S(1)} %collective-permute-done.6.refs_2_, bf16[2,128,128]{2,1,0:T(8,128)(2,1)S(1)} %collective-permute-done.7.refs_3_, ...), custom_call_target="tpu_custom_call" | custom-call | flops 603979776 | bytes 2000000 | tf_op jit(solution)/shard_map/taps/pallas_call | solution.py:232
  (1 shorter events, 0.0 us)
Async XLA Ops:
  0.6 7.1 %copy-start = (f32[1,16,16,256]{3,2,1,0:T(8,128)S(1)}, f32[1,16,16,256]{3,2,1,0:T(8,128)}, u32[]{:S(2)}) copy-start(f32[1,16,16,256]{3,2,1,0:T(8,128)} %param.9) | copy-start | bytes 786436
  0.6 7.1 %collective-permute-start = (f32[256,256]{1,0:T(8,128)}, f32[256,256]{1,0:T(8,128)}, u32[]{:S(2)}, u32[]{:S(2)}) collective-permute-start(f32[256,256]{1,0:T(8,128)} %bitcast.29), channel_id=1, source_target_pairs={{4,0},{8,4},{12,8},{16,12},{20,16},{24,20},{28,24},{32,28},{36,32}... | collective-permute-start | bytes 786440 | tf_op jit(solution)/shard_map/ppermute | solution.py:179
  4.0 1.7 %copy-start.1 = (bf16[2,3,3,256,256]{4,3,2,1,0:T(8,128)(2,1)S(1)}, bf16[2,3,3,256,256]{4,3,2,1,0:T(8,128)(2,1)}, u32[]{:S(2)}) copy-start(bf16[2,3,3,256,256]{4,3,2,1,0:T(8,128)(2,1)} %kernels_ref.1) | copy-start | bytes 7077892
  5.6 0.9 %copy-start.3 = (bf16[2,1,16,16,256]{4,3,2,1,0:T(8,128)(2,1)S(1)}, bf16[2,1,16,16,256]{4,3,2,1,0:T(8,128)(2,1)}, u32[]{:S(2)}) copy-start(bf16[2,1,16,16,256]{4,3,2,1,0:T(8,128)(2,1)} %states_ref.1) | copy-start | bytes 786436
  6.6 1.1 %copy-start.8 = (f32[1,1,16,16,256]{4,3,2,1,0:T(8,128)S(1)}, f32[1,1,16,16,256]{4,3,2,1,0:T(8,128)}, u32[]{:S(2)}) copy-start(f32[1,1,16,16,256]{4,3,2,1,0:T(8,128)} %param.7) | copy-start | bytes 786436
  10.1 16.6 %copy-start.2 = (f32[1,16,16,256]{3,2,1,0:T(8,128)S(1)}, f32[1,16,16,256]{3,2,1,0:T(8,128)}, u32[]{:S(2)}) copy-start(f32[1,16,16,256]{3,2,1,0:T(8,128)} %param.8) | copy-start | bytes 786436
  10.1 7.3 %collective-permute-start.1 = (bf16[256,256]{1,0:T(8,128)(2,1)S(1)}, bf16[256,256]{1,0:T(8,128)(2,1)S(1)}, u32[]{:S(2)}, u32[]{:S(2)}) collective-permute-start(bf16[256,256]{1,0:T(8,128)(2,1)S(1)} %get-tuple-element.16), channel_id=1, source_target_pairs={{4,0},{8,4},{12,8},{16,12},{20,16},{24,20},{28,24},{32,28},{36,32}... | collective-permute-start | bytes 393224 | tf_op jit(solution)/shard_map/ppermute | solution.py:179
  18.9 7.8 %collective-permute-start.2 = (bf16[256,256]{1,0:T(8,128)(2,1)S(1)}, bf16[256,256]{1,0:T(8,128)(2,1)S(1)}, u32[]{:S(2)}, u32[]{:S(2)}) collective-permute-start(bf16[256,256]{1,0:T(8,128)(2,1)S(1)} %get-tuple-element.18), channel_id=1, source_target_pairs={{4,0},{8,4},{12,8},{16,12},{20,16},{24,20},{28,24},{32,28},{36,32}... | collective-permute-start | bytes 393224 | tf_op jit(solution)/shard_map/ppermute | solution.py:179
  28.1 0.7 copy-start.6
  55.7 0.7 copy-start.5
  56.4 16.3 %all-to-all-start.1 = ((bf16[64,8,128]{2,1,0:T(8,128)(2,1)}), bf16[64,8,128]{2,1,0:T(8,128)(2,1)}, u32[]{:S(2)}, u32[]{:S(2)}) async-start(bf16[64,8,128]{2,1,0:T(8,128)(2,1)} %copy-done.5), calls=%async_computation.1 | async-start | bytes 262144 | tf_op jit(solution)/shard_map/all_to_all | solution.py:213
  61.5 18.5 %collective-permute-start.3 = (bf16[2,256,256]{2,1,0:T(8,128)(2,1)}, bf16[2,256,256]{2,1,0:T(8,128)(2,1)}, u32[]{:S(2)}, u32[]{:S(2)}) collective-permute-start(bf16[2,256,256]{2,1,0:T(8,128)(2,1)} %bitcast.24), channel_id=1, source_target_pairs={{0,1},{1,2},{2,3},{3,0},{4,5},{5,6},{6,7},{7,4},{8,9},{9,10},{10,1... | collective-permute-start | bytes 786440 | tf_op jit(solution)/shard_map/ppermute | solution.py:226
  62.8 18.2 %collective-permute-start.4 = (bf16[2,256,256]{2,1,0:T(8,128)(2,1)}, bf16[2,256,256]{2,1,0:T(8,128)(2,1)}, u32[]{:S(2)}, u32[]{:S(2)}) collective-permute-start(bf16[2,256,256]{2,1,0:T(8,128)(2,1)} %bitcast.25), channel_id=1, source_target_pairs={{0,2},{1,3},{2,0},{3,1},{4,6},{5,7},{6,4},{7,5},{8,10},{9,11},{10,... | collective-permute-start | bytes 786440 | tf_op jit(solution)/shard_map/ppermute | solution.py:226
  65.5 15.6 %collective-permute-start.5 = (bf16[2,256,256]{2,1,0:T(8,128)(2,1)}, bf16[2,256,256]{2,1,0:T(8,128)(2,1)}, u32[]{:S(2)}, u32[]{:S(2)}) collective-permute-start(bf16[2,256,256]{2,1,0:T(8,128)(2,1)} %bitcast.26), channel_id=1, source_target_pairs={{0,3},{1,0},{2,1},{3,2},{4,7},{5,4},{6,5},{7,6},{8,11},{9,8},{10,9... | collective-permute-start | bytes 786440 | tf_op jit(solution)/shard_map/ppermute | solution.py:226
  72.7 8.3 %copy-start.4 = (bf16[2,1,16,16,256]{4,3,2,1,0:T(8,128)(2,1)S(1)}, bf16[2,1,16,16,256]{4,3,2,1,0:T(8,128)(2,1)}, u32[]{:S(2)}) copy-start(bf16[2,1,16,16,256]{4,3,2,1,0:T(8,128)(2,1)} %states_ref.1) | copy-start | bytes 786436
  72.7 1.0 %copy-start.7 = (f32[256,256]{1,0:T(8,128)S(1)}, f32[256,256]{1,0:T(8,128)}, u32[]{:S(2)}) copy-start(f32[256,256]{1,0:T(8,128)} %copy-done.6) | copy-start | bytes 786436
  76.0 6.5 %collective-permute-start.6 = (bf16[2,128,128]{2,1,0:T(8,128)(2,1)S(1)}, bf16[2,128,128]{2,1,0:T(8,128)(2,1)S(1)}, u32[]{:S(2)}, u32[]{:S(2)}) collective-permute-start(bf16[2,128,128]{2,1,0:T(8,128)(2,1)S(1)} %get-tuple-element.30), channel_id=1, source_target_pairs={{0,1},{1,2},{2,3},{3,0},{4,5},{5,6},{6,7},{7,4},{8,9},{9,10},{10,1... | collective-permute-start | bytes 196616 | tf_op jit(solution)/shard_map/ppermute | solution.py:228
  77.3 5.5 %collective-permute-start.7 = (bf16[2,128,128]{2,1,0:T(8,128)(2,1)S(1)}, bf16[2,128,128]{2,1,0:T(8,128)(2,1)S(1)}, u32[]{:S(2)}, u32[]{:S(2)}) collective-permute-start(bf16[2,128,128]{2,1,0:T(8,128)(2,1)S(1)} %get-tuple-element.29), channel_id=1, source_target_pairs={{0,2},{1,3},{2,0},{3,1},{4,6},{5,7},{6,4},{7,5},{8,10},{9,11},{10,... | collective-permute-start | bytes 196616 | tf_op jit(solution)/shard_map/ppermute | solution.py:228
  80.0 3.4 %collective-permute-start.8 = (bf16[2,128,128]{2,1,0:T(8,128)(2,1)S(1)}, bf16[2,128,128]{2,1,0:T(8,128)(2,1)S(1)}, u32[]{:S(2)}, u32[]{:S(2)}) collective-permute-start(bf16[2,128,128]{2,1,0:T(8,128)(2,1)S(1)} %get-tuple-element.28), channel_id=1, source_target_pairs={{0,3},{1,0},{2,1},{3,2},{4,7},{5,4},{6,5},{7,6},{8,11},{9,8},{10,9... | collective-permute-start | bytes 196616 | tf_op jit(solution)/shard_map/ppermute | solution.py:228

commit v3 on v2

v3 whole, which is shorter than its diff:
```python
import functools

import jax
import jax.numpy as jnp
from jax import lax
from jax.experimental import pallas as pl
from jax.experimental.pallas import tpu as pltpu
from jax.sharding import PartitionSpec as P

STEP = 0.5
DAMPING = 0.5
BF = jnp.bfloat16
F32 = jnp.float32
VMEM_LIMIT = 12 * 1024 * 1024


def call(body, outs, ins, flops=0, moved=2_000_000, name=None, scratch=(), far_in=(), far_out=(), alias=None):
    def spec(far):
        return pl.BlockSpec(memory_space=pltpu.HBM if far else pltpu.VMEM)

    single = not isinstance(outs, tuple)
    placed = tuple(
        (pltpu.HBM if k in far_out else pltpu.VMEM)(out.shape, out.dtype)
        for k, out in enumerate((outs,) if single else outs)
    )
    ins = [
        pltpu.with_memory_space_constraint(value, pltpu.HBM if k in far_in else pltpu.VMEM)
        for k, value in enumerate(ins)
    ]
    out_specs = [spec(k in far_out) for k in range(1 if single else len(outs))]
    return pl.pallas_call(
        body,
        out_shape=placed[0] if single else placed,
        in_specs=[spec(k in far_in) for k in range(len(ins))],
        out_specs=out_specs[0] if single else tuple(out_specs),
        scratch_shapes=scratch,
        input_output_aliases=alias or {},
        compiler_params=pltpu.CompilerParams(vmem_limit_bytes=VMEM_LIMIT),
        cost_estimate=pl.CostEstimate(flops=flops, bytes_accessed=moved, transcendentals=0),
        name=name,
    )(*ins)


def is_even():
    return lax.axis_index("layer") % 2 == 0


def is_last():
    return lax.axis_index("layer") == lax.axis_size("layer") - 1


def columns(value, width):
    cells = value.shape[0]
    col = lax.broadcasted_iota(jnp.int32, value.shape, 0) % width
    ahead = jnp.where(col == width - 1, 0.0, pltpu.roll(value, cells - 1, 0))
    behind = jnp.where(col == 0, 0.0, pltpu.roll(value, 1, 0))
    return ahead, value, behind


def rows(value, width):
    edge = jnp.zeros((width, value.shape[1]), value.dtype)
    return jnp.concatenate([edge, value, edge], 0)


def forward_patches(value, width):
    cells = value.shape[0]
    ahead, here, behind = columns(value, width)
    padded = [rows(part.astype(BF), width) for part in (behind, here, ahead)]
    return [padded[j][i * width : i * width + cells] for i in range(3) for j in range(3)]


def adjoint_patches(value, width):
    cells = value.shape[0]
    ahead, here, behind = columns(value, width)
    padded = [rows(part.astype(BF), width) for part in (ahead, here, behind)]
    return [padded[j][(2 - i) * width : (2 - i) * width + cells] for i in range(3) for j in range(3)]


def adjoint_conv(signal, turned_ref, block, width):
    patches = jnp.concatenate(adjoint_patches(signal, width), 1)
    return jnp.dot(patches, turned_ref[block], preferred_element_type=F32)


def block_map(value, slope, turned_ref, block, width):
    signal = (slope * value).astype(BF).astype(F32)
    return value + STEP * adjoint_conv(signal, turned_ref, block, width)


def relaxed(right, slope_ref, turned_ref, width):
    for block in range(turned_ref.shape[0] - 1, -1, -1):
        right = block_map(right, slope_ref[block], turned_ref, block, width)
    return right


def slope_body(width, states_far, kernels_far, points_far, slope_ref, turned_ref, points_ref, states_ref, kernels_ref, sems):
    blocks, height, _, channels = states_ref.shape
    held = [pltpu.make_async_copy(states_far.at[:, 0], states_ref, sems.at[blocks])]
    for block in range(blocks):
        held.append(pltpu.make_async_copy(kernels_far.at[block], kernels_ref.at[block], sems.at[block]))
    held.append(pltpu.make_async_copy(points_far, points_ref, sems.at[blocks + 1]))
    for copy in held:
        copy.start()
    held[0].wait()
    for block in range(blocks):
        value = states_ref[block].reshape(height * width, channels).astype(F32)
        patches = jnp.concatenate(forward_patches(value, width), 1)
        held[1 + block].wait()
        taps = kernels_ref[block].reshape(9 * channels, channels)
        act = jnp.tanh(jnp.dot(patches, taps, preferred_element_type=F32))
        slope_ref[block] = 1.0 - act * act
        for i in range(3):
            for j in range(3):
                at = (i * 3 + j) * channels
                turned_ref[block, at : at + channels, :] = kernels_ref[block, i, j].T
    held[-1].wait()


def fetch(far_ref, near_ref, sem):
    copy = pltpu.make_async_copy(far_ref, near_ref, sem)
    copy.start()
    copy.wait()


def enter(right_ref, swapped_ref, crossed_ref, terminal_far, sem):
    @pl.when(is_even())
    def _():
        right_ref[...] = swapped_ref[...].astype(F32)

    @pl.when(jnp.logical_not(jnp.logical_or(is_even(), is_last())))
    def _():
        right_ref[...] = crossed_ref[...].astype(F32)

    @pl.when(is_last())
    def _():
        fetch(terminal_far, right_ref, sem)


def sweep(right, slope_ref, turned_ref, points_ref, width):
    points = points_ref[...]
    points_ref[...] = points + DAMPING * (relaxed(right, slope_ref, turned_ref, width) - points)


def even_body(width, swapped_ref, slope_ref, turned_ref, _, points_ref, send_ref):
    @pl.when(is_even())
    def _():
        sweep(swapped_ref[...].astype(F32), slope_ref, turned_ref, points_ref, width)

    send_ref[...] = points_ref[...].astype(BF)


def odd_body(width, crossed_ref, terminal_far, slope_ref, turned_ref, _, points_ref, send_ref, right_ref, sem):
    @pl.when(is_last())
    def _():
        fetch(terminal_far, right_ref, sem)

    @pl.when(jnp.logical_not(jnp.logical_or(is_even(), is_last())))
    def _():
        right_ref[...] = crossed_ref[...].astype(F32)

    @pl.when(jnp.logical_not(is_even()))
    def _():
        sweep(right_ref[...], slope_ref, turned_ref, points_ref, width)

    send_ref[...] = points_ref[...].astype(BF)


def sweep_body(width, swapped_ref, crossed_ref, terminal_far, slope_ref, turned_ref, _, points_ref, send_ref, right_ref, sem):
    enter(right_ref, swapped_ref, crossed_ref, terminal_far, sem)
    sweep(right_ref[...], slope_ref, turned_ref, points_ref, width)
    send_ref[...] = points_ref[...].astype(BF)


def residual_body(width, swapped_ref, crossed_ref, terminal_far, slope_ref, turned_ref, _, gain_far, relax_far, send_far, points_ref, right_ref, gain_ref, relax_ref, send_ref, sem, sems):
    gain_copy = pltpu.make_async_copy(gain_far, gain_ref, sems.at[0])
    gain_copy.start()
    enter(right_ref, swapped_ref, crossed_ref, terminal_far, sem)
    right = right_ref[...]
    relax = relaxed(right, slope_ref, turned_ref, width)
    residual = (relax - points_ref[...]).reshape(32, 8, 256)
    gain_copy.wait()
    decay = (1.0 - gain_ref[...]).reshape(32, 8, 256)
    for half in range(2):
        lanes = slice(128 * half, 128 * half + 128)
        send_ref[:, half] = jnp.concatenate([residual[:, :, lanes], decay[:, :, lanes]], 1).astype(BF)
    send_copy = pltpu.make_async_copy(send_ref, send_far, sems.at[1])
    send_copy.start()
    relax_ref[...] = relax
    relax_copy = pltpu.make_async_copy(relax_ref, relax_far, sems.at[2])
    relax_copy.start()
    points_ref[...] = right
    send_copy.wait()
    relax_copy.wait()


def scan_body(given_ref, out_far, out_ref, sem):
    count = given_ref.shape[0]
    error = jnp.zeros((8, 128), F32)
    for at in range(count - 1, -1, -1):
        out_ref[at] = error.astype(BF)
        term = given_ref[at].astype(F32)
        error = error - term[8:] * error + term[:8]
    copy = pltpu.make_async_copy(out_ref, out_far, sem)
    copy.start()
    copy.wait()


def final_body(width, points_ref, error_ref, slope_ref, turned_ref, inner_ref, error_out_ref, signal_ref):
    error = error_ref[...].astype(F32).reshape(32, 2, 8, 128)
    error = jnp.concatenate([error[:, 0], error[:, 1]], 2).reshape(256, 256)
    error_out_ref[...] = error
    right = points_ref[...] + error
    last = (slope_ref[1] * right).astype(BF).astype(F32)
    inner = right + STEP * adjoint_conv(last, turned_ref, 1, width)
    inner_ref[...] = inner
    first = (slope_ref[0] * inner).astype(BF).astype(F32)
    low = lax.broadcasted_iota(jnp.int32, (128, 128), 1) < 64
    for block, signal in ((0, first), (1, last)):
        for half in range(2):
            top = signal[:128, 128 * half : 128 * half + 128]
            bottom = signal[128:, 128 * half : 128 * half + 128]
            signal_ref[2 * half, block] = jnp.where(low, top, pltpu.roll(bottom, 64, 1)).astype(BF)
            signal_ref[2 * half + 1, block] = jnp.where(low, pltpu.roll(top, 64, 1), bottom).astype(BF)


def corrected_body(error_ref, gain_ref, relax_ref, inner_ref, adjoint_far, out_ref, sems):
    inner_copy = pltpu.make_async_copy(inner_ref, adjoint_far.at[1], sems.at[1])
    inner_copy.start()
    out_ref[...] = gain_ref[...] * error_ref[...] + relax_ref[...]
    out_copy = pltpu.make_async_copy(out_ref, adjoint_far.at[0], sems.at[0])
    out_copy.start()
    inner_copy.wait()
    out_copy.wait()


def turn_body(*refs):
    out_ref = refs[-1]
    for image, states_ref in enumerate(refs[:-1]):
        for block in range(states_ref.shape[0]):
            out_ref[block, :, 256 * image : 256 * image + 256] = states_ref[block].T


def taps_body(width, *refs, images):
    states_ref, signal_refs = refs[0], refs[1 : 1 + images]
    out_far, out_ref, sems = refs[1 + images :]
    copies = []
    low = lax.broadcasted_iota(jnp.int32, (128, 128), 1) < 64
    wide = lax.broadcasted_iota(jnp.int32, (256, 128), 1) < 64
    for block in range(out_ref.shape[0]):
        parts = []
        for image in range(images):
            packed = signal_refs[image][block].astype(F32)
            other = pltpu.roll(packed, 64, 1)
            both = jnp.concatenate([jnp.where(low, packed, other), jnp.where(low, other, packed)], 0)
            patches = adjoint_patches(both, width)
            patches.append(patches[-1])
            parts.append(
                jnp.concatenate([jnp.where(wide, patches[2 * k], patches[2 * k + 1]) for k in range(5)], 1)
            )
        moved = jnp.concatenate(parts, 0)
        grads = (STEP * jnp.dot(states_ref[block], moved, preferred_element_type=F32)).T
        for tap in range(9):
            out_ref[block, tap // 3, tap % 3] = grads[64 * tap : 64 * tap + 64]
        copies.append(pltpu.make_async_copy(out_ref.at[block], out_far.at[block], sems.at[block]))
        copies[-1].start()
    for copy in copies:
        copy.wait()


def on_device(states, kernels, adjoint_guess, coarse_gain, terminal):
    blocks, _, height, width, channels = states.shape
    cells = height * width
    slabs = lax.axis_size("layer")
    images = lax.axis_size("dp")
    here = lax.axis_index("dp")
    slab = lax.axis_index("layer")
    conv_flops = 2 * cells * 9 * channels * channels
    shape = jax.ShapeDtypeStruct

    def swapped(part):
        return lax.ppermute(part, "layer", [(i ^ 1, i) for i in range(slabs)])

    def crossed(part):
        route = [((i + 1) % slabs if i % 2 else (i - 1) % slabs, i) for i in range(slabs)]
        return lax.ppermute(part, "layer", route)

    whole = shape((cells, channels), F32)
    rounded = shape((cells, channels), BF)

    def step(body, outs, *ins, name, **more):
        return call(functools.partial(body, width), outs, ins, flops=blocks * conv_flops, name=name, **more)

    def right_of(part):
        return jnp.where(slab == slabs - 1, jnp.zeros_like(part), part)

    points = adjoint_guess.reshape(cells, channels)
    last_value = terminal.reshape(cells, channels)
    gain = coarse_gain.reshape(cells, channels)
    rough = points.astype(BF)
    across, beside = crossed(rough), swapped(rough)
    slopes, turned, points = step(
        slope_body,
        (shape((blocks, cells, channels), F32), shape((blocks, 9 * channels, channels), BF), whole),
        states,
        kernels,
        points,
        name="slopes",
        far_in=(0, 1, 2),
        scratch=(
            pltpu.VMEM((blocks, height, width, channels), BF),
            pltpu.VMEM((blocks, 3, 3, channels, channels), BF),
            pltpu.SemaphoreType.DMA((blocks + 2,)),
        ),
    )
    points, send = step(
        even_body, (whole, rounded), beside, slopes, turned, points, name="even", alias={3: 0}
    )
    next_across = crossed(send)
    right_scratch = (pltpu.VMEM((cells, channels), F32), pltpu.SemaphoreType.DMA)
    points, send = step(
        odd_body,
        (whole, rounded),
        across,
        last_value,
        slopes,
        turned,
        points,
        name="odd",
        alias={4: 0},
        far_in=(1,),
        scratch=right_scratch,
    )
    beside, across = swapped(send), right_of(next_across)
    points, send = step(
        sweep_body,
        (whole, rounded),
        beside,
        across,
        last_value,
        slopes,
        turned,
        points,
        name="sweep",
        alias={5: 0},
        far_in=(2,),
        scratch=right_scratch,
    )
    across, beside = right_of(crossed(send)), swapped(send)
    packed = (32, 2, 16, 128)
    relax, send, points = step(
        residual_body,
        (whole, shape(packed, BF), whole),
        beside,
        across,
        last_value,
        slopes,
        turned,
        points,
        gain,
        name="residual",
        far_in=(2, 6),
        far_out=(0, 1),
        alias={5: 2},
        scratch=(
            pltpu.VMEM((cells, channels), F32),
            pltpu.VMEM((cells, channels), F32),
            pltpu.VMEM((cells, channels), F32),
            pltpu.VMEM(packed, BF),
            pltpu.SemaphoreType.DMA,
            pltpu.SemaphoreType.DMA((3,)),
        ),
    )

    def spread(parts):
        return lax.all_to_all(parts, "layer", 0, 0, tiled=True)

    own_states, send = lax.optimization_barrier((states.reshape(blocks, cells, channels), send))
    errors = call(
        scan_body,
        shape((slabs, 8, 128), BF),
        (spread(send.reshape(slabs, 16, 128)),),
        name="scan",
        moved=0,
        far_out=(0,),
        scratch=(pltpu.VMEM((slabs, 8, 128), BF), pltpu.SemaphoreType.DMA),
    )
    error = spread(errors)
    all_states = [own_states]
    for k in range(1, images):
        all_states.append(lax.ppermute(own_states, "dp", [(i, (i + k) % images) for i in range(images)]))
    states_turned = call(
        turn_body, shape((blocks, channels, images * cells), BF), all_states, name="turn"
    )
    error, states_turned = lax.optimization_barrier((error, states_turned))
    inner, error, signals = step(
        final_body,
        (whole, whole, shape((images, blocks, 128, 128), BF)),
        points,
        error,
        slopes,
        turned,
        name="final",
    )

    received = [lax.dynamic_index_in_dim(signals, here, 0, keepdims=False)]
    for k in range(1, images):
        part = lax.dynamic_index_in_dim(signals, (here + k) % images, 0, keepdims=False)
        received.append(lax.ppermute(part, "dp", [(i, (i + k) % images) for i in range(images)]))
    adjoint = call(
        corrected_body, shape((blocks, cells, channels), F32), (error, gain, relax, inner), name="corrected", far_out=(0,),
        scratch=(pltpu.VMEM((cells, channels), F32), pltpu.SemaphoreType.DMA((2,))),
    )
    slices = (blocks, 3, 3, channels // images, channels)
    grads = step(
        functools.partial(taps_body, images=images),
        shape(slices, F32),
        states_turned,
        *received,
        name="taps",
        far_out=(0,),
        scratch=(pltpu.VMEM(slices, F32), pltpu.SemaphoreType.DMA((blocks,))),
    )
    return adjoint.reshape(blocks, 1, height, width, channels), jnp.swapaxes(grads, 3, 4)


def solution(mesh):
    in_specs = (
        P("layer", "dp", None, None, None),
        P("layer", None, None, None, None),
        P("layer", "dp", None, None, None),
        P("layer", None, None, None),
        P("dp", None, None, None),
    )
    out_specs = (P("layer", "dp", None, None, None), P("layer", None, None, None, "dp"))
    return jax.shard_map(
        on_device, mesh=mesh, in_specs=in_specs, out_specs=out_specs, check_vma=False
    )
```

time: 86 us -> 81.1 us (0.943)
  blocking collectives: 26.7 us -> 0 us
  starting transfers between devices: 31.6 us -> 43.4 us
  waiting for transfers between devices: 9.34 us -> 18.4 us
  local copies, waits for them, and re-layouts: 4.99 us -> 1.95 us
  other arithmetic: 0 us -> 1.9 us
  Pallas kernels: 12.2 us -> 14 us
    all_to_all x1 -> x0, blocking collectives: 26.7 us -> none  [on_device(): lax.all_to_all(send.reshape(slabs, 16, 128), 'layer', 0, 0, tiled=True)]
    all_to_all x1 -> x2, waiting for transfers between devices: 6.19 us -> 15.8 us  [spread(): return lax.all_to_all(parts, 'layer', 0, 0, tiled=True)]
    all_to_all x1 -> x2, starting transfers between devices: 5.06 us -> 14.5 us  [spread(): return lax.all_to_all(parts, 'layer', 0, 0, tiled=True)]
    unnamed x18 -> x10, local copies, waits for them, and re-layouts: 4.97 us -> 1.92 us
    ppermute x9 -> x12, starting transfers between devices: 26.6 us -> 28.9 us  [the longest x3 15.4 us: swapped(): return lax.ppermute(part, 'layer', [(i ^ 1, i) for i in range(slabs)])]
    pallas_call x8 -> x10, Pallas kernels: 12.2 us -> 14 us  [call(): pl.pallas_call(body, out_shape=placed[0] if single else placed, in_specs=...]
    convert_element_type x0 -> x1, other arithmetic: none -> 0.97 us  [on_device(): rough = points.astype(BF)]
    select_n x0 -> x2, other arithmetic: none -> 0.93 us  [right_of(): return jnp.where(slab == slabs - 1, jnp.zeros_like(part), part)]
  transfers between devices with their start and end apart: 10 -> 14, of which waited for: 6 -> 6; matrix products, arithmetic and copies ran while one was open for 0% -> 1% of each run, Pallas kernels for 5% -> 9%
where the time goes in v3:
time: 81.1 us; the launch traced here: 80.7 us
  starting transfers between devices  43.4 us (54%)
  waiting for transfers between devices  18.4 us (23%)
  Pallas kernels  14 us (17%)
  local copies, waits for them, and re-layouts  1.95 us (2%)
  other arithmetic  1.9 us (2%)
  between operations  1.02 us (1%)
    all_to_all x2, waiting for transfers between devices, spread(): return lax.all_to_all(parts, 'layer', 0, 0, tiled=True)  15.8 us
    ppermute x3, starting transfers between devices, swapped(): return lax.ppermute(part, 'layer', [(i ^ 1, i) for i in range(slabs)])  15.4 us
    all_to_all x2, starting transfers between devices, spread(): return lax.all_to_all(parts, 'layer', 0, 0, tiled=True)  14.5 us
    pallas_call x10, Pallas kernels, call(): pl.pallas_call(body, out_shape=placed[0] if single else placed, in_specs=...  14 us
    ppermute x3, starting transfers between devices, on_device(): lax.ppermute(own_states, 'dp', [(i, (i + k) % images) for i in range(imag...  5.06 us
    ppermute x3, starting transfers between devices, on_device(): lax.ppermute(part, 'dp', [(i, (i + k) % images) for i in range(images)])  5.06 us
    ppermute x3, starting transfers between devices, crossed(): return lax.ppermute(part, 'layer', route)  3.36 us
    unnamed x10, local copies, waits for them, and re-layouts  1.92 us
  transfers between devices with their start and end apart: 14, of which 6 were waited for; matrix products, arithmetic and copies ran while one was open for 1% of the time, Pallas kernels for 9%

profile of v3, /device:TPU:1, one launch (start us, length us, event | category | flops | bytes accessed | tf_op | source)
XLA Modules:
  0.0 80.7 jit_solution(16860354370203572877)
XLA Ops:
  0.6 1.0 %bitcast_convert_fusion = bf16[256,256]{1,0:T(8,128)(2,1)S(1)} fusion(f32[1,1,16,16,256]{4,3,2,1,0:T(8,128)} %param.7), kind=kLoop, calls=%fused_computation.6 | loop fusion | flops 65536 | bytes 393216 | tf_op jit(solution)/shard_map/convert_element_type | solution.py:298
  1.6 3.3 %collective-permute-start.1 = (bf16[256,256]{1,0:T(8,128)(2,1)S(1)}, bf16[256,256]{1,0:T(8,128)(2,1)S(1)}, u32[]{:S(2)}, u32[]{:S(2)}) collective-permute-start(bf16[256,256]{1,0:T(8,128)(2,1)S(1)} %bitcast_convert_fusion), channel_id=1, source_target_pairs={{4,0},{0,4},{12,8},{8,12},{20,16},{16,20},{28,24},{24,28},{36,32},... | collective-permute-start | bytes 393224 | tf_op jit(solution)/shard_map/ppermute | solution.py:280
  4.9 0.0 collective-permute-start
  4.9 3.0 %slopes.1 = (f32[2,256,256]{2,1,0:T(8,128)S(1)}, bf16[2,2304,256]{2,1,0:T(8,128)(2,1)S(1)}, f32[256,256]{1,0:T(8,128)S(1)}) custom-call(bf16[2,1,16,16,256]{4,3,2,1,0:T(8,128)(2,1)} %states_far.1, bf16[2,3,3,256,256]{4,3,2,1,0:T(8,128)(2,1)} %kernels_far.1, f32[256,256]{1,0:T(8,128)} %bitcast.28), custom_call_target="tpu_custom_call" | custom-call | flops 603979776 | bytes 2000000 | tf_op jit(solution)/shard_map/slopes/pallas_call | solution.py:31
  7.9 0.0 collective-permute-done.1.swapped_ref
  7.9 3.3 %collective-permute-start.3 = (bf16[256,256]{1,0:T(8,128)(2,1)S(1)}, bf16[256,256]{1,0:T(8,128)(2,1)}, u32[]{:S(2)}, u32[]{:S(2)}) collective-permute-start(bf16[256,256]{1,0:T(8,128)(2,1)S(1)} %get-tuple-element.26), channel_id=1, source_target_pairs={{252,0},{8,4},{4,8},{16,12},{12,16},{24,20},{20,24},{32,28},{28,32... | collective-permute-start | bytes 393224 | tf_op jit(solution)/shard_map/ppermute | solution.py:284
  11.2 0.0 collective-permute-done.crossed_ref
  11.2 1.5 %odd.1 = (f32[256,256]{1,0:T(8,128)S(1)}, bf16[256,256]{1,0:T(8,128)(2,1)S(1)}) custom-call(bf16[256,256]{1,0:T(8,128)(2,1)S(1)} %collective-permute-done.crossed_ref, f32[256,256]{1,0:T(8,128)} %bitcast.24, f32[2,256,256]{2,1,0:T(8,128)S(1)} %get-tuple-element.21.slope_ref, ...), custom_call_target="tpu_custom_call", output_to_operand_aliasing={{0}: (4, {})} | custom-call | flops 603979776 | bytes 2000000 | tf_op jit(solution)/shard_map/odd/pallas_call | solution.py:31
  12.7 3.4 %collective-permute-start.2 = (bf16[256,256]{1,0:T(8,128)(2,1)S(1)}, bf16[256,256]{1,0:T(8,128)(2,1)S(1)}, u32[]{:S(2)}, u32[]{:S(2)}) collective-permute-start(bf16[256,256]{1,0:T(8,128)(2,1)S(1)} %get-tuple-element.25), channel_id=1, source_target_pairs={{4,0},{0,4},{12,8},{8,12},{20,16},{16,20},{28,24},{24,28},{36,32},... | collective-permute-start | bytes 393224 | tf_op jit(solution)/shard_map/ppermute | solution.py:280
  16.1 0.0 collective-permute-done.3
  16.1 0.9 %broadcast_select_fusion.1.crossed_ref = bf16[256,256]{1,0:T(8,128)(2,1)S(1)} fusion(bf16[256,256]{1,0:T(8,128)(2,1)} %collective-permute-done.3, pred[]{:T(512)S(6)} %eq.8), kind=kLoop, calls=%fused_computation.1 | loop fusion | flops 65536 | bytes 262145 | tf_op jit(solution)/shard_map/jit(_where)/select_n | solution.py:293
  17.0 0.1 collective-permute-done.2.swapped_ref
  17.1 1.5 %sweep.1 = (f32[256,256]{1,0:T(8,128)S(1)}, bf16[256,256]{1,0:T(8,128)(2,1)S(1)}) custom-call(bf16[256,256]{1,0:T(8,128)(2,1)S(1)} %collective-permute-done.2.swapped_ref, bf16[256,256]{1,0:T(8,128)(2,1)S(1)} %broadcast_select_fusion.1.crossed_ref, f32[256,256]{1,0:T(8,128)} %bitcast.25, ...), custom_call_target="tpu_custom_call", output_to_operand_aliasing={{0}: (5, {})} | custom-call | flops 603979776 | bytes 2000000 | tf_op jit(solution)/shard_map/sweep/pallas_call | solution.py:31
  18.5 0.1 collective-permute-start.5
  18.6 8.7 %collective-permute-start.4 = (bf16[256,256]{1,0:T(8,128)(2,1)S(1)}, bf16[256,256]{1,0:T(8,128)(2,1)S(1)}, u32[]{:S(2)}, u32[]{:S(2)}) collective-permute-start(bf16[256,256]{1,0:T(8,128)(2,1)S(1)} %get-tuple-element.28), channel_id=1, source_target_pairs={{4,0},{0,4},{12,8},{8,12},{20,16},{16,20},{28,24},{24,28},{36,32},... | collective-permute-start | bytes 393224 | tf_op jit(solution)/shard_map/ppermute | solution.py:280
  27.3 0.0 collective-permute-done.5
  27.3 1.0 %collective-permute-done.4.swapped_ref = bf16[256,256]{1,0:T(8,128)(2,1)S(1)} collective-permute-done((bf16[256,256]{1,0:T(8,128)(2,1)S(1)}, bf16[256,256]{1,0:T(8,128)(2,1)S(1)}, u32[]{:S(2)}, u32[]{:S(2)}) %collective-permute-start.4) | collective-permute-done | bytes 131104 | tf_op jit(solution)/shard_map/ppermute | solution.py:280
  28.3 2.3 %residual.1 = (f32[256,256]{1,0:T(8,128)}, bf16[32,2,16,128]{3,2,1,0:T(8,128)(2,1)}, f32[256,256]{1,0:T(8,128)S(1)}) custom-call(bf16[256,256]{1,0:T(8,128)(2,1)S(1)} %collective-permute-done.4.swapped_ref, bf16[256,256]{1,0:T(8,128)(2,1)S(1)} %broadcast_select_fusion.crossed_ref, f32[256,256]{1,0:T(8,128)} %bitcast.26, ...), custom_call_target="tpu_custom_call", output_to_operand_aliasing={{2}: (5, {})} | custom-call | flops 603979776 | bytes 2000000 | tf_op jit(solution)/shard_map/residual/pallas_call | solution.py:31
  30.7 9.8 %all-to-all-start = ((bf16[64,16,128]{2,1,0:T(8,128)(2,1)}), bf16[64,16,128]{2,1,0:T(8,128)(2,1)S(1)}, u32[]{:S(2)}, u32[]{:S(2)}) async-start(bf16[64,16,128]{2,1,0:T(8,128)(2,1)} %bitcast.30), calls=%async_computation | async-start | bytes 524288 | tf_op jit(solution)/shard_map/all_to_all | solution.py:374
  40.4 1.4 %collective-permute-start.6 = (bf16[2,256,256]{2,1,0:T(8,128)(2,1)}, bf16[2,256,256]{2,1,0:T(8,128)(2,1)}, u32[]{:S(2)}, u32[]{:S(2)}) collective-permute-start(bf16[2,256,256]{2,1,0:T(8,128)(2,1)} %bitcast.18), channel_id=1, source_target_pairs={{0,1},{1,2},{2,3},{3,0},{4,5},{5,6},{6,7},{7,4},{8,9},{9,10},{10,1... | collective-permute-start | bytes 786440 | tf_op jit(solution)/shard_map/ppermute | solution.py:389
  41.8 2.6 %collective-permute-start.7 = (bf16[2,256,256]{2,1,0:T(8,128)(2,1)}, bf16[2,256,256]{2,1,0:T(8,128)(2,1)}, u32[]{:S(2)}, u32[]{:S(2)}) collective-permute-start(bf16[2,256,256]{2,1,0:T(8,128)(2,1)} %bitcast.19), channel_id=1, source_target_pairs={{0,2},{1,3},{2,0},{3,1},{4,6},{5,7},{6,4},{7,5},{8,10},{9,11},{10,... | collective-permute-start | bytes 786440 | tf_op jit(solution)/shard_map/ppermute | solution.py:389
  44.4 1.1 %collective-permute-start.8 = (bf16[2,256,256]{2,1,0:T(8,128)(2,1)}, bf16[2,256,256]{2,1,0:T(8,128)(2,1)}, u32[]{:S(2)}, u32[]{:S(2)}) collective-permute-start(bf16[2,256,256]{2,1,0:T(8,128)(2,1)} %bitcast.20), channel_id=1, source_target_pairs={{0,3},{1,0},{2,1},{3,2},{4,7},{5,4},{6,5},{7,6},{8,11},{9,8},{10,9... | collective-permute-start | bytes 786440 | tf_op jit(solution)/shard_map/ppermute | solution.py:389
  45.5 8.2 %all-to-all-done.given_ref = bf16[64,16,128]{2,1,0:T(8,128)(2,1)S(1)} async-done(((bf16[64,16,128]{2,1,0:T(8,128)(2,1)}), bf16[64,16,128]{2,1,0:T(8,128)(2,1)S(1)}, u32[]{:S(2)}, u32[]{:S(2)}) %all-to-all-start) | async-done | bytes 262176 | tf_op jit(solution)/shard_map/all_to_all | solution.py:374
  53.7 0.8 %scan.1 = bf16[64,8,128]{2,1,0:T(8,128)(2,1)} custom-call(bf16[64,16,128]{2,1,0:T(8,128)(2,1)S(1)} %all-to-all-done.given_ref), custom_call_target="tpu_custom_call" | custom-call | tf_op jit(solution)/shard_map/scan/pallas_call | solution.py:31
  54.5 4.7 %all-to-all-start.1 = ((bf16[64,8,128]{2,1,0:T(8,128)(2,1)}), bf16[64,8,128]{2,1,0:T(8,128)(2,1)S(1)}, u32[]{:S(2)}, u32[]{:S(2)}) async-start(bf16[64,8,128]{2,1,0:T(8,128)(2,1)} %scan.1), calls=%async_computation.1 | async-start | bytes 262144 | tf_op jit(solution)/shard_map/all_to_all | solution.py:374
  59.3 0.0 collective-permute-done.6.refs_1_
  59.3 0.0 collective-permute-done.7.refs_2_
  59.4 0.0 collective-permute-done.8.refs_3_
  59.4 0.0 copy-start.2
  59.4 0.9 %copy-done.2 = bf16[2,1,16,16,256]{4,3,2,1,0:T(8,128)(2,1)S(1)} copy-done((bf16[2,1,16,16,256]{4,3,2,1,0:T(8,128)(2,1)S(1)}, bf16[2,1,16,16,256]{4,3,2,1,0:T(8,128)(2,1)}, u32[]{:S(2)}) %copy-start.2) | copy-done | bytes 262168
  60.3 1.4 %turn.1.refs_0_ = bf16[2,256,1024]{2,1,0:T(8,128)(2,1)S(1)} custom-call(bf16[2,256,256]{2,1,0:T(8,128)(2,1)S(1)} %bitcast.21, bf16[2,256,256]{2,1,0:T(8,128)(2,1)} %collective-permute-done.6.refs_1_, bf16[2,256,256]{2,1,0:T(8,128)(2,1)} %collective-permute-done.7.refs_2_, bf16[2,256,256]{2,1,0:T(8,128)(2,1)} %collective-permute-done.8.refs_3_), custom_call_target="tpu_custom_call" | custom-call | bytes 2000000 | tf_op jit(solution)/shard_map/turn/pallas_call | solution.py:31
  61.8 0.0 copy-start
  61.8 1.0 %copy-done = bf16[2,256,1024]{2,1,0:T(8,128)(2,1)} copy-done((bf16[2,256,1024]{2,1,0:T(8,128)(2,1)}, bf16[2,256,1024]{2,1,0:T(8,128)(2,1)S(1)}, u32[]{:S(2)}) %copy-start) | copy-done | bytes 1048600
  62.7 0.0 copy-start.3
  62.7 7.7 %all-to-all-done.1.error_ref = bf16[64,8,128]{2,1,0:T(8,128)(2,1)S(1)} async-done(((bf16[64,8,128]{2,1,0:T(8,128)(2,1)}), bf16[64,8,128]{2,1,0:T(8,128)(2,1)S(1)}, u32[]{:S(2)}, u32[]{:S(2)}) %all-to-all-start.1) | async-done | bytes 131104 | tf_op jit(solution)/shard_map/all_to_all | solution.py:374
  70.4 0.0 copy-start.4
  70.4 0.0 copy-start.1
  70.4 0.6 final.1
  71.0 1.4 %collective-permute-start.9 = (bf16[2,128,128]{2,1,0:T(8,128)(2,1)S(1)}, bf16[2,128,128]{2,1,0:T(8,128)(2,1)S(1)}, u32[]{:S(2)}, u32[]{:S(2)}) collective-permute-start(bf16[2,128,128]{2,1,0:T(8,128)(2,1)S(1)} %get-tuple-element.44), channel_id=1, source_target_pairs={{0,1},{1,2},{2,3},{3,0},{4,5},{5,6},{6,7},{7,4},{8,9},{9,10},{10,1... | collective-permute-start | bytes 196616 | tf_op jit(solution)/shard_map/ppermute | solution.py:407
  72.4 2.6 %collective-permute-start.10 = (bf16[2,128,128]{2,1,0:T(8,128)(2,1)S(1)}, bf16[2,128,128]{2,1,0:T(8,128)(2,1)S(1)}, u32[]{:S(2)}, u32[]{:S(2)}) collective-permute-start(bf16[2,128,128]{2,1,0:T(8,128)(2,1)S(1)} %get-tuple-element.43), channel_id=1, source_target_pairs={{0,2},{1,3},{2,0},{3,1},{4,6},{5,7},{6,4},{7,5},{8,10},{9,11},{10,... | collective-permute-start | bytes 196616 | tf_op jit(solution)/shard_map/ppermute | solution.py:407
  75.0 1.1 %collective-permute-start.11 = (bf16[2,128,128]{2,1,0:T(8,128)(2,1)S(1)}, bf16[2,128,128]{2,1,0:T(8,128)(2,1)S(1)}, u32[]{:S(2)}, u32[]{:S(2)}) collective-permute-start(bf16[2,128,128]{2,1,0:T(8,128)(2,1)S(1)} %get-tuple-element.42), channel_id=1, source_target_pairs={{0,3},{1,0},{2,1},{3,2},{4,7},{5,4},{6,5},{7,6},{8,11},{9,8},{10,9... | collective-permute-start | bytes 196616 | tf_op jit(solution)/shard_map/ppermute | solution.py:407
  76.1 0.0 copy-done.3
  76.1 0.0 copy-done.4
  76.1 0.8 corrected.1
  76.9 0.0 collective-permute-done.9.refs_2_
  76.9 1.0 %collective-permute-done.10.refs_3_ = bf16[2,128,128]{2,1,0:T(8,128)(2,1)S(1)} collective-permute-done((bf16[2,128,128]{2,1,0:T(8,128)(2,1)S(1)}, bf16[2,128,128]{2,1,0:T(8,128)(2,1)S(1)}, u32[]{:S(2)}, u32[]{:S(2)}) %collective-permute-start.10) | collective-permute-done | bytes 65568 | tf_op jit(solution)/shard_map/ppermute | solution.py:407
  77.9 0.5 collective-permute-done.11.refs_4_
  78.4 0.0 copy-done.1
  78.4 2.1 %taps.1 = f32[2,3,3,64,256]{4,3,2,1,0:T(8,128)} custom-call(bf16[2,256,1024]{2,1,0:T(8,128)(2,1)S(1)} %copy-done.1, bf16[2,128,128]{2,1,0:T(8,128)(2,1)S(1)} %get-tuple-element.45.refs_1_, bf16[2,128,128]{2,1,0:T(8,128)(2,1)S(1)} %collective-permute-done.9.refs_2_, bf16[2,128,128]{2,1,0:T(8,128)(2,1)S(1)} %collective-permute-done.10.refs_3_, ...), custom_call_target="tpu_custom_call" | custom-call | flops 603979776 | bytes 2000000 | tf_op jit(solution)/shard_map/taps/pallas_call | solution.py:31
  (3 shorter events, 0.1 us)
Async XLA Ops:
  1.6 6.3 %collective-permute-start.1 = (bf16[256,256]{1,0:T(8,128)(2,1)S(1)}, bf16[256,256]{1,0:T(8,128)(2,1)S(1)}, u32[]{:S(2)}, u32[]{:S(2)}) collective-permute-start(bf16[256,256]{1,0:T(8,128)(2,1)S(1)} %bitcast_convert_fusion), channel_id=1, source_target_pairs={{4,0},{0,4},{12,8},{8,12},{20,16},{16,20},{28,24},{24,28},{36,32},... | collective-permute-start | bytes 393224 | tf_op jit(solution)/shard_map/ppermute | solution.py:280
  4.9 6.3 %collective-permute-start = (bf16[256,256]{1,0:T(8,128)(2,1)S(1)}, bf16[256,256]{1,0:T(8,128)(2,1)S(1)}, u32[]{:S(2)}, u32[]{:S(2)}) collective-permute-start(bf16[256,256]{1,0:T(8,128)(2,1)S(1)} %bitcast_convert_fusion), channel_id=1, source_target_pairs={{252,0},{8,4},{4,8},{16,12},{12,16},{24,20},{20,24},{32,28},{28,32... | collective-permute-start | bytes 393224 | tf_op jit(solution)/shard_map/ppermute | solution.py:284
  7.9 8.1 %collective-permute-start.3 = (bf16[256,256]{1,0:T(8,128)(2,1)S(1)}, bf16[256,256]{1,0:T(8,128)(2,1)}, u32[]{:S(2)}, u32[]{:S(2)}) collective-permute-start(bf16[256,256]{1,0:T(8,128)(2,1)S(1)} %get-tuple-element.26), channel_id=1, source_target_pairs={{252,0},{8,4},{4,8},{16,12},{12,16},{24,20},{20,24},{32,28},{28,32... | collective-permute-start | bytes 393224 | tf_op jit(solution)/shard_map/ppermute | solution.py:284
  12.7 4.4 %collective-permute-start.2 = (bf16[256,256]{1,0:T(8,128)(2,1)S(1)}, bf16[256,256]{1,0:T(8,128)(2,1)S(1)}, u32[]{:S(2)}, u32[]{:S(2)}) collective-permute-start(bf16[256,256]{1,0:T(8,128)(2,1)S(1)} %get-tuple-element.25), channel_id=1, source_target_pairs={{4,0},{0,4},{12,8},{8,12},{20,16},{16,20},{28,24},{24,28},{36,32},... | collective-permute-start | bytes 393224 | tf_op jit(solution)/shard_map/ppermute | solution.py:280
  18.5 8.8 %collective-permute-start.5 = (bf16[256,256]{1,0:T(8,128)(2,1)S(1)}, bf16[256,256]{1,0:T(8,128)(2,1)S(1)}, u32[]{:S(2)}, u32[]{:S(2)}) collective-permute-start(bf16[256,256]{1,0:T(8,128)(2,1)S(1)} %get-tuple-element.28), channel_id=1, source_target_pairs={{252,0},{8,4},{4,8},{16,12},{12,16},{24,20},{20,24},{32,28},{28,32... | collective-permute-start | bytes 393224 | tf_op jit(solution)/shard_map/ppermute | solution.py:284
  18.6 9.7 %collective-permute-start.4 = (bf16[256,256]{1,0:T(8,128)(2,1)S(1)}, bf16[256,256]{1,0:T(8,128)(2,1)S(1)}, u32[]{:S(2)}, u32[]{:S(2)}) collective-permute-start(bf16[256,256]{1,0:T(8,128)(2,1)S(1)} %get-tuple-element.28), channel_id=1, source_target_pairs={{4,0},{0,4},{12,8},{8,12},{20,16},{16,20},{28,24},{24,28},{36,32},... | collective-permute-start | bytes 393224 | tf_op jit(solution)/shard_map/ppermute | solution.py:280
  30.7 23.0 %all-to-all-start = ((bf16[64,16,128]{2,1,0:T(8,128)(2,1)}), bf16[64,16,128]{2,1,0:T(8,128)(2,1)S(1)}, u32[]{:S(2)}, u32[]{:S(2)}) async-start(bf16[64,16,128]{2,1,0:T(8,128)(2,1)} %bitcast.30), calls=%async_computation | async-start | bytes 524288 | tf_op jit(solution)/shard_map/all_to_all | solution.py:374
  40.4 18.9 %collective-permute-start.6 = (bf16[2,256,256]{2,1,0:T(8,128)(2,1)}, bf16[2,256,256]{2,1,0:T(8,128)(2,1)}, u32[]{:S(2)}, u32[]{:S(2)}) collective-permute-start(bf16[2,256,256]{2,1,0:T(8,128)(2,1)} %bitcast.18), channel_id=1, source_target_pairs={{0,1},{1,2},{2,3},{3,0},{4,5},{5,6},{6,7},{7,4},{8,9},{9,10},{10,1... | collective-permute-start | bytes 786440 | tf_op jit(solution)/shard_map/ppermute | solution.py:389
  41.8 17.5 %collective-permute-start.7 = (bf16[2,256,256]{2,1,0:T(8,128)(2,1)}, bf16[2,256,256]{2,1,0:T(8,128)(2,1)}, u32[]{:S(2)}, u32[]{:S(2)}) collective-permute-start(bf16[2,256,256]{2,1,0:T(8,128)(2,1)} %bitcast.19), channel_id=1, source_target_pairs={{0,2},{1,3},{2,0},{3,1},{4,6},{5,7},{6,4},{7,5},{8,10},{9,11},{10,... | collective-permute-start | bytes 786440 | tf_op jit(solution)/shard_map/ppermute | solution.py:389
  44.4 14.9 %collective-permute-start.8 = (bf16[2,256,256]{2,1,0:T(8,128)(2,1)}, bf16[2,256,256]{2,1,0:T(8,128)(2,1)}, u32[]{:S(2)}, u32[]{:S(2)}) collective-permute-start(bf16[2,256,256]{2,1,0:T(8,128)(2,1)} %bitcast.20), channel_id=1, source_target_pairs={{0,3},{1,0},{2,1},{3,2},{4,7},{5,4},{6,5},{7,6},{8,11},{9,8},{10,9... | collective-permute-start | bytes 786440 | tf_op jit(solution)/shard_map/ppermute | solution.py:389
  54.5 15.9 %all-to-all-start.1 = ((bf16[64,8,128]{2,1,0:T(8,128)(2,1)}), bf16[64,8,128]{2,1,0:T(8,128)(2,1)S(1)}, u32[]{:S(2)}, u32[]{:S(2)}) async-start(bf16[64,8,128]{2,1,0:T(8,128)(2,1)} %scan.1), calls=%async_computation.1 | async-start | bytes 262144 | tf_op jit(solution)/shard_map/all_to_all | solution.py:374
  59.4 1.0 %copy-start.2 = (bf16[2,1,16,16,256]{4,3,2,1,0:T(8,128)(2,1)S(1)}, bf16[2,1,16,16,256]{4,3,2,1,0:T(8,128)(2,1)}, u32[]{:S(2)}) copy-start(bf16[2,1,16,16,256]{4,3,2,1,0:T(8,128)(2,1)} %states_far.1) | copy-start | bytes 786436
  61.8 1.0 %copy-start = (bf16[2,256,1024]{2,1,0:T(8,128)(2,1)}, bf16[2,256,1024]{2,1,0:T(8,128)(2,1)S(1)}, u32[]{:S(2)}) copy-start(bf16[2,256,1024]{2,1,0:T(8,128)(2,1)S(1)} %turn.1.refs_0_) | copy-start | bytes 3145732
  62.7 13.4 %copy-start.3 = (f32[1,16,16,256]{3,2,1,0:T(8,128)S(1)}, f32[1,16,16,256]{3,2,1,0:T(8,128)}, u32[]{:S(2)}) copy-start(f32[1,16,16,256]{3,2,1,0:T(8,128)} %param.8) | copy-start | bytes 786436
  70.4 5.7 %copy-start.4 = (f32[256,256]{1,0:T(8,128)S(1)}, f32[256,256]{1,0:T(8,128)}, u32[]{:S(2)}) copy-start(f32[256,256]{1,0:T(8,128)} %get-tuple-element.36.relax_ref) | copy-start | bytes 786436
  70.4 8.0 %copy-start.1 = (bf16[2,256,1024]{2,1,0:T(8,128)(2,1)S(1)}, bf16[2,256,1024]{2,1,0:T(8,128)(2,1)}, u32[]{:S(2)}) copy-start(bf16[2,256,1024]{2,1,0:T(8,128)(2,1)} %copy-done) | copy-start | bytes 3145732
  71.0 5.9 %collective-permute-start.9 = (bf16[2,128,128]{2,1,0:T(8,128)(2,1)S(1)}, bf16[2,128,128]{2,1,0:T(8,128)(2,1)S(1)}, u32[]{:S(2)}, u32[]{:S(2)}) collective-permute-start(bf16[2,128,128]{2,1,0:T(8,128)(2,1)S(1)} %get-tuple-element.44), channel_id=1, source_target_pairs={{0,1},{1,2},{2,3},{3,0},{4,5},{5,6},{6,7},{7,4},{8,9},{9,10},{10,1... | collective-permute-start | bytes 196616 | tf_op jit(solution)/shard_map/ppermute | solution.py:407
  72.4 5.5 %collective-permute-start.10 = (bf16[2,128,128]{2,1,0:T(8,128)(2,1)S(1)}, bf16[2,128,128]{2,1,0:T(8,128)(2,1)S(1)}, u32[]{:S(2)}, u32[]{:S(2)}) collective-permute-start(bf16[2,128,128]{2,1,0:T(8,128)(2,1)S(1)} %get-tuple-element.43), channel_id=1, source_target_pairs={{0,2},{1,3},{2,0},{3,1},{4,6},{5,7},{6,4},{7,5},{8,10},{9,11},{10,... | collective-permute-start | bytes 196616 | tf_op jit(solution)/shard_map/ppermute | solution.py:407
  75.0 3.4 %collective-permute-start.11 = (bf16[2,128,128]{2,1,0:T(8,128)(2,1)S(1)}, bf16[2,128,128]{2,1,0:T(8,128)(2,1)S(1)}, u32[]{:S(2)}, u32[]{:S(2)}) collective-permute-start(bf16[2,128,128]{2,1,0:T(8,128)(2,1)S(1)} %get-tuple-element.42), channel_id=1, source_target_pairs={{0,3},{1,0},{2,1},{3,2},{4,7},{5,4},{6,5},{7,6},{8,11},{9,8},{10,9... | collective-permute-start | bytes 196616 | tf_op jit(solution)/shard_map/ppermute | solution.py:407

commit v4 on v3

--- a/solution.py
+++ b/solution.py
@@ -45,8 +45,12 @@
     return lax.axis_index("layer") % 2 == 0
 
 
-def is_last():
-    return lax.axis_index("layer") == lax.axis_size("layer") - 1
+def stage(body):
+    pl.when(lax.axis_index("layer") >= 0)(body)
+
+
+def is_first():
+    return lax.axis_index("layer") == 0
 
 
 def columns(value, width):
@@ -92,47 +96,65 @@
     return right
 
 
+def round_body(width, points_far, terminal_far, out_ref, held_ref, sem):
+    edge = pltpu.make_async_copy(terminal_far, held_ref, sem)
+    plain = pltpu.make_async_copy(points_far, held_ref, sem)
+    pl.when(is_first())(edge.start)
+    pl.when(jnp.logical_not(is_first()))(plain.start)
+    plain.wait()
+    out_ref[...] = held_ref[...].astype(BF)
+
+
 def slope_body(width, states_far, kernels_far, points_far, slope_ref, turned_ref, points_ref, states_ref, kernels_ref, sems):
     blocks, height, _, channels = states_ref.shape
-    held = [pltpu.make_async_copy(states_far.at[:, 0], states_ref, sems.at[blocks])]
+    held = [pltpu.make_async_copy(states_far.at[:, 0], states_ref, sems.at[3 * blocks])]
     for block in range(blocks):
-        held.append(pltpu.make_async_copy(kernels_far.at[block], kernels_ref.at[block], sems.at[block]))
-    held.append(pltpu.make_async_copy(points_far, points_ref, sems.at[blocks + 1]))
+        for i in range(3):
+            sem = sems.at[3 * block + i]
+            held.append(pltpu.make_async_copy(kernels_far.at[block, i], kernels_ref.at[block, i], sem))
+    held.append(pltpu.make_async_copy(points_far, points_ref, sems.at[3 * blocks + 1]))
     for copy in held:
         copy.start()
     held[0].wait()
-    for block in range(blocks):
+
+
+    def one(block):
+        for i in range(3):
+            held[1 + 3 * block + i].wait()
         value = states_ref[block].reshape(height * width, channels).astype(F32)
         patches = jnp.concatenate(forward_patches(value, width), 1)
-        held[1 + block].wait()
         taps = kernels_ref[block].reshape(9 * channels, channels)
         act = jnp.tanh(jnp.dot(patches, taps, preferred_element_type=F32))
-        slope_ref[block] = 1.0 - act * act
+        slope_ref[block] = (1.0 - act * act).astype(BF)
         for i in range(3):
             for j in range(3):
                 at = (i * 3 + j) * channels
                 turned_ref[block, at : at + channels, :] = kernels_ref[block, i, j].T
+
+    for block in range(blocks):
+        stage(functools.partial(one, block))
     held[-1].wait()
 
 
-def fetch(far_ref, near_ref, sem):
-    copy = pltpu.make_async_copy(far_ref, near_ref, sem)
-    copy.start()
-    copy.wait()
-
-
-def enter(right_ref, swapped_ref, crossed_ref, terminal_far, sem):
-    @pl.when(is_even())
-    def _():
-        right_ref[...] = swapped_ref[...].astype(F32)
-
-    @pl.when(jnp.logical_not(jnp.logical_or(is_even(), is_last())))
-    def _():
-        right_ref[...] = crossed_ref[...].astype(F32)
-
-    @pl.when(is_last())
-    def _():
-        fetch(terminal_far, right_ref, sem)
+def entering(swapped_ref, shifted_ref):
+    return jnp.where(is_even(), swapped_ref[...], shifted_ref[...]).astype(F32)
+
+
+class Edge:
+    def __init__(self, terminal_far, edge_ref, sem):
+        self.copy = pltpu.make_async_copy(terminal_far, edge_ref, sem)
+        self.edge_ref = edge_ref
+        pl.when(is_first())(self.copy.start)
+
+    def write(self, points_ref, send_ref):
+        @pl.when(is_first())
+        def _():
+            self.copy.wait()
+            send_ref[...] = self.edge_ref[...].astype(BF)
+
+        @pl.when(jnp.logical_not(is_first()))
+        def _():
+            send_ref[...] = points_ref[...].astype(BF)
 
 
 def sweep(right, slope_ref, turned_ref, points_ref, width):
@@ -140,56 +162,53 @@
     points_ref[...] = points + DAMPING * (relaxed(right, slope_ref, turned_ref, width) - points)
 
 
-def even_body(width, swapped_ref, slope_ref, turned_ref, _, points_ref, send_ref):
+def even_body(width, swapped_ref, terminal_far, slope_ref, turned_ref, _, points_ref, send_ref, edge_ref, sem):
+    edge = Edge(terminal_far, edge_ref, sem)
+
     @pl.when(is_even())
     def _():
         sweep(swapped_ref[...].astype(F32), slope_ref, turned_ref, points_ref, width)
 
-    send_ref[...] = points_ref[...].astype(BF)
-
-
-def odd_body(width, crossed_ref, terminal_far, slope_ref, turned_ref, _, points_ref, send_ref, right_ref, sem):
-    @pl.when(is_last())
-    def _():
-        fetch(terminal_far, right_ref, sem)
-
-    @pl.when(jnp.logical_not(jnp.logical_or(is_even(), is_last())))
-    def _():
-        right_ref[...] = crossed_ref[...].astype(F32)
-
+    edge.write(points_ref, send_ref)
+
+
+def odd_body(width, shifted_ref, slope_ref, turned_ref, _, points_ref, send_ref):
     @pl.when(jnp.logical_not(is_even()))
     def _():
-        sweep(right_ref[...], slope_ref, turned_ref, points_ref, width)
+        sweep(shifted_ref[...].astype(F32), slope_ref, turned_ref, points_ref, width)
 
     send_ref[...] = points_ref[...].astype(BF)
 
 
-def sweep_body(width, swapped_ref, crossed_ref, terminal_far, slope_ref, turned_ref, _, points_ref, send_ref, right_ref, sem):
-    enter(right_ref, swapped_ref, crossed_ref, terminal_far, sem)
-    sweep(right_ref[...], slope_ref, turned_ref, points_ref, width)
-    send_ref[...] = points_ref[...].astype(BF)
-
-
-def residual_body(width, swapped_ref, crossed_ref, terminal_far, slope_ref, turned_ref, _, gain_far, relax_far, send_far, points_ref, right_ref, gain_ref, relax_ref, send_ref, sem, sems):
+def sweep_body(width, swapped_ref, shifted_ref, terminal_far, slope_ref, turned_ref, _, points_ref, send_ref, edge_ref, sem):
+    edge = Edge(terminal_far, edge_ref, sem)
+    sweep(entering(swapped_ref, shifted_ref), slope_ref, turned_ref, points_ref, width)
+    edge.write(points_ref, send_ref)
+
+
+def residual_body(width, shifted_ref, slope_ref, turned_ref, _, gain_far, relax_far, send_far, points_ref, gain_ref, relax_ref, send_ref, sems):
     gain_copy = pltpu.make_async_copy(gain_far, gain_ref, sems.at[0])
     gain_copy.start()
-    enter(right_ref, swapped_ref, crossed_ref, terminal_far, sem)
-    right = right_ref[...]
-    relax = relaxed(right, slope_ref, turned_ref, width)
-    residual = (relax - points_ref[...]).reshape(32, 8, 256)
-    gain_copy.wait()
-    decay = (1.0 - gain_ref[...]).reshape(32, 8, 256)
-    for half in range(2):
-        lanes = slice(128 * half, 128 * half + 128)
-        send_ref[:, half] = jnp.concatenate([residual[:, :, lanes], decay[:, :, lanes]], 1).astype(BF)
-    send_copy = pltpu.make_async_copy(send_ref, send_far, sems.at[1])
-    send_copy.start()
-    relax_ref[...] = relax
     relax_copy = pltpu.make_async_copy(relax_ref, relax_far, sems.at[2])
-    relax_copy.start()
-    points_ref[...] = right
-    send_copy.wait()
-    relax_copy.wait()
+
+    @stage
+    def _():
+        relax_ref[...] = relaxed(shifted_ref[...].astype(F32), slope_ref, turned_ref, width)
+
+    @stage
+    def _():
+        gain_copy.wait()
+        residual = (relax_ref[...] - points_ref[...]).reshape(32, 8, 256)
+        decay = (1.0 - gain_ref[...]).reshape(32, 8, 256)
+        for half in range(2):
+            lanes = slice(128 * half, 128 * half + 128)
+            send_ref[:, half] = jnp.concatenate([residual[:, :, lanes], decay[:, :, lanes]], 1).astype(BF)
+        send_copy = pltpu.make_async_copy(send_ref, send_far, sems.at[1])
+        send_copy.start()
+        relax_copy.start()
+        points_ref[...] = shifted_ref[...].astype(F32)
+        send_copy.wait()
+        relax_copy.wait()
 
 
 def scan_body(given_ref, out_far, out_ref, sem):
@@ -242,10 +261,14 @@
 def taps_body(width, *refs, images):
     states_ref, signal_refs = refs[0], refs[1 : 1 + images]
     out_far, out_ref, sems = refs[1 + images :]
-    copies = []
     low = lax.broadcasted_iota(jnp.int32, (128, 128), 1) < 64
     wide = lax.broadcasted_iota(jnp.int32, (256, 128), 1) < 64
-    for block in range(out_ref.shape[0]):
+    copies = [
+        pltpu.make_async_copy(out_ref.at[block], out_far.at[block], sems.at[block])
+        for block in range(out_ref.shape[0])
+    ]
+
+    def one(block):
         parts = []
         for image in range(images):
             packed = signal_refs[image][block].astype(F32)
@@ -260,8 +283,10 @@
         grads = (STEP * jnp.dot(states_ref[block], moved, preferred_element_type=F32)).T
         for tap in range(9):
             out_ref[block, tap // 3, tap % 3] = grads[64 * tap : 64 * tap + 64]
-        copies.append(pltpu.make_async_copy(out_ref.at[block], out_far.at[block], sems.at[block]))
-        copies[-1].start()
+        copies[block].start()
+
+    for block in range(out_ref.shape[0]):
+        stage(functools.partial(one, block))
     for copy in copies:
         copy.wait()
 
@@ -279,27 +304,24 @@
     def swapped(part):
         return lax.ppermute(part, "layer", [(i ^ 1, i) for i in range(slabs)])
 
-    def crossed(part):
-        route = [((i + 1) % slabs if i % 2 else (i - 1) % slabs, i) for i in range(slabs)]
-        return lax.ppermute(part, "layer", route)
+    def shifted(part):
+        return lax.ppermute(part, "layer", [((i + 1) % slabs, i) for i in range(slabs)])
 
     whole = shape((cells, channels), F32)
     rounded = shape((cells, channels), BF)
 
     def step(body, outs, *ins, name, **more):
         return call(functools.partial(body, width), outs, ins, flops=blocks * conv_flops, name=name, **more)
-
-    def right_of(part):
-        return jnp.where(slab == slabs - 1, jnp.zeros_like(part), part)
 
     points = adjoint_guess.reshape(cells, channels)
     last_value = terminal.reshape(cells, channels)
     gain = coarse_gain.reshape(cells, channels)
-    rough = points.astype(BF)
-    across, beside = crossed(rough), swapped(rough)
+    edge = (pltpu.VMEM((cells, channels), F32), pltpu.SemaphoreType.DMA)
+    rough = step(round_body, rounded, points, last_value, name="round", far_in=(0, 1), scratch=edge)
+    across, beside = shifted(rough), swapped(rough)
     slopes, turned, points = step(
         slope_body,
-        (shape((blocks, cells, channels), F32), shape((blocks, 9 * channels, channels), BF), whole),
+        (shape((blocks, cells, channels), BF), shape((blocks, 9 * channels, channels), BF), whole),
         states,
         kernels,
         points,
@@ -308,32 +330,31 @@
         scratch=(
             pltpu.VMEM((blocks, height, width, channels), BF),
             pltpu.VMEM((blocks, 3, 3, channels, channels), BF),
-            pltpu.SemaphoreType.DMA((blocks + 2,)),
+            pltpu.SemaphoreType.DMA((3 * blocks + 2,)),
         ),
     )
     points, send = step(
-        even_body, (whole, rounded), beside, slopes, turned, points, name="even", alias={3: 0}
-    )
-    next_across = crossed(send)
-    right_scratch = (pltpu.VMEM((cells, channels), F32), pltpu.SemaphoreType.DMA)
-    points, send = step(
-        odd_body,
+        even_body,
         (whole, rounded),
-        across,
+        beside,
         last_value,
         slopes,
         turned,
         points,
-        name="odd",
+        name="even",
         alias={4: 0},
         far_in=(1,),
-        scratch=right_scratch,
-    )
-    beside, across = swapped(send), right_of(next_across)
+        scratch=edge,
+    )
+    next_across = shifted(send)
+    points, send = step(
+        odd_body, (whole, rounded), across, slopes, turned, points, name="odd", alias={3: 0}
+    )
+    across = jnp.where(slab == slabs, jnp.zeros_like(next_across), next_across)
     points, send = step(
         sweep_body,
         (whole, rounded),
-        beside,
+        swapped(send),
         across,
         last_value,
         slopes,
@@ -342,30 +363,26 @@
         name="sweep",
         alias={5: 0},
         far_in=(2,),
-        scratch=right_scratch,
-    )
-    across, beside = right_of(crossed(send)), swapped(send)
+        scratch=edge,
+    )
+    across = shifted(send)
     packed = (32, 2, 16, 128)
     relax, send, points = step(
         residual_body,
         (whole, shape(packed, BF), whole),
-        beside,
         across,
-        last_value,
         slopes,
         turned,
         points,
         gain,
         name="residual",
-        far_in=(2, 6),
+        far_in=(4,),
         far_out=(0, 1),
-        alias={5: 2},
+        alias={3: 2},
         scratch=(
             pltpu.VMEM((cells, channels), F32),
             pltpu.VMEM((cells, channels), F32),
-            pltpu.VMEM((cells, channels), F32),
             pltpu.VMEM(packed, BF),
-            pltpu.SemaphoreType.DMA,
             pltpu.SemaphoreType.DMA((3,)),
         ),
     )

time: 81.1 us -> 77.6 us (0.957)
  starting transfers between devices: 43.4 us -> 36.5 us
  waiting for transfers between devices: 18.4 us -> 22.8 us
  other arithmetic: 1.9 us -> 0.02 us
  Pallas kernels: 14 us -> 15 us
    ppermute x3 -> x2, starting transfers between devices: 15.4 us -> 3.42 us  [swapped(): return lax.ppermute(part, 'layer', [(i ^ 1, i) for i in range(slabs)])]
    ppermute x3, starting transfers between devices: 3.36 us -> 8.18 us  [shifted(): lax.ppermute(part, 'layer', [((i + 1) % slabs, i) for i in range(slabs)])]
    ppermute x3, waiting for transfers between devices: 0.01 us -> 4.25 us  [shifted(): lax.ppermute(part, 'layer', [((i + 1) % slabs, i) for i in range(slabs)])]
    convert_element_type x1 -> x0, other arithmetic: 0.97 us -> none  [on_device(): rough = points.astype(BF)]
    pallas_call x10 -> x11, Pallas kernels: 14 us -> 15 us  [call(): pl.pallas_call(body, out_shape=placed[0] if single else placed, in_specs=...]
    ppermute x3, waiting for transfers between devices: 1.51 us -> 0.57 us  [on_device(): lax.ppermute(part, 'dp', [(i, (i + k) % images) for i in range(images)])]
    select_n x2 -> x1, other arithmetic: 0.93 us -> 0.02 us  [on_device(): across = jnp.where(slab == slabs, jnp.zeros_like(next_across), next_across)]
  transfers between devices with their start and end apart: 14 -> 13, of which waited for: 6 -> 6; matrix products, arithmetic and copies ran while one was open for 1% -> 0% of each run, Pallas kernels for 9% -> 10%
where the time goes in v4:
time: 77.6 us; the launch traced here: 77.3 us
  starting transfers between devices  36.5 us (47%)
  waiting for transfers between devices  22.8 us (29%)
  Pallas kernels  15 us (19%)
  local copies, waits for them, and re-layouts  1.96 us (3%)
  between operations  1.04 us (1%)
    all_to_all x2, waiting for transfers between devices, spread(): return lax.all_to_all(parts, 'layer', 0, 0, tiled=True)  16.7 us
    pallas_call x11, Pallas kernels, call(): pl.pallas_call(body, out_shape=placed[0] if single else placed, in_specs=...  15 us
    all_to_all x2, starting transfers between devices, spread(): return lax.all_to_all(parts, 'layer', 0, 0, tiled=True)  14.7 us
    ppermute x3, starting transfers between devices, shifted(): lax.ppermute(part, 'layer', [((i + 1) % slabs, i) for i in range(slabs)])  8.18 us
    ppermute x3, starting transfers between devices, on_device(): lax.ppermute(part, 'dp', [(i, (i + k) % images) for i in range(images)])  5.07 us
    ppermute x3, starting transfers between devices, on_device(): lax.ppermute(own_states, 'dp', [(i, (i + k) % images) for i in range(imag...  5.06 us
    ppermute x3, waiting for transfers between devices, shifted(): lax.ppermute(part, 'layer', [((i + 1) % slabs, i) for i in range(slabs)])  4.25 us
    ppermute x2, starting transfers between devices, swapped(): return lax.ppermute(part, 'layer', [(i ^ 1, i) for i in range(slabs)])  3.42 us
  transfers between devices with their start and end apart: 13, of which 6 were waited for; matrix products, arithmetic and copies ran while one was open for 0% of the time, Pallas kernels for 10%

profile of v4, /device:TPU:1, one launch (start us, length us, event | category | flops | bytes accessed | tf_op | source)
XLA Modules:
  0.0 77.3 jit_solution(15589835904243310172)
XLA Ops:
  0.6 1.0 %round.1 = bf16[256,256]{1,0:T(8,128)(2,1)S(1)} custom-call(f32[256,256]{1,0:T(8,128)} %bitcast.29, f32[256,256]{1,0:T(8,128)} %bitcast.24), custom_call_target="tpu_custom_call" | custom-call | flops 603979776 | bytes 2000000 | tf_op jit(solution)/shard_map/round/pallas_call | solution.py:31
  1.6 3.3 %collective-permute-start.1 = (bf16[256,256]{1,0:T(8,128)(2,1)S(1)}, bf16[256,256]{1,0:T(8,128)(2,1)S(1)}, u32[]{:S(2)}, u32[]{:S(2)}) collective-permute-start(bf16[256,256]{1,0:T(8,128)(2,1)S(1)} %round.1), channel_id=1, source_target_pairs={{4,0},{0,4},{12,8},{8,12},{20,16},{16,20},{28,24},{24,28},{36,32},... | collective-permute-start | bytes 393224 | tf_op jit(solution)/shard_map/ppermute | solution.py:305
  4.9 0.1 collective-permute-start
  5.0 2.9 %slopes.1 = (bf16[2,256,256]{2,1,0:T(8,128)(2,1)S(1)}, bf16[2,2304,256]{2,1,0:T(8,128)(2,1)S(1)}, f32[256,256]{1,0:T(8,128)S(1)}) custom-call(bf16[2,1,16,16,256]{4,3,2,1,0:T(8,128)(2,1)} %states_far.1, bf16[2,3,3,256,256]{4,3,2,1,0:T(8,128)(2,1)} %kernels_far.1, f32[256,256]{1,0:T(8,128)} %bitcast.30), custom_call_target="tpu_custom_call" | custom-call | flops 603979776 | bytes 2000000 | tf_op jit(solution)/shard_map/slopes/pallas_call | solution.py:31
  8.0 0.0 collective-permute-done.1.swapped_ref
  8.0 7.9 %collective-permute-start.3 = (bf16[256,256]{1,0:T(8,128)(2,1)S(1)}, bf16[256,256]{1,0:T(8,128)(2,1)S(1)}, u32[]{:S(2)}, u32[]{:S(2)}) collective-permute-start(bf16[256,256]{1,0:T(8,128)(2,1)S(1)} %get-tuple-element.26), channel_id=1, source_target_pairs={{4,0},{8,4},{12,8},{16,12},{20,16},{24,20},{28,24},{32,28},{36,32}... | collective-permute-start | bytes 393224 | tf_op jit(solution)/shard_map/ppermute | solution.py:308
  15.9 0.0 collective-permute-done.shifted_ref
  15.9 1.5 %odd.1 = (f32[256,256]{1,0:T(8,128)S(1)}, bf16[256,256]{1,0:T(8,128)(2,1)S(1)}) custom-call(bf16[256,256]{1,0:T(8,128)(2,1)S(1)} %collective-permute-done.shifted_ref, bf16[2,256,256]{2,1,0:T(8,128)(2,1)S(1)} %get-tuple-element.21.slope_ref, bf16[2,2304,256]{2,1,0:T(8,128)(2,1)S(1)} %get-tuple-element.22.turned_ref, ...), custom_call_target="tpu_custom_call", output_to_operand_aliasing={{0}: (3, {})} | custom-call | flops 603979776 | bytes 2000000 | tf_op jit(solution)/shard_map/odd/pallas_call | solution.py:31
  17.4 0.1 collective-permute-start.2
  17.5 0.0 collective-permute-done.3
  17.5 1.3 %collective-permute-done.2.swapped_ref = bf16[256,256]{1,0:T(8,128)(2,1)S(1)} collective-permute-done((bf16[256,256]{1,0:T(8,128)(2,1)S(1)}, bf16[256,256]{1,0:T(8,128)(2,1)S(1)}, u32[]{:S(2)}, u32[]{:S(2)}) %collective-permute-start.2) | collective-permute-done | bytes 131104 | tf_op jit(solution)/shard_map/ppermute | solution.py:305
  18.8 1.5 %sweep.1 = (f32[256,256]{1,0:T(8,128)S(1)}, bf16[256,256]{1,0:T(8,128)(2,1)S(1)}) custom-call(bf16[256,256]{1,0:T(8,128)(2,1)S(1)} %collective-permute-done.2.swapped_ref, bf16[256,256]{1,0:T(8,128)(2,1)S(1)} %broadcast_select_fusion.shifted_ref, f32[256,256]{1,0:T(8,128)} %bitcast.26, ...), custom_call_target="tpu_custom_call", output_to_operand_aliasing={{0}: (5, {})} | custom-call | flops 603979776 | bytes 2000000 | tf_op jit(solution)/shard_map/sweep/pallas_call | solution.py:31
  20.3 0.0 copy-start.3
  20.3 0.2 collective-permute-start.4
  20.5 4.2 %collective-permute-done.4.shifted_ref = bf16[256,256]{1,0:T(8,128)(2,1)S(1)} collective-permute-done((bf16[256,256]{1,0:T(8,128)(2,1)S(1)}, bf16[256,256]{1,0:T(8,128)(2,1)S(1)}, u32[]{:S(2)}, u32[]{:S(2)}) %collective-permute-start.4) | collective-permute-done | bytes 131104 | tf_op jit(solution)/shard_map/ppermute | solution.py:308
  24.8 2.3 %residual.1 = (f32[256,256]{1,0:T(8,128)}, bf16[32,2,16,128]{3,2,1,0:T(8,128)(2,1)}, f32[256,256]{1,0:T(8,128)S(1)}) custom-call(bf16[256,256]{1,0:T(8,128)(2,1)S(1)} %collective-permute-done.4.shifted_ref, bf16[2,256,256]{2,1,0:T(8,128)(2,1)S(1)} %get-tuple-element.21.slope_ref, ...), custom_call_target="tpu_custom_call", output_to_operand_aliasing={{2}: (3, {})} | custom-call | flops 603979776 | bytes 2000000 | tf_op jit(solution)/shard_map/residual/pallas_call | solution.py:31
  27.1 10.0 %all-to-all-start = ((bf16[64,16,128]{2,1,0:T(8,128)(2,1)}), bf16[64,16,128]{2,1,0:T(8,128)(2,1)S(1)}, u32[]{:S(2)}, u32[]{:S(2)}) async-start(bf16[64,16,128]{2,1,0:T(8,128)(2,1)} %bitcast.28), calls=%async_computation | async-start | bytes 524288 | tf_op jit(solution)/shard_map/all_to_all | solution.py:391
  37.1 0.0 copy-done.3
  37.1 1.4 %collective-permute-start.5 = (bf16[2,256,256]{2,1,0:T(8,128)(2,1)S(1)}, bf16[2,256,256]{2,1,0:T(8,128)(2,1)}, u32[]{:S(2)}, u32[]{:S(2)}) collective-permute-start(bf16[2,256,256]{2,1,0:T(8,128)(2,1)S(1)} %bitcast.19), channel_id=1, source_target_pairs={{0,1},{1,2},{2,3},{3,0},{4,5},{5,6},{6,7},{7,4},{8,9},{9,10},{10,1... | collective-permute-start | bytes 786440 | tf_op jit(solution)/shard_map/ppermute | solution.py:406
  38.5 2.6 %collective-permute-start.6 = (bf16[2,256,256]{2,1,0:T(8,128)(2,1)S(1)}, bf16[2,256,256]{2,1,0:T(8,128)(2,1)}, u32[]{:S(2)}, u32[]{:S(2)}) collective-permute-start(bf16[2,256,256]{2,1,0:T(8,128)(2,1)S(1)} %bitcast.20), channel_id=1, source_target_pairs={{0,2},{1,3},{2,0},{3,1},{4,6},{5,7},{6,4},{7,5},{8,10},{9,11},{10,... | collective-permute-start | bytes 786440 | tf_op jit(solution)/shard_map/ppermute | solution.py:406
  41.1 1.1 %collective-permute-start.7 = (bf16[2,256,256]{2,1,0:T(8,128)(2,1)S(1)}, bf16[2,256,256]{2,1,0:T(8,128)(2,1)}, u32[]{:S(2)}, u32[]{:S(2)}) collective-permute-start(bf16[2,256,256]{2,1,0:T(8,128)(2,1)S(1)} %bitcast.21), channel_id=1, source_target_pairs={{0,3},{1,0},{2,1},{3,2},{4,7},{5,4},{6,5},{7,6},{8,11},{9,8},{10,9... | collective-permute-start | bytes 786440 | tf_op jit(solution)/shard_map/ppermute | solution.py:406
  42.2 8.1 %all-to-all-done.given_ref = bf16[64,16,128]{2,1,0:T(8,128)(2,1)S(1)} async-done(((bf16[64,16,128]{2,1,0:T(8,128)(2,1)}), bf16[64,16,128]{2,1,0:T(8,128)(2,1)S(1)}, u32[]{:S(2)}, u32[]{:S(2)}) %all-to-all-start) | async-done | bytes 262176 | tf_op jit(solution)/shard_map/all_to_all | solution.py:391
  50.3 0.9 %scan.1 = bf16[64,8,128]{2,1,0:T(8,128)(2,1)} custom-call(bf16[64,16,128]{2,1,0:T(8,128)(2,1)S(1)} %all-to-all-done.given_ref), custom_call_target="tpu_custom_call" | custom-call | tf_op jit(solution)/shard_map/scan/pallas_call | solution.py:31
  51.1 4.7 %all-to-all-start.1 = ((bf16[64,8,128]{2,1,0:T(8,128)(2,1)}), bf16[64,8,128]{2,1,0:T(8,128)(2,1)S(1)}, u32[]{:S(2)}, u32[]{:S(2)}) async-start(bf16[64,8,128]{2,1,0:T(8,128)(2,1)} %scan.1), calls=%async_computation.1 | async-start | bytes 262144 | tf_op jit(solution)/shard_map/all_to_all | solution.py:391
  55.9 0.0 copy-start.2
  55.9 0.0 collective-permute-done.5.refs_1_
  55.9 0.0 collective-permute-done.6.refs_2_
  56.0 0.0 collective-permute-done.7.refs_3_
  56.0 1.5 %turn.1.refs_0_ = bf16[2,256,1024]{2,1,0:T(8,128)(2,1)S(1)} custom-call(bf16[2,256,256]{2,1,0:T(8,128)(2,1)S(1)} %bitcast.22, bf16[2,256,256]{2,1,0:T(8,128)(2,1)} %collective-permute-done.5.refs_1_, bf16[2,256,256]{2,1,0:T(8,128)(2,1)} %collective-permute-done.6.refs_2_, bf16[2,256,256]{2,1,0:T(8,128)(2,1)} %collective-permute-done.7.refs_3_), custom_call_target="tpu_custom_call" | custom-call | bytes 2000000 | tf_op jit(solution)/shard_map/turn/pallas_call | solution.py:31
  57.5 0.0 copy-start
  57.5 1.0 %copy-done = bf16[2,256,1024]{2,1,0:T(8,128)(2,1)} copy-done((bf16[2,256,1024]{2,1,0:T(8,128)(2,1)}, bf16[2,256,1024]{2,1,0:T(8,128)(2,1)S(1)}, u32[]{:S(2)}) %copy-start) | copy-done | bytes 1048600
  58.4 8.6 %all-to-all-done.1.error_ref = bf16[64,8,128]{2,1,0:T(8,128)(2,1)S(1)} async-done(((bf16[64,8,128]{2,1,0:T(8,128)(2,1)}), bf16[64,8,128]{2,1,0:T(8,128)(2,1)S(1)}, u32[]{:S(2)}, u32[]{:S(2)}) %all-to-all-start.1) | async-done | bytes 131104 | tf_op jit(solution)/shard_map/all_to_all | solution.py:391
  67.0 0.0 copy-start.1
  67.0 0.6 final.1
  67.6 1.4 %collective-permute-start.8 = (bf16[2,128,128]{2,1,0:T(8,128)(2,1)S(1)}, bf16[2,128,128]{2,1,0:T(8,128)(2,1)S(1)}, u32[]{:S(2)}, u32[]{:S(2)}) collective-permute-start(bf16[2,128,128]{2,1,0:T(8,128)(2,1)S(1)} %get-tuple-element.44), channel_id=1, source_target_pairs={{0,1},{1,2},{2,3},{3,0},{4,5},{5,6},{6,7},{7,4},{8,9},{9,10},{10,1... | collective-permute-start | bytes 196616 | tf_op jit(solution)/shard_map/ppermute | solution.py:424
  69.0 2.6 %collective-permute-start.9 = (bf16[2,128,128]{2,1,0:T(8,128)(2,1)S(1)}, bf16[2,128,128]{2,1,0:T(8,128)(2,1)S(1)}, u32[]{:S(2)}, u32[]{:S(2)}) collective-permute-start(bf16[2,128,128]{2,1,0:T(8,128)(2,1)S(1)} %get-tuple-element.43), channel_id=1, source_target_pairs={{0,2},{1,3},{2,0},{3,1},{4,6},{5,7},{6,4},{7,5},{8,10},{9,11},{10,... | collective-permute-start | bytes 196616 | tf_op jit(solution)/shard_map/ppermute | solution.py:424
  71.6 1.1 %collective-permute-start.10 = (bf16[2,128,128]{2,1,0:T(8,128)(2,1)S(1)}, bf16[2,128,128]{2,1,0:T(8,128)(2,1)S(1)}, u32[]{:S(2)}, u32[]{:S(2)}) collective-permute-start(bf16[2,128,128]{2,1,0:T(8,128)(2,1)S(1)} %get-tuple-element.42), channel_id=1, source_target_pairs={{0,3},{1,0},{2,1},{3,2},{4,7},{5,4},{6,5},{7,6},{8,11},{9,8},{10,9... | collective-permute-start | bytes 196616 | tf_op jit(solution)/shard_map/ppermute | solution.py:424
  72.7 0.0 copy-done.2
  72.7 0.0 copy-start.4
  72.7 0.9 %copy-done.4 = f32[256,256]{1,0:T(8,128)S(1)} copy-done((f32[256,256]{1,0:T(8,128)S(1)}, f32[256,256]{1,0:T(8,128)}, u32[]{:S(2)}) %copy-start.4) | copy-done | bytes 262168
  73.6 0.8 %corrected.1 = f32[2,256,256]{2,1,0:T(8,128)} custom-call(f32[256,256]{1,0:T(8,128)S(1)} %get-tuple-element.35.error_ref, f32[256,256]{1,0:T(8,128)S(1)} %bitcast.18, f32[256,256]{1,0:T(8,128)S(1)} %copy-done.4, f32[256,256]{1,0:T(8,128)S(1)} %get-tuple-element.37.inner_ref), custom_call_target="tpu_custom_call" | custom-call | bytes 2000000 | tf_op jit(solution)/shard_map/corrected/pallas_call | solution.py:31
  74.4 0.0 collective-permute-done.8.refs_2_
  74.4 0.1 collective-permute-done.9.refs_3_
  74.5 0.5 collective-permute-done.10.refs_4_
  75.0 0.0 copy-done.1
  75.0 2.1 %taps.1 = f32[2,3,3,64,256]{4,3,2,1,0:T(8,128)} custom-call(bf16[2,256,1024]{2,1,0:T(8,128)(2,1)S(1)} %copy-done.1, bf16[2,128,128]{2,1,0:T(8,128)(2,1)S(1)} %get-tuple-element.45.refs_1_, bf16[2,128,128]{2,1,0:T(8,128)(2,1)S(1)} %collective-permute-done.8.refs_2_, bf16[2,128,128]{2,1,0:T(8,128)(2,1)S(1)} %collective-permute-done.9.refs_3_, ...), custom_call_target="tpu_custom_call" | custom-call | flops 603979776 | bytes 2000000 | tf_op jit(solution)/shard_map/taps/pallas_call | solution.py:31
  (3 shorter events, 0.1 us)
Async XLA Ops:
  1.6 6.3 %collective-permute-start.1 = (bf16[256,256]{1,0:T(8,128)(2,1)S(1)}, bf16[256,256]{1,0:T(8,128)(2,1)S(1)}, u32[]{:S(2)}, u32[]{:S(2)}) collective-permute-start(bf16[256,256]{1,0:T(8,128)(2,1)S(1)} %round.1), channel_id=1, source_target_pairs={{4,0},{0,4},{12,8},{8,12},{20,16},{16,20},{28,24},{24,28},{36,32},... | collective-permute-start | bytes 393224 | tf_op jit(solution)/shard_map/ppermute | solution.py:305
  4.9 11.0 %collective-permute-start = (bf16[256,256]{1,0:T(8,128)(2,1)S(1)}, bf16[256,256]{1,0:T(8,128)(2,1)S(1)}, u32[]{:S(2)}, u32[]{:S(2)}) collective-permute-start(bf16[256,256]{1,0:T(8,128)(2,1)S(1)} %round.1), channel_id=1, source_target_pairs={{4,0},{8,4},{12,8},{16,12},{20,16},{24,20},{28,24},{32,28},{36,32}... | collective-permute-start | bytes 393224 | tf_op jit(solution)/shard_map/ppermute | solution.py:308
  8.0 9.4 %collective-permute-start.3 = (bf16[256,256]{1,0:T(8,128)(2,1)S(1)}, bf16[256,256]{1,0:T(8,128)(2,1)S(1)}, u32[]{:S(2)}, u32[]{:S(2)}) collective-permute-start(bf16[256,256]{1,0:T(8,128)(2,1)S(1)} %get-tuple-element.26), channel_id=1, source_target_pairs={{4,0},{8,4},{12,8},{16,12},{20,16},{24,20},{28,24},{32,28},{36,32}... | collective-permute-start | bytes 393224 | tf_op jit(solution)/shard_map/ppermute | solution.py:308
  17.4 1.4 %collective-permute-start.2 = (bf16[256,256]{1,0:T(8,128)(2,1)S(1)}, bf16[256,256]{1,0:T(8,128)(2,1)S(1)}, u32[]{:S(2)}, u32[]{:S(2)}) collective-permute-start(bf16[256,256]{1,0:T(8,128)(2,1)S(1)} %get-tuple-element.25), channel_id=1, source_target_pairs={{4,0},{0,4},{12,8},{8,12},{20,16},{16,20},{28,24},{24,28},{36,32},... | collective-permute-start | bytes 393224 | tf_op jit(solution)/shard_map/ppermute | solution.py:305
  20.3 16.8 %copy-start.3 = (bf16[2,1,16,16,256]{4,3,2,1,0:T(8,128)(2,1)S(1)}, bf16[2,1,16,16,256]{4,3,2,1,0:T(8,128)(2,1)}, u32[]{:S(2)}) copy-start(bf16[2,1,16,16,256]{4,3,2,1,0:T(8,128)(2,1)} %states_far.1) | copy-start | bytes 786436
  20.3 4.5 %collective-permute-start.4 = (bf16[256,256]{1,0:T(8,128)(2,1)S(1)}, bf16[256,256]{1,0:T(8,128)(2,1)S(1)}, u32[]{:S(2)}, u32[]{:S(2)}) collective-permute-start(bf16[256,256]{1,0:T(8,128)(2,1)S(1)} %get-tuple-element.28), channel_id=1, source_target_pairs={{4,0},{8,4},{12,8},{16,12},{20,16},{24,20},{28,24},{32,28},{36,32}... | collective-permute-start | bytes 393224 | tf_op jit(solution)/shard_map/ppermute | solution.py:308
  27.1 23.2 %all-to-all-start = ((bf16[64,16,128]{2,1,0:T(8,128)(2,1)}), bf16[64,16,128]{2,1,0:T(8,128)(2,1)S(1)}, u32[]{:S(2)}, u32[]{:S(2)}) async-start(bf16[64,16,128]{2,1,0:T(8,128)(2,1)} %bitcast.28), calls=%async_computation | async-start | bytes 524288 | tf_op jit(solution)/shard_map/all_to_all | solution.py:391
  37.1 18.8 %collective-permute-start.5 = (bf16[2,256,256]{2,1,0:T(8,128)(2,1)S(1)}, bf16[2,256,256]{2,1,0:T(8,128)(2,1)}, u32[]{:S(2)}, u32[]{:S(2)}) collective-permute-start(bf16[2,256,256]{2,1,0:T(8,128)(2,1)S(1)} %bitcast.19), channel_id=1, source_target_pairs={{0,1},{1,2},{2,3},{3,0},{4,5},{5,6},{6,7},{7,4},{8,9},{9,10},{10,1... | collective-permute-start | bytes 786440 | tf_op jit(solution)/shard_map/ppermute | solution.py:406
  38.5 17.5 %collective-permute-start.6 = (bf16[2,256,256]{2,1,0:T(8,128)(2,1)S(1)}, bf16[2,256,256]{2,1,0:T(8,128)(2,1)}, u32[]{:S(2)}, u32[]{:S(2)}) collective-permute-start(bf16[2,256,256]{2,1,0:T(8,128)(2,1)S(1)} %bitcast.20), channel_id=1, source_target_pairs={{0,2},{1,3},{2,0},{3,1},{4,6},{5,7},{6,4},{7,5},{8,10},{9,11},{10,... | collective-permute-start | bytes 786440 | tf_op jit(solution)/shard_map/ppermute | solution.py:406
  41.1 14.8 %collective-permute-start.7 = (bf16[2,256,256]{2,1,0:T(8,128)(2,1)S(1)}, bf16[2,256,256]{2,1,0:T(8,128)(2,1)}, u32[]{:S(2)}, u32[]{:S(2)}) collective-permute-start(bf16[2,256,256]{2,1,0:T(8,128)(2,1)S(1)} %bitcast.21), channel_id=1, source_target_pairs={{0,3},{1,0},{2,1},{3,2},{4,7},{5,4},{6,5},{7,6},{8,11},{9,8},{10,9... | collective-permute-start | bytes 786440 | tf_op jit(solution)/shard_map/ppermute | solution.py:406
  51.1 15.8 %all-to-all-start.1 = ((bf16[64,8,128]{2,1,0:T(8,128)(2,1)}), bf16[64,8,128]{2,1,0:T(8,128)(2,1)S(1)}, u32[]{:S(2)}, u32[]{:S(2)}) async-start(bf16[64,8,128]{2,1,0:T(8,128)(2,1)} %scan.1), calls=%async_computation.1 | async-start | bytes 262144 | tf_op jit(solution)/shard_map/all_to_all | solution.py:391
  55.9 16.7 %copy-start.2 = (f32[1,16,16,256]{3,2,1,0:T(8,128)S(1)}, f32[1,16,16,256]{3,2,1,0:T(8,128)}, u32[]{:S(2)}) copy-start(f32[1,16,16,256]{3,2,1,0:T(8,128)} %param.8) | copy-start | bytes 786436
  57.5 1.0 %copy-start = (bf16[2,256,1024]{2,1,0:T(8,128)(2,1)}, bf16[2,256,1024]{2,1,0:T(8,128)(2,1)S(1)}, u32[]{:S(2)}) copy-start(bf16[2,256,1024]{2,1,0:T(8,128)(2,1)S(1)} %turn.1.refs_0_) | copy-start | bytes 3145732
  67.0 8.0 %copy-start.1 = (bf16[2,256,1024]{2,1,0:T(8,128)(2,1)S(1)}, bf16[2,256,1024]{2,1,0:T(8,128)(2,1)}, u32[]{:S(2)}) copy-start(bf16[2,256,1024]{2,1,0:T(8,128)(2,1)} %copy-done) | copy-start | bytes 3145732
  67.6 6.8 %collective-permute-start.8 = (bf16[2,128,128]{2,1,0:T(8,128)(2,1)S(1)}, bf16[2,128,128]{2,1,0:T(8,128)(2,1)S(1)}, u32[]{:S(2)}, u32[]{:S(2)}) collective-permute-start(bf16[2,128,128]{2,1,0:T(8,128)(2,1)S(1)} %get-tuple-element.44), channel_id=1, source_target_pairs={{0,1},{1,2},{2,3},{3,0},{4,5},{5,6},{6,7},{7,4},{8,9},{9,10},{10,1... | collective-permute-start | bytes 196616 | tf_op jit(solution)/shard_map/ppermute | solution.py:424
  69.0 5.5 %collective-permute-start.9 = (bf16[2,128,128]{2,1,0:T(8,128)(2,1)S(1)}, bf16[2,128,128]{2,1,0:T(8,128)(2,1)S(1)}, u32[]{:S(2)}, u32[]{:S(2)}) collective-permute-start(bf16[2,128,128]{2,1,0:T(8,128)(2,1)S(1)} %get-tuple-element.43), channel_id=1, source_target_pairs={{0,2},{1,3},{2,0},{3,1},{4,6},{5,7},{6,4},{7,5},{8,10},{9,11},{10,... | collective-permute-start | bytes 196616 | tf_op jit(solution)/shard_map/ppermute | solution.py:424
  71.6 3.4 %collective-permute-start.10 = (bf16[2,128,128]{2,1,0:T(8,128)(2,1)S(1)}, bf16[2,128,128]{2,1,0:T(8,128)(2,1)S(1)}, u32[]{:S(2)}, u32[]{:S(2)}) collective-permute-start(bf16[2,128,128]{2,1,0:T(8,128)(2,1)S(1)} %get-tuple-element.42), channel_id=1, source_target_pairs={{0,3},{1,0},{2,1},{3,2},{4,7},{5,4},{6,5},{7,6},{8,11},{9,8},{10,9... | collective-permute-start | bytes 196616 | tf_op jit(solution)/shard_map/ppermute | solution.py:424
  72.7 1.0 %copy-start.4 = (f32[256,256]{1,0:T(8,128)S(1)}, f32[256,256]{1,0:T(8,128)}, u32[]{:S(2)}) copy-start(f32[256,256]{1,0:T(8,128)} %get-tuple-element.36.relax_ref) | copy-start | bytes 786436

commit v5 on v4

--- a/solution.py
+++ b/solution.py
@@ -96,32 +96,25 @@
     return right
 
 
-def round_body(width, points_far, terminal_far, out_ref, held_ref, sem):
-    edge = pltpu.make_async_copy(terminal_far, held_ref, sem)
-    plain = pltpu.make_async_copy(points_far, held_ref, sem)
-    pl.when(is_first())(edge.start)
-    pl.when(jnp.logical_not(is_first()))(plain.start)
-    plain.wait()
-    out_ref[...] = held_ref[...].astype(BF)
-
-
-def slope_body(width, states_far, kernels_far, points_far, slope_ref, turned_ref, points_ref, states_ref, kernels_ref, sems):
-    blocks, height, _, channels = states_ref.shape
-    held = [pltpu.make_async_copy(states_far.at[:, 0], states_ref, sems.at[3 * blocks])]
-    for block in range(blocks):
-        for i in range(3):
-            sem = sems.at[3 * block + i]
-            held.append(pltpu.make_async_copy(kernels_far.at[block, i], kernels_ref.at[block, i], sem))
-    held.append(pltpu.make_async_copy(points_far, points_ref, sems.at[3 * blocks + 1]))
+def load_body(width, points_far, terminal_far, states_far, kernels_far, rough_ref, points_ref, states_ref, kernels_ref, edge_ref, sems):
+    held = [
+        pltpu.make_async_copy(points_far, points_ref, sems.at[0]),
+        pltpu.make_async_copy(kernels_far, kernels_ref, sems.at[1]),
+        pltpu.make_async_copy(states_far, states_ref, sems.at[2]),
+    ]
     for copy in held:
         copy.start()
+    edge = Edge(terminal_far, edge_ref, sems.at[3])
     held[0].wait()
-
-
-    def one(block):
-        for i in range(3):
-            held[1 + 3 * block + i].wait()
-        value = states_ref[block].reshape(height * width, channels).astype(F32)
+    edge.write(points_ref, rough_ref)
+    held[1].wait()
+    held[2].wait()
+
+
+def slope_body(width, states_ref, kernels_ref, slope_ref, turned_ref):
+    blocks, _, height, _, channels = states_ref.shape
+    for block in range(blocks):
+        value = states_ref[block, 0].reshape(height * width, channels).astype(F32)
         patches = jnp.concatenate(forward_patches(value, width), 1)
         taps = kernels_ref[block].reshape(9 * channels, channels)
         act = jnp.tanh(jnp.dot(patches, taps, preferred_element_type=F32))
@@ -130,10 +123,6 @@
             for j in range(3):
                 at = (i * 3 + j) * channels
                 turned_ref[block, at : at + channels, :] = kernels_ref[block, i, j].T
-
-    for block in range(blocks):
-        stage(functools.partial(one, block))
-    held[-1].wait()
 
 
 def entering(swapped_ref, shifted_ref):
@@ -296,6 +285,7 @@
     cells = height * width
     slabs = lax.axis_size("layer")
     images = lax.axis_size("dp")
+    places = [1, 3, 2] if images == 4 else list(range(1, images))
     here = lax.axis_index("dp")
     slab = lax.axis_index("layer")
     conv_flops = 2 * cells * 9 * channels * channels
@@ -316,23 +306,26 @@
     points = adjoint_guess.reshape(cells, channels)
     last_value = terminal.reshape(cells, channels)
     gain = coarse_gain.reshape(cells, channels)
-    edge = (pltpu.VMEM((cells, channels), F32), pltpu.SemaphoreType.DMA)
-    rough = step(round_body, rounded, points, last_value, name="round", far_in=(0, 1), scratch=edge)
-    across, beside = shifted(rough), swapped(rough)
-    slopes, turned, points = step(
-        slope_body,
-        (shape((blocks, cells, channels), BF), shape((blocks, 9 * channels, channels), BF), whole),
+    rough, points, near_states, near_kernels = step(
+        load_body,
+        (rounded, whole, shape(states.shape, BF), shape(kernels.shape, BF)),
+        points,
+        last_value,
         states,
         kernels,
-        points,
+        name="load",
+        far_in=(0, 1, 2, 3),
+        scratch=(pltpu.VMEM((cells, channels), F32), pltpu.SemaphoreType.DMA((4,))),
+    )
+    across, beside = shifted(rough), swapped(rough)
+    slopes, turned = step(
+        slope_body,
+        (shape((blocks, cells, channels), BF), shape((blocks, 9 * channels, channels), BF)),
+        near_states,
+        near_kernels,
         name="slopes",
-        far_in=(0, 1, 2),
-        scratch=(
-            pltpu.VMEM((blocks, height, width, channels), BF),
-            pltpu.VMEM((blocks, 3, 3, channels, channels), BF),
-            pltpu.SemaphoreType.DMA((3 * blocks + 2,)),
-        ),
-    )
+    )
+    edge = (pltpu.VMEM((cells, channels), F32), pltpu.SemaphoreType.DMA)
     points, send = step(
         even_body,
         (whole, rounded),
@@ -402,7 +395,7 @@
     )
     error = spread(errors)
     all_states = [own_states]
-    for k in range(1, images):
+    for k in places:
         all_states.append(lax.ppermute(own_states, "dp", [(i, (i + k) % images) for i in range(images)]))
     states_turned = call(
         turn_body, shape((blocks, channels, images * cells), BF), all_states, name="turn"
@@ -419,7 +412,7 @@
     )
 
     received = [lax.dynamic_index_in_dim(signals, here, 0, keepdims=False)]
-    for k in range(1, images):
+    for k in places:
         part = lax.dynamic_index_in_dim(signals, (here + k) % images, 0, keepdims=False)
         received.append(lax.ppermute(part, "dp", [(i, (i + k) % images) for i in range(images)]))
     adjoint = call(

time: 77.6 us -> 77.2 us (level)
  Pallas kernels: 15 us -> 13.7 us
    pallas_call x11, Pallas kernels: 15 us -> 13.7 us  [call(): pl.pallas_call(body, out_shape=placed[0] if single else placed, in_specs=...]
  transfers between devices with their start and end apart: 13 -> 13, of which waited for: 6 -> 5; matrix products, arithmetic and copies ran while one was open for 0% -> 0% of each run, Pallas kernels for 10% -> 7%
where the time goes in v5:
time: 77.2 us; the launch traced here: 76.5 us
  starting transfers between devices  36.9 us (48%)
  waiting for transfers between devices  22.9 us (30%)
  Pallas kernels  13.7 us (18%)
  local copies, waits for them, and re-layouts  1.96 us (3%)
  between operations  1.06 us (1%)
    all_to_all x2, waiting for transfers between devices, spread(): return lax.all_to_all(parts, 'layer', 0, 0, tiled=True)  17.2 us
    all_to_all x2, starting transfers between devices, spread(): return lax.all_to_all(parts, 'layer', 0, 0, tiled=True)  15.2 us
    pallas_call x11, Pallas kernels, call(): pl.pallas_call(body, out_shape=placed[0] if single else placed, in_specs=...  13.7 us
    ppermute x3, starting transfers between devices, shifted(): lax.ppermute(part, 'layer', [((i + 1) % slabs, i) for i in range(slabs)])  8.08 us
    ppermute x3, starting transfers between devices, on_device(): lax.ppermute(part, 'dp', [(i, (i + k) % images) for i in range(images)])  5.67 us
    ppermute x3, starting transfers between devices, on_device(): lax.ppermute(own_states, 'dp', [(i, (i + k) % images) for i in range(imag...  4.46 us
    ppermute x3, waiting for transfers between devices, shifted(): lax.ppermute(part, 'layer', [((i + 1) % slabs, i) for i in range(slabs)])  4.25 us
    ppermute x2, starting transfers between devices, swapped(): return lax.ppermute(part, 'layer', [(i ^ 1, i) for i in range(slabs)])  3.49 us
  transfers between devices with their start and end apart: 13, of which 5 were waited for; matrix products, arithmetic and copies ran while one was open for 0% of the time, Pallas kernels for 7%

profile of v5, /device:TPU:1, one launch (start us, length us, event | category | flops | bytes accessed | tf_op | source)
XLA Modules:
  0.0 76.5 jit_solution(12900721934384191422)
XLA Ops:
  0.6 1.8 %load.1 = (bf16[256,256]{1,0:T(8,128)(2,1)S(1)}, f32[256,256]{1,0:T(8,128)S(1)}, bf16[2,1,16,16,256]{4,3,2,1,0:T(8,128)(2,1)S(1)}, bf16[2,3,3,256,256]{4,3,2,1,0:T(8,128)(2,1)S(1)}) custom-call(f32[256,256]{1,0:T(8,128)} %bitcast.28, f32[256,256]{1,0:T(8,128)} %bitcast.23, bf16[2,1,16,16,256]{4,3,2,1,0:T(8,128)(2,1)} %states_far.1, ...), custom_call_target="tpu_custom_call" | custom-call | flops 603979776 | bytes 2000000 | tf_op jit(solution)/shard_map/load/pallas_call | solution.py:31
  2.4 3.4 %collective-permute-start.1 = (bf16[256,256]{1,0:T(8,128)(2,1)S(1)}, bf16[256,256]{1,0:T(8,128)(2,1)S(1)}, u32[]{:S(2)}, u32[]{:S(2)}) collective-permute-start(bf16[256,256]{1,0:T(8,128)(2,1)S(1)} %get-tuple-element.24), channel_id=1, source_target_pairs={{4,0},{0,4},{12,8},{8,12},{20,16},{16,20},{28,24},{24,28},{36,32},... | collective-permute-start | bytes 393224 | tf_op jit(solution)/shard_map/ppermute | solution.py:295
  5.8 0.1 collective-permute-start
  5.9 0.8 %slopes.1 = (bf16[2,256,256]{2,1,0:T(8,128)(2,1)S(1)}, bf16[2,2304,256]{2,1,0:T(8,128)(2,1)S(1)}) custom-call(bf16[2,1,16,16,256]{4,3,2,1,0:T(8,128)(2,1)S(1)} %get-tuple-element.25.states_ref, bf16[2,3,3,256,256]{4,3,2,1,0:T(8,128)(2,1)S(1)} %get-tuple-element.26.kernels_ref), custom_call_target="tpu_custom_call" | custom-call | flops 603979776 | bytes 2000000 | tf_op jit(solution)/shard_map/slopes/pallas_call | solution.py:31
  6.8 0.1 collective-permute-done.1.swapped_ref
  6.9 7.8 %collective-permute-start.3 = (bf16[256,256]{1,0:T(8,128)(2,1)S(1)}, bf16[256,256]{1,0:T(8,128)(2,1)S(1)}, u32[]{:S(2)}, u32[]{:S(2)}) collective-permute-start(bf16[256,256]{1,0:T(8,128)(2,1)S(1)} %get-tuple-element.32), channel_id=1, source_target_pairs={{4,0},{8,4},{12,8},{16,12},{20,16},{24,20},{28,24},{32,28},{36,32}... | collective-permute-start | bytes 393224 | tf_op jit(solution)/shard_map/ppermute | solution.py:298
  14.6 0.0 collective-permute-done.shifted_ref
  14.6 1.5 %odd.1 = (f32[256,256]{1,0:T(8,128)S(1)}, bf16[256,256]{1,0:T(8,128)(2,1)S(1)}) custom-call(bf16[256,256]{1,0:T(8,128)(2,1)S(1)} %collective-permute-done.shifted_ref, bf16[2,256,256]{2,1,0:T(8,128)(2,1)S(1)} %get-tuple-element.27.slope_ref, bf16[2,2304,256]{2,1,0:T(8,128)(2,1)S(1)} %get-tuple-element.28.turned_ref, ...), custom_call_target="tpu_custom_call", output_to_operand_aliasing={{0}: (3, {})} | custom-call | flops 603979776 | bytes 2000000 | tf_op jit(solution)/shard_map/odd/pallas_call | solution.py:31
  16.1 0.1 collective-permute-start.2
  16.2 0.0 collective-permute-done.3
  16.2 1.3 %collective-permute-done.2.swapped_ref = bf16[256,256]{1,0:T(8,128)(2,1)S(1)} collective-permute-done((bf16[256,256]{1,0:T(8,128)(2,1)S(1)}, bf16[256,256]{1,0:T(8,128)(2,1)S(1)}, u32[]{:S(2)}, u32[]{:S(2)}) %collective-permute-start.2) | collective-permute-done | bytes 131104 | tf_op jit(solution)/shard_map/ppermute | solution.py:295
  17.5 1.5 %sweep.1 = (f32[256,256]{1,0:T(8,128)S(1)}, bf16[256,256]{1,0:T(8,128)(2,1)S(1)}) custom-call(bf16[256,256]{1,0:T(8,128)(2,1)S(1)} %collective-permute-done.2.swapped_ref, bf16[256,256]{1,0:T(8,128)(2,1)S(1)} %broadcast_select_fusion.shifted_ref, f32[256,256]{1,0:T(8,128)} %bitcast.25, ...), custom_call_target="tpu_custom_call", output_to_operand_aliasing={{0}: (5, {})} | custom-call | flops 603979776 | bytes 2000000 | tf_op jit(solution)/shard_map/sweep/pallas_call | solution.py:31
  19.0 0.0 copy-start.3
  19.0 0.2 collective-permute-start.4
  19.3 4.2 %collective-permute-done.4.shifted_ref = bf16[256,256]{1,0:T(8,128)(2,1)S(1)} collective-permute-done((bf16[256,256]{1,0:T(8,128)(2,1)S(1)}, bf16[256,256]{1,0:T(8,128)(2,1)S(1)}, u32[]{:S(2)}, u32[]{:S(2)}) %collective-permute-start.4) | collective-permute-done | bytes 131104 | tf_op jit(solution)/shard_map/ppermute | solution.py:298
  23.5 2.3 %residual.1 = (f32[256,256]{1,0:T(8,128)}, bf16[32,2,16,128]{3,2,1,0:T(8,128)(2,1)}, f32[256,256]{1,0:T(8,128)S(1)}) custom-call(bf16[256,256]{1,0:T(8,128)(2,1)S(1)} %collective-permute-done.4.shifted_ref, bf16[2,256,256]{2,1,0:T(8,128)(2,1)S(1)} %get-tuple-element.27.slope_ref, ...), custom_call_target="tpu_custom_call", output_to_operand_aliasing={{2}: (3, {})} | custom-call | flops 603979776 | bytes 2000000 | tf_op jit(solution)/shard_map/residual/pallas_call | solution.py:31
  25.8 10.5 %all-to-all-start = ((bf16[64,16,128]{2,1,0:T(8,128)(2,1)}), bf16[64,16,128]{2,1,0:T(8,128)(2,1)S(1)}, u32[]{:S(2)}, u32[]{:S(2)}) async-start(bf16[64,16,128]{2,1,0:T(8,128)(2,1)} %bitcast.29), calls=%async_computation | async-start | bytes 524288 | tf_op jit(solution)/shard_map/all_to_all | solution.py:384
  36.3 0.0 copy-done.3
  36.3 1.4 %collective-permute-start.5 = (bf16[2,256,256]{2,1,0:T(8,128)(2,1)S(1)}, bf16[2,256,256]{2,1,0:T(8,128)(2,1)}, u32[]{:S(2)}, u32[]{:S(2)}) collective-permute-start(bf16[2,256,256]{2,1,0:T(8,128)(2,1)S(1)} %bitcast.19), channel_id=1, source_target_pairs={{0,1},{1,2},{2,3},{3,0},{4,5},{5,6},{6,7},{7,4},{8,9},{9,10},{10,1... | collective-permute-start | bytes 786440 | tf_op jit(solution)/shard_map/ppermute | solution.py:399
  37.7 1.5 %collective-permute-start.6 = (bf16[2,256,256]{2,1,0:T(8,128)(2,1)S(1)}, bf16[2,256,256]{2,1,0:T(8,128)(2,1)}, u32[]{:S(2)}, u32[]{:S(2)}) collective-permute-start(bf16[2,256,256]{2,1,0:T(8,128)(2,1)S(1)} %bitcast.20), channel_id=1, source_target_pairs={{0,3},{1,0},{2,1},{3,2},{4,7},{5,4},{6,5},{7,6},{8,11},{9,8},{10,9... | collective-permute-start | bytes 786440 | tf_op jit(solution)/shard_map/ppermute | solution.py:399
  39.2 1.6 %collective-permute-start.7 = (bf16[2,256,256]{2,1,0:T(8,128)(2,1)S(1)}, bf16[2,256,256]{2,1,0:T(8,128)(2,1)}, u32[]{:S(2)}, u32[]{:S(2)}) collective-permute-start(bf16[2,256,256]{2,1,0:T(8,128)(2,1)S(1)} %bitcast.21), channel_id=1, source_target_pairs={{0,2},{1,3},{2,0},{3,1},{4,6},{5,7},{6,4},{7,5},{8,10},{9,11},{10,... | collective-permute-start | bytes 786440 | tf_op jit(solution)/shard_map/ppermute | solution.py:399
  40.8 8.7 %all-to-all-done.given_ref = bf16[64,16,128]{2,1,0:T(8,128)(2,1)S(1)} async-done(((bf16[64,16,128]{2,1,0:T(8,128)(2,1)}), bf16[64,16,128]{2,1,0:T(8,128)(2,1)S(1)}, u32[]{:S(2)}, u32[]{:S(2)}) %all-to-all-start) | async-done | bytes 262176 | tf_op jit(solution)/shard_map/all_to_all | solution.py:384
  49.4 0.8 %scan.1 = bf16[64,8,128]{2,1,0:T(8,128)(2,1)} custom-call(bf16[64,16,128]{2,1,0:T(8,128)(2,1)S(1)} %all-to-all-done.given_ref), custom_call_target="tpu_custom_call" | custom-call | tf_op jit(solution)/shard_map/scan/pallas_call | solution.py:31
  50.3 4.7 %all-to-all-start.1 = ((bf16[64,8,128]{2,1,0:T(8,128)(2,1)}), bf16[64,8,128]{2,1,0:T(8,128)(2,1)S(1)}, u32[]{:S(2)}, u32[]{:S(2)}) async-start(bf16[64,8,128]{2,1,0:T(8,128)(2,1)} %scan.1), calls=%async_computation.1 | async-start | bytes 262144 | tf_op jit(solution)/shard_map/all_to_all | solution.py:384
  55.1 0.0 copy-start.2
  55.1 0.0 collective-permute-done.5.refs_1_
  55.1 0.0 collective-permute-done.6.refs_2_
  55.1 0.0 collective-permute-done.7.refs_3_
  55.1 1.5 %turn.1.refs_0_ = bf16[2,256,1024]{2,1,0:T(8,128)(2,1)S(1)} custom-call(bf16[2,256,256]{2,1,0:T(8,128)(2,1)S(1)} %bitcast.22, bf16[2,256,256]{2,1,0:T(8,128)(2,1)} %collective-permute-done.5.refs_1_, bf16[2,256,256]{2,1,0:T(8,128)(2,1)} %collective-permute-done.6.refs_2_, bf16[2,256,256]{2,1,0:T(8,128)(2,1)} %collective-permute-done.7.refs_3_), custom_call_target="tpu_custom_call" | custom-call | bytes 2000000 | tf_op jit(solution)/shard_map/turn/pallas_call | solution.py:31
  56.6 0.0 copy-start
  56.6 1.0 %copy-done = bf16[2,256,1024]{2,1,0:T(8,128)(2,1)} copy-done((bf16[2,256,1024]{2,1,0:T(8,128)(2,1)}, bf16[2,256,1024]{2,1,0:T(8,128)(2,1)S(1)}, u32[]{:S(2)}) %copy-start) | copy-done | bytes 1048600
  57.6 8.6 %all-to-all-done.1.error_ref = bf16[64,8,128]{2,1,0:T(8,128)(2,1)S(1)} async-done(((bf16[64,8,128]{2,1,0:T(8,128)(2,1)}), bf16[64,8,128]{2,1,0:T(8,128)(2,1)S(1)}, u32[]{:S(2)}, u32[]{:S(2)}) %all-to-all-start.1) | async-done | bytes 131104 | tf_op jit(solution)/shard_map/all_to_all | solution.py:384
  66.1 0.0 copy-start.1
  66.1 0.6 final.1
  66.8 3.0 %collective-permute-start.10 = (bf16[2,128,128]{2,1,0:T(8,128)(2,1)S(1)}, bf16[2,128,128]{2,1,0:T(8,128)(2,1)S(1)}, u32[]{:S(2)}, u32[]{:S(2)}) collective-permute-start(bf16[2,128,128]{2,1,0:T(8,128)(2,1)S(1)} %get-tuple-element.48), channel_id=1, source_target_pairs={{0,2},{1,3},{2,0},{3,1},{4,6},{5,7},{6,4},{7,5},{8,10},{9,11},{10,... | collective-permute-start | bytes 196616 | tf_op jit(solution)/shard_map/ppermute | solution.py:417
  69.8 0.4 collective-permute-start.8
  70.1 2.3 %collective-permute-start.9 = (bf16[2,128,128]{2,1,0:T(8,128)(2,1)S(1)}, bf16[2,128,128]{2,1,0:T(8,128)(2,1)S(1)}, u32[]{:S(2)}, u32[]{:S(2)}) collective-permute-start(bf16[2,128,128]{2,1,0:T(8,128)(2,1)S(1)} %get-tuple-element.49), channel_id=1, source_target_pairs={{0,3},{1,0},{2,1},{3,2},{4,7},{5,4},{6,5},{7,6},{8,11},{9,8},{10,9... | collective-permute-start | bytes 196616 | tf_op jit(solution)/shard_map/ppermute | solution.py:417
  72.4 0.0 copy-done.2
  72.4 0.0 copy-start.4
  72.4 0.9 %copy-done.4 = f32[256,256]{1,0:T(8,128)S(1)} copy-done((f32[256,256]{1,0:T(8,128)S(1)}, f32[256,256]{1,0:T(8,128)}, u32[]{:S(2)}) %copy-start.4) | copy-done | bytes 262168
  73.4 0.8 %corrected.1 = f32[2,256,256]{2,1,0:T(8,128)} custom-call(f32[256,256]{1,0:T(8,128)S(1)} %get-tuple-element.41.error_ref, f32[256,256]{1,0:T(8,128)S(1)} %bitcast.18, f32[256,256]{1,0:T(8,128)S(1)} %copy-done.4, f32[256,256]{1,0:T(8,128)S(1)} %get-tuple-element.43.inner_ref), custom_call_target="tpu_custom_call" | custom-call | bytes 2000000 | tf_op jit(solution)/shard_map/corrected/pallas_call | solution.py:31
  74.2 0.0 collective-permute-done.10.refs_4_
  74.2 0.0 collective-permute-done.8.refs_2_
  74.2 0.0 collective-permute-done.9.refs_3_
  74.2 0.0 copy-done.1
  74.2 2.1 %taps.1 = f32[2,3,3,64,256]{4,3,2,1,0:T(8,128)} custom-call(bf16[2,256,1024]{2,1,0:T(8,128)(2,1)S(1)} %copy-done.1, bf16[2,128,128]{2,1,0:T(8,128)(2,1)S(1)} %get-tuple-element.51.refs_1_, bf16[2,128,128]{2,1,0:T(8,128)(2,1)S(1)} %collective-permute-done.8.refs_2_, bf16[2,128,128]{2,1,0:T(8,128)(2,1)S(1)} %collective-permute-done.9.refs_3_, ...), custom_call_target="tpu_custom_call" | custom-call | flops 603979776 | bytes 2000000 | tf_op jit(solution)/shard_map/taps/pallas_call | solution.py:31
  (3 shorter events, 0.1 us)
Async XLA Ops:
  2.4 4.4 %collective-permute-start.1 = (bf16[256,256]{1,0:T(8,128)(2,1)S(1)}, bf16[256,256]{1,0:T(8,128)(2,1)S(1)}, u32[]{:S(2)}, u32[]{:S(2)}) collective-permute-start(bf16[256,256]{1,0:T(8,128)(2,1)S(1)} %get-tuple-element.24), channel_id=1, source_target_pairs={{4,0},{0,4},{12,8},{8,12},{20,16},{16,20},{28,24},{24,28},{36,32},... | collective-permute-start | bytes 393224 | tf_op jit(solution)/shard_map/ppermute | solution.py:295
  5.8 8.8 %collective-permute-start = (bf16[256,256]{1,0:T(8,128)(2,1)S(1)}, bf16[256,256]{1,0:T(8,128)(2,1)S(1)}, u32[]{:S(2)}, u32[]{:S(2)}) collective-permute-start(bf16[256,256]{1,0:T(8,128)(2,1)S(1)} %get-tuple-element.24), channel_id=1, source_target_pairs={{4,0},{8,4},{12,8},{16,12},{20,16},{24,20},{28,24},{32,28},{36,32}... | collective-permute-start | bytes 393224 | tf_op jit(solution)/shard_map/ppermute | solution.py:298
  6.9 9.3 %collective-permute-start.3 = (bf16[256,256]{1,0:T(8,128)(2,1)S(1)}, bf16[256,256]{1,0:T(8,128)(2,1)S(1)}, u32[]{:S(2)}, u32[]{:S(2)}) collective-permute-start(bf16[256,256]{1,0:T(8,128)(2,1)S(1)} %get-tuple-element.32), channel_id=1, source_target_pairs={{4,0},{8,4},{12,8},{16,12},{20,16},{24,20},{28,24},{32,28},{36,32}... | collective-permute-start | bytes 393224 | tf_op jit(solution)/shard_map/ppermute | solution.py:298
  16.1 1.4 %collective-permute-start.2 = (bf16[256,256]{1,0:T(8,128)(2,1)S(1)}, bf16[256,256]{1,0:T(8,128)(2,1)S(1)}, u32[]{:S(2)}, u32[]{:S(2)}) collective-permute-start(bf16[256,256]{1,0:T(8,128)(2,1)S(1)} %get-tuple-element.31), channel_id=1, source_target_pairs={{4,0},{0,4},{12,8},{8,12},{20,16},{16,20},{28,24},{24,28},{36,32},... | collective-permute-start | bytes 393224 | tf_op jit(solution)/shard_map/ppermute | solution.py:295
  19.0 17.3 %copy-start.3 = (bf16[2,1,16,16,256]{4,3,2,1,0:T(8,128)(2,1)S(1)}, bf16[2,1,16,16,256]{4,3,2,1,0:T(8,128)(2,1)}, u32[]{:S(2)}) copy-start(bf16[2,1,16,16,256]{4,3,2,1,0:T(8,128)(2,1)} %states_far.1) | copy-start | bytes 786436
  19.0 4.5 %collective-permute-start.4 = (bf16[256,256]{1,0:T(8,128)(2,1)S(1)}, bf16[256,256]{1,0:T(8,128)(2,1)S(1)}, u32[]{:S(2)}, u32[]{:S(2)}) collective-permute-start(bf16[256,256]{1,0:T(8,128)(2,1)S(1)} %get-tuple-element.34), channel_id=1, source_target_pairs={{4,0},{8,4},{12,8},{16,12},{20,16},{24,20},{28,24},{32,28},{36,32}... | collective-permute-start | bytes 393224 | tf_op jit(solution)/shard_map/ppermute | solution.py:298
  25.8 23.6 %all-to-all-start = ((bf16[64,16,128]{2,1,0:T(8,128)(2,1)}), bf16[64,16,128]{2,1,0:T(8,128)(2,1)S(1)}, u32[]{:S(2)}, u32[]{:S(2)}) async-start(bf16[64,16,128]{2,1,0:T(8,128)(2,1)} %bitcast.29), calls=%async_computation | async-start | bytes 524288 | tf_op jit(solution)/shard_map/all_to_all | solution.py:384
  36.3 18.8 %collective-permute-start.5 = (bf16[2,256,256]{2,1,0:T(8,128)(2,1)S(1)}, bf16[2,256,256]{2,1,0:T(8,128)(2,1)}, u32[]{:S(2)}, u32[]{:S(2)}) collective-permute-start(bf16[2,256,256]{2,1,0:T(8,128)(2,1)S(1)} %bitcast.19), channel_id=1, source_target_pairs={{0,1},{1,2},{2,3},{3,0},{4,5},{5,6},{6,7},{7,4},{8,9},{9,10},{10,1... | collective-permute-start | bytes 786440 | tf_op jit(solution)/shard_map/ppermute | solution.py:399
  37.7 17.4 %collective-permute-start.6 = (bf16[2,256,256]{2,1,0:T(8,128)(2,1)S(1)}, bf16[2,256,256]{2,1,0:T(8,128)(2,1)}, u32[]{:S(2)}, u32[]{:S(2)}) collective-permute-start(bf16[2,256,256]{2,1,0:T(8,128)(2,1)S(1)} %bitcast.20), channel_id=1, source_target_pairs={{0,3},{1,0},{2,1},{3,2},{4,7},{5,4},{6,5},{7,6},{8,11},{9,8},{10,9... | collective-permute-start | bytes 786440 | tf_op jit(solution)/shard_map/ppermute | solution.py:399
  39.2 15.9 %collective-permute-start.7 = (bf16[2,256,256]{2,1,0:T(8,128)(2,1)S(1)}, bf16[2,256,256]{2,1,0:T(8,128)(2,1)}, u32[]{:S(2)}, u32[]{:S(2)}) collective-permute-start(bf16[2,256,256]{2,1,0:T(8,128)(2,1)S(1)} %bitcast.21), channel_id=1, source_target_pairs={{0,2},{1,3},{2,0},{3,1},{4,6},{5,7},{6,4},{7,5},{8,10},{9,11},{10,... | collective-permute-start | bytes 786440 | tf_op jit(solution)/shard_map/ppermute | solution.py:399
  50.3 15.8 %all-to-all-start.1 = ((bf16[64,8,128]{2,1,0:T(8,128)(2,1)}), bf16[64,8,128]{2,1,0:T(8,128)(2,1)S(1)}, u32[]{:S(2)}, u32[]{:S(2)}) async-start(bf16[64,8,128]{2,1,0:T(8,128)(2,1)} %scan.1), calls=%async_computation.1 | async-start | bytes 262144 | tf_op jit(solution)/shard_map/all_to_all | solution.py:384
  55.1 17.3 %copy-start.2 = (f32[1,16,16,256]{3,2,1,0:T(8,128)S(1)}, f32[1,16,16,256]{3,2,1,0:T(8,128)}, u32[]{:S(2)}) copy-start(f32[1,16,16,256]{3,2,1,0:T(8,128)} %param.8) | copy-start | bytes 786436
  56.6 1.0 %copy-start = (bf16[2,256,1024]{2,1,0:T(8,128)(2,1)}, bf16[2,256,1024]{2,1,0:T(8,128)(2,1)S(1)}, u32[]{:S(2)}) copy-start(bf16[2,256,1024]{2,1,0:T(8,128)(2,1)S(1)} %turn.1.refs_0_) | copy-start | bytes 3145732
  66.1 8.1 %copy-start.1 = (bf16[2,256,1024]{2,1,0:T(8,128)(2,1)S(1)}, bf16[2,256,1024]{2,1,0:T(8,128)(2,1)}, u32[]{:S(2)}) copy-start(bf16[2,256,1024]{2,1,0:T(8,128)(2,1)} %copy-done) | copy-start | bytes 3145732
  66.8 7.4 %collective-permute-start.10 = (bf16[2,128,128]{2,1,0:T(8,128)(2,1)S(1)}, bf16[2,128,128]{2,1,0:T(8,128)(2,1)S(1)}, u32[]{:S(2)}, u32[]{:S(2)}) collective-permute-start(bf16[2,128,128]{2,1,0:T(8,128)(2,1)S(1)} %get-tuple-element.48), channel_id=1, source_target_pairs={{0,2},{1,3},{2,0},{3,1},{4,6},{5,7},{6,4},{7,5},{8,10},{9,11},{10,... | collective-permute-start | bytes 196616 | tf_op jit(solution)/shard_map/ppermute | solution.py:417
  69.8 4.5 %collective-permute-start.8 = (bf16[2,128,128]{2,1,0:T(8,128)(2,1)S(1)}, bf16[2,128,128]{2,1,0:T(8,128)(2,1)S(1)}, u32[]{:S(2)}, u32[]{:S(2)}) collective-permute-start(bf16[2,128,128]{2,1,0:T(8,128)(2,1)S(1)} %get-tuple-element.50), channel_id=1, source_target_pairs={{0,1},{1,2},{2,3},{3,0},{4,5},{5,6},{6,7},{7,4},{8,9},{9,10},{10,1... | collective-permute-start | bytes 196616 | tf_op jit(solution)/shard_map/ppermute | solution.py:417
  70.1 4.1 %collective-permute-start.9 = (bf16[2,128,128]{2,1,0:T(8,128)(2,1)S(1)}, bf16[2,128,128]{2,1,0:T(8,128)(2,1)S(1)}, u32[]{:S(2)}, u32[]{:S(2)}) collective-permute-start(bf16[2,128,128]{2,1,0:T(8,128)(2,1)S(1)} %get-tuple-element.49), channel_id=1, source_target_pairs={{0,3},{1,0},{2,1},{3,2},{4,7},{5,4},{6,5},{7,6},{8,11},{9,8},{10,9... | collective-permute-start | bytes 196616 | tf_op jit(solution)/shard_map/ppermute | solution.py:417
  72.4 1.0 %copy-start.4 = (f32[256,256]{1,0:T(8,128)S(1)}, f32[256,256]{1,0:T(8,128)}, u32[]{:S(2)}) copy-start(f32[256,256]{1,0:T(8,128)} %get-tuple-element.42.relax_ref) | copy-start | bytes 786436

commit v6 on v5

--- a/solution.py
+++ b/solution.py
@@ -285,7 +285,7 @@
     cells = height * width
     slabs = lax.axis_size("layer")
     images = lax.axis_size("dp")
-    places = [1, 3, 2] if images == 4 else list(range(1, images))
+    places = [2, 3, 1] if images == 4 else list(range(1, images))
     here = lax.axis_index("dp")
     slab = lax.axis_index("layer")
     conv_flops = 2 * cells * 9 * channels * channels

time: 77.2 us -> 76.7 us (level)
  transfers between devices with their start and end apart: 13 -> 13, of which waited for: 5 -> 7; matrix products, arithmetic and copies ran while one was open for 0% -> 0% of each run, Pallas kernels for 7% -> 7%
where the time goes in v6:
time: 76.7 us; the launch traced here: 76.4 us
  starting transfers between devices  36.3 us (47%)
  waiting for transfers between devices  23.4 us (31%)
  Pallas kernels  13.7 us (18%)
  local copies, waits for them, and re-layouts  1.96 us (3%)
  between operations  1.04 us (1%)
    all_to_all x2, waiting for transfers between devices, spread(): return lax.all_to_all(parts, 'layer', 0, 0, tiled=True)  17.2 us
    all_to_all x2, starting transfers between devices, spread(): return lax.all_to_all(parts, 'layer', 0, 0, tiled=True)  15.2 us
    pallas_call x11, Pallas kernels, call(): pl.pallas_call(body, out_shape=placed[0] if single else placed, in_specs=...  13.7 us
    ppermute x3, starting transfers between devices, shifted(): lax.ppermute(part, 'layer', [((i + 1) % slabs, i) for i in range(slabs)])  8.08 us
    ppermute x3, starting transfers between devices, on_device(): lax.ppermute(part, 'dp', [(i, (i + k) % images) for i in range(images)])  5.06 us
    ppermute x3, starting transfers between devices, on_device(): lax.ppermute(own_states, 'dp', [(i, (i + k) % images) for i in range(imag...  4.47 us
    ppermute x3, waiting for transfers between devices, shifted(): lax.ppermute(part, 'layer', [((i + 1) % slabs, i) for i in range(slabs)])  4.25 us
    ppermute x2, starting transfers between devices, swapped(): return lax.ppermute(part, 'layer', [(i ^ 1, i) for i in range(slabs)])  3.49 us
  transfers between devices with their start and end apart: 13, of which 7 were waited for; matrix products, arithmetic and copies ran while one was open for 0% of the time, Pallas kernels for 7%

profile of v6, /device:TPU:1, one launch (start us, length us, event | category | flops | bytes accessed | tf_op | source)
XLA Modules:
  0.0 76.4 jit_solution(2347727843525251407)
XLA Ops:
  0.6 1.8 %load.1 = (bf16[256,256]{1,0:T(8,128)(2,1)S(1)}, f32[256,256]{1,0:T(8,128)S(1)}, bf16[2,1,16,16,256]{4,3,2,1,0:T(8,128)(2,1)S(1)}, bf16[2,3,3,256,256]{4,3,2,1,0:T(8,128)(2,1)S(1)}) custom-call(f32[256,256]{1,0:T(8,128)} %bitcast.28, f32[256,256]{1,0:T(8,128)} %bitcast.23, bf16[2,1,16,16,256]{4,3,2,1,0:T(8,128)(2,1)} %states_far.1, ...), custom_call_target="tpu_custom_call" | custom-call | flops 603979776 | bytes 2000000 | tf_op jit(solution)/shard_map/load/pallas_call | solution.py:31
  2.4 3.4 %collective-permute-start.1 = (bf16[256,256]{1,0:T(8,128)(2,1)S(1)}, bf16[256,256]{1,0:T(8,128)(2,1)S(1)}, u32[]{:S(2)}, u32[]{:S(2)}) collective-permute-start(bf16[256,256]{1,0:T(8,128)(2,1)S(1)} %get-tuple-element.24), channel_id=1, source_target_pairs={{4,0},{0,4},{12,8},{8,12},{20,16},{16,20},{28,24},{24,28},{36,32},... | collective-permute-start | bytes 393224 | tf_op jit(solution)/shard_map/ppermute | solution.py:295
  5.8 0.1 collective-permute-start
  5.9 0.8 %slopes.1 = (bf16[2,256,256]{2,1,0:T(8,128)(2,1)S(1)}, bf16[2,2304,256]{2,1,0:T(8,128)(2,1)S(1)}) custom-call(bf16[2,1,16,16,256]{4,3,2,1,0:T(8,128)(2,1)S(1)} %get-tuple-element.25.states_ref, bf16[2,3,3,256,256]{4,3,2,1,0:T(8,128)(2,1)S(1)} %get-tuple-element.26.kernels_ref), custom_call_target="tpu_custom_call" | custom-call | flops 603979776 | bytes 2000000 | tf_op jit(solution)/shard_map/slopes/pallas_call | solution.py:31
  6.8 0.1 collective-permute-done.1.swapped_ref
  6.9 7.8 %collective-permute-start.3 = (bf16[256,256]{1,0:T(8,128)(2,1)S(1)}, bf16[256,256]{1,0:T(8,128)(2,1)S(1)}, u32[]{:S(2)}, u32[]{:S(2)}) collective-permute-start(bf16[256,256]{1,0:T(8,128)(2,1)S(1)} %get-tuple-element.32), channel_id=1, source_target_pairs={{4,0},{8,4},{12,8},{16,12},{20,16},{24,20},{28,24},{32,28},{36,32}... | collective-permute-start | bytes 393224 | tf_op jit(solution)/shard_map/ppermute | solution.py:298
  14.6 0.0 collective-permute-done.shifted_ref
  14.6 1.5 %odd.1 = (f32[256,256]{1,0:T(8,128)S(1)}, bf16[256,256]{1,0:T(8,128)(2,1)S(1)}) custom-call(bf16[256,256]{1,0:T(8,128)(2,1)S(1)} %collective-permute-done.shifted_ref, bf16[2,256,256]{2,1,0:T(8,128)(2,1)S(1)} %get-tuple-element.27.slope_ref, bf16[2,2304,256]{2,1,0:T(8,128)(2,1)S(1)} %get-tuple-element.28.turned_ref, ...), custom_call_target="tpu_custom_call", output_to_operand_aliasing={{0}: (3, {})} | custom-call | flops 603979776 | bytes 2000000 | tf_op jit(solution)/shard_map/odd/pallas_call | solution.py:31
  16.1 0.1 collective-permute-start.2
  16.2 0.0 collective-permute-done.3
  16.2 1.3 %collective-permute-done.2.swapped_ref = bf16[256,256]{1,0:T(8,128)(2,1)S(1)} collective-permute-done((bf16[256,256]{1,0:T(8,128)(2,1)S(1)}, bf16[256,256]{1,0:T(8,128)(2,1)S(1)}, u32[]{:S(2)}, u32[]{:S(2)}) %collective-permute-start.2) | collective-permute-done | bytes 131104 | tf_op jit(solution)/shard_map/ppermute | solution.py:295
  17.5 1.5 %sweep.1 = (f32[256,256]{1,0:T(8,128)S(1)}, bf16[256,256]{1,0:T(8,128)(2,1)S(1)}) custom-call(bf16[256,256]{1,0:T(8,128)(2,1)S(1)} %collective-permute-done.2.swapped_ref, bf16[256,256]{1,0:T(8,128)(2,1)S(1)} %broadcast_select_fusion.shifted_ref, f32[256,256]{1,0:T(8,128)} %bitcast.25, ...), custom_call_target="tpu_custom_call", output_to_operand_aliasing={{0}: (5, {})} | custom-call | flops 603979776 | bytes 2000000 | tf_op jit(solution)/shard_map/sweep/pallas_call | solution.py:31
  19.0 0.0 copy-start.3
  19.0 0.2 collective-permute-start.4
  19.3 4.2 %collective-permute-done.4.shifted_ref = bf16[256,256]{1,0:T(8,128)(2,1)S(1)} collective-permute-done((bf16[256,256]{1,0:T(8,128)(2,1)S(1)}, bf16[256,256]{1,0:T(8,128)(2,1)S(1)}, u32[]{:S(2)}, u32[]{:S(2)}) %collective-permute-start.4) | collective-permute-done | bytes 131104 | tf_op jit(solution)/shard_map/ppermute | solution.py:298
  23.5 2.3 %residual.1 = (f32[256,256]{1,0:T(8,128)}, bf16[32,2,16,128]{3,2,1,0:T(8,128)(2,1)}, f32[256,256]{1,0:T(8,128)S(1)}) custom-call(bf16[256,256]{1,0:T(8,128)(2,1)S(1)} %collective-permute-done.4.shifted_ref, bf16[2,256,256]{2,1,0:T(8,128)(2,1)S(1)} %get-tuple-element.27.slope_ref, ...), custom_call_target="tpu_custom_call", output_to_operand_aliasing={{2}: (3, {})} | custom-call | flops 603979776 | bytes 2000000 | tf_op jit(solution)/shard_map/residual/pallas_call | solution.py:31
  25.8 10.5 %all-to-all-start = ((bf16[64,16,128]{2,1,0:T(8,128)(2,1)}), bf16[64,16,128]{2,1,0:T(8,128)(2,1)S(1)}, u32[]{:S(2)}, u32[]{:S(2)}) async-start(bf16[64,16,128]{2,1,0:T(8,128)(2,1)} %bitcast.29), calls=%async_computation | async-start | bytes 524288 | tf_op jit(solution)/shard_map/all_to_all | solution.py:384
  36.3 0.0 copy-done.3
  36.3 3.0 %collective-permute-start.5 = (bf16[2,256,256]{2,1,0:T(8,128)(2,1)S(1)}, bf16[2,256,256]{2,1,0:T(8,128)(2,1)}, u32[]{:S(2)}, u32[]{:S(2)}) collective-permute-start(bf16[2,256,256]{2,1,0:T(8,128)(2,1)S(1)} %bitcast.19), channel_id=1, source_target_pairs={{0,2},{1,3},{2,0},{3,1},{4,6},{5,7},{6,4},{7,5},{8,10},{9,11},{10,... | collective-permute-start | bytes 786440 | tf_op jit(solution)/shard_map/ppermute | solution.py:399
  39.3 0.8 %collective-permute-start.6 = (bf16[2,256,256]{2,1,0:T(8,128)(2,1)S(1)}, bf16[2,256,256]{2,1,0:T(8,128)(2,1)}, u32[]{:S(2)}, u32[]{:S(2)}) collective-permute-start(bf16[2,256,256]{2,1,0:T(8,128)(2,1)S(1)} %bitcast.20), channel_id=1, source_target_pairs={{0,3},{1,0},{2,1},{3,2},{4,7},{5,4},{6,5},{7,6},{8,11},{9,8},{10,9... | collective-permute-start | bytes 786440 | tf_op jit(solution)/shard_map/ppermute | solution.py:399
  40.1 0.7 collective-permute-start.7
  40.8 8.7 %all-to-all-done.given_ref = bf16[64,16,128]{2,1,0:T(8,128)(2,1)S(1)} async-done(((bf16[64,16,128]{2,1,0:T(8,128)(2,1)}), bf16[64,16,128]{2,1,0:T(8,128)(2,1)S(1)}, u32[]{:S(2)}, u32[]{:S(2)}) %all-to-all-start) | async-done | bytes 262176 | tf_op jit(solution)/shard_map/all_to_all | solution.py:384
  49.4 0.8 %scan.1 = bf16[64,8,128]{2,1,0:T(8,128)(2,1)} custom-call(bf16[64,16,128]{2,1,0:T(8,128)(2,1)S(1)} %all-to-all-done.given_ref), custom_call_target="tpu_custom_call" | custom-call | tf_op jit(solution)/shard_map/scan/pallas_call | solution.py:31
  50.3 4.7 %all-to-all-start.1 = ((bf16[64,8,128]{2,1,0:T(8,128)(2,1)}), bf16[64,8,128]{2,1,0:T(8,128)(2,1)S(1)}, u32[]{:S(2)}, u32[]{:S(2)}) async-start(bf16[64,8,128]{2,1,0:T(8,128)(2,1)} %scan.1), calls=%async_computation.1 | async-start | bytes 262144 | tf_op jit(solution)/shard_map/all_to_all | solution.py:384
  55.1 0.0 copy-start.2
  55.1 0.0 collective-permute-done.5.refs_1_
  55.1 0.0 collective-permute-done.6.refs_2_
  55.1 0.0 collective-permute-done.7.refs_3_
  55.1 1.5 %turn.1.refs_0_ = bf16[2,256,1024]{2,1,0:T(8,128)(2,1)S(1)} custom-call(bf16[2,256,256]{2,1,0:T(8,128)(2,1)S(1)} %bitcast.22, bf16[2,256,256]{2,1,0:T(8,128)(2,1)} %collective-permute-done.5.refs_1_, bf16[2,256,256]{2,1,0:T(8,128)(2,1)} %collective-permute-done.6.refs_2_, bf16[2,256,256]{2,1,0:T(8,128)(2,1)} %collective-permute-done.7.refs_3_), custom_call_target="tpu_custom_call" | custom-call | bytes 2000000 | tf_op jit(solution)/shard_map/turn/pallas_call | solution.py:31
  56.6 0.0 copy-start
  56.6 1.0 %copy-done = bf16[2,256,1024]{2,1,0:T(8,128)(2,1)} copy-done((bf16[2,256,1024]{2,1,0:T(8,128)(2,1)}, bf16[2,256,1024]{2,1,0:T(8,128)(2,1)S(1)}, u32[]{:S(2)}) %copy-start) | copy-done | bytes 1048600
  57.6 8.6 %all-to-all-done.1.error_ref = bf16[64,8,128]{2,1,0:T(8,128)(2,1)S(1)} async-done(((bf16[64,8,128]{2,1,0:T(8,128)(2,1)}), bf16[64,8,128]{2,1,0:T(8,128)(2,1)S(1)}, u32[]{:S(2)}, u32[]{:S(2)}) %all-to-all-start.1) | async-done | bytes 131104 | tf_op jit(solution)/shard_map/all_to_all | solution.py:384
  66.1 0.0 copy-start.1
  66.1 0.6 final.1
  66.8 1.4 %collective-permute-start.10 = (bf16[2,128,128]{2,1,0:T(8,128)(2,1)S(1)}, bf16[2,128,128]{2,1,0:T(8,128)(2,1)S(1)}, u32[]{:S(2)}, u32[]{:S(2)}) collective-permute-start(bf16[2,128,128]{2,1,0:T(8,128)(2,1)S(1)} %get-tuple-element.48), channel_id=1, source_target_pairs={{0,1},{1,2},{2,3},{3,0},{4,5},{5,6},{6,7},{7,4},{8,9},{9,10},{10,1... | collective-permute-start | bytes 196616 | tf_op jit(solution)/shard_map/ppermute | solution.py:417
  68.1 2.6 %collective-permute-start.8 = (bf16[2,128,128]{2,1,0:T(8,128)(2,1)S(1)}, bf16[2,128,128]{2,1,0:T(8,128)(2,1)S(1)}, u32[]{:S(2)}, u32[]{:S(2)}) collective-permute-start(bf16[2,128,128]{2,1,0:T(8,128)(2,1)S(1)} %get-tuple-element.50), channel_id=1, source_target_pairs={{0,2},{1,3},{2,0},{3,1},{4,6},{5,7},{6,4},{7,5},{8,10},{9,11},{10,... | collective-permute-start | bytes 196616 | tf_op jit(solution)/shard_map/ppermute | solution.py:417
  70.7 1.1 %collective-permute-start.9 = (bf16[2,128,128]{2,1,0:T(8,128)(2,1)S(1)}, bf16[2,128,128]{2,1,0:T(8,128)(2,1)S(1)}, u32[]{:S(2)}, u32[]{:S(2)}) collective-permute-start(bf16[2,128,128]{2,1,0:T(8,128)(2,1)S(1)} %get-tuple-element.49), channel_id=1, source_target_pairs={{0,3},{1,0},{2,1},{3,2},{4,7},{5,4},{6,5},{7,6},{8,11},{9,8},{10,9... | collective-permute-start | bytes 196616 | tf_op jit(solution)/shard_map/ppermute | solution.py:417
  71.8 0.0 copy-done.2
  71.8 0.0 copy-start.4
  71.8 0.9 %copy-done.4 = f32[256,256]{1,0:T(8,128)S(1)} copy-done((f32[256,256]{1,0:T(8,128)S(1)}, f32[256,256]{1,0:T(8,128)}, u32[]{:S(2)}) %copy-start.4) | copy-done | bytes 262168
  72.8 0.8 %corrected.1 = f32[2,256,256]{2,1,0:T(8,128)} custom-call(f32[256,256]{1,0:T(8,128)S(1)} %get-tuple-element.41.error_ref, f32[256,256]{1,0:T(8,128)S(1)} %bitcast.18, f32[256,256]{1,0:T(8,128)S(1)} %copy-done.4, f32[256,256]{1,0:T(8,128)S(1)} %get-tuple-element.43.inner_ref), custom_call_target="tpu_custom_call" | custom-call | bytes 2000000 | tf_op jit(solution)/shard_map/corrected/pallas_call | solution.py:31
  73.6 0.0 collective-permute-done.10.refs_4_
  73.6 0.1 collective-permute-done.8.refs_2_
  73.7 0.5 collective-permute-done.9.refs_3_
  74.2 0.0 copy-done.1
  74.2 2.1 %taps.1 = f32[2,3,3,64,256]{4,3,2,1,0:T(8,128)} custom-call(bf16[2,256,1024]{2,1,0:T(8,128)(2,1)S(1)} %copy-done.1, bf16[2,128,128]{2,1,0:T(8,128)(2,1)S(1)} %get-tuple-element.51.refs_1_, bf16[2,128,128]{2,1,0:T(8,128)(2,1)S(1)} %collective-permute-done.8.refs_2_, bf16[2,128,128]{2,1,0:T(8,128)(2,1)S(1)} %collective-permute-done.9.refs_3_, ...), custom_call_target="tpu_custom_call" | custom-call | flops 603979776 | bytes 2000000 | tf_op jit(solution)/shard_map/taps/pallas_call | solution.py:31
  (3 shorter events, 0.1 us)
Async XLA Ops:
  2.4 4.4 %collective-permute-start.1 = (bf16[256,256]{1,0:T(8,128)(2,1)S(1)}, bf16[256,256]{1,0:T(8,128)(2,1)S(1)}, u32[]{:S(2)}, u32[]{:S(2)}) collective-permute-start(bf16[256,256]{1,0:T(8,128)(2,1)S(1)} %get-tuple-element.24), channel_id=1, source_target_pairs={{4,0},{0,4},{12,8},{8,12},{20,16},{16,20},{28,24},{24,28},{36,32},... | collective-permute-start | bytes 393224 | tf_op jit(solution)/shard_map/ppermute | solution.py:295
  5.8 8.8 %collective-permute-start = (bf16[256,256]{1,0:T(8,128)(2,1)S(1)}, bf16[256,256]{1,0:T(8,128)(2,1)S(1)}, u32[]{:S(2)}, u32[]{:S(2)}) collective-permute-start(bf16[256,256]{1,0:T(8,128)(2,1)S(1)} %get-tuple-element.24), channel_id=1, source_target_pairs={{4,0},{8,4},{12,8},{16,12},{20,16},{24,20},{28,24},{32,28},{36,32}... | collective-permute-start | bytes 393224 | tf_op jit(solution)/shard_map/ppermute | solution.py:298
  6.9 9.3 %collective-permute-start.3 = (bf16[256,256]{1,0:T(8,128)(2,1)S(1)}, bf16[256,256]{1,0:T(8,128)(2,1)S(1)}, u32[]{:S(2)}, u32[]{:S(2)}) collective-permute-start(bf16[256,256]{1,0:T(8,128)(2,1)S(1)} %get-tuple-element.32), channel_id=1, source_target_pairs={{4,0},{8,4},{12,8},{16,12},{20,16},{24,20},{28,24},{32,28},{36,32}... | collective-permute-start | bytes 393224 | tf_op jit(solution)/shard_map/ppermute | solution.py:298
  16.1 1.4 %collective-permute-start.2 = (bf16[256,256]{1,0:T(8,128)(2,1)S(1)}, bf16[256,256]{1,0:T(8,128)(2,1)S(1)}, u32[]{:S(2)}, u32[]{:S(2)}) collective-permute-start(bf16[256,256]{1,0:T(8,128)(2,1)S(1)} %get-tuple-element.31), channel_id=1, source_target_pairs={{4,0},{0,4},{12,8},{8,12},{20,16},{16,20},{28,24},{24,28},{36,32},... | collective-permute-start | bytes 393224 | tf_op jit(solution)/shard_map/ppermute | solution.py:295
  19.0 17.3 %copy-start.3 = (bf16[2,1,16,16,256]{4,3,2,1,0:T(8,128)(2,1)S(1)}, bf16[2,1,16,16,256]{4,3,2,1,0:T(8,128)(2,1)}, u32[]{:S(2)}) copy-start(bf16[2,1,16,16,256]{4,3,2,1,0:T(8,128)(2,1)} %states_far.1) | copy-start | bytes 786436
  19.0 4.5 %collective-permute-start.4 = (bf16[256,256]{1,0:T(8,128)(2,1)S(1)}, bf16[256,256]{1,0:T(8,128)(2,1)S(1)}, u32[]{:S(2)}, u32[]{:S(2)}) collective-permute-start(bf16[256,256]{1,0:T(8,128)(2,1)S(1)} %get-tuple-element.34), channel_id=1, source_target_pairs={{4,0},{8,4},{12,8},{16,12},{20,16},{24,20},{28,24},{32,28},{36,32}... | collective-permute-start | bytes 393224 | tf_op jit(solution)/shard_map/ppermute | solution.py:298
  25.8 23.6 %all-to-all-start = ((bf16[64,16,128]{2,1,0:T(8,128)(2,1)}), bf16[64,16,128]{2,1,0:T(8,128)(2,1)S(1)}, u32[]{:S(2)}, u32[]{:S(2)}) async-start(bf16[64,16,128]{2,1,0:T(8,128)(2,1)} %bitcast.29), calls=%async_computation | async-start | bytes 524288 | tf_op jit(solution)/shard_map/all_to_all | solution.py:384
  36.3 18.8 %collective-permute-start.5 = (bf16[2,256,256]{2,1,0:T(8,128)(2,1)S(1)}, bf16[2,256,256]{2,1,0:T(8,128)(2,1)}, u32[]{:S(2)}, u32[]{:S(2)}) collective-permute-start(bf16[2,256,256]{2,1,0:T(8,128)(2,1)S(1)} %bitcast.19), channel_id=1, source_target_pairs={{0,2},{1,3},{2,0},{3,1},{4,6},{5,7},{6,4},{7,5},{8,10},{9,11},{10,... | collective-permute-start | bytes 786440 | tf_op jit(solution)/shard_map/ppermute | solution.py:399
  39.3 15.8 %collective-permute-start.6 = (bf16[2,256,256]{2,1,0:T(8,128)(2,1)S(1)}, bf16[2,256,256]{2,1,0:T(8,128)(2,1)}, u32[]{:S(2)}, u32[]{:S(2)}) collective-permute-start(bf16[2,256,256]{2,1,0:T(8,128)(2,1)S(1)} %bitcast.20), channel_id=1, source_target_pairs={{0,3},{1,0},{2,1},{3,2},{4,7},{5,4},{6,5},{7,6},{8,11},{9,8},{10,9... | collective-permute-start | bytes 786440 | tf_op jit(solution)/shard_map/ppermute | solution.py:399
  40.1 15.0 %collective-permute-start.7 = (bf16[2,256,256]{2,1,0:T(8,128)(2,1)S(1)}, bf16[2,256,256]{2,1,0:T(8,128)(2,1)}, u32[]{:S(2)}, u32[]{:S(2)}) collective-permute-start(bf16[2,256,256]{2,1,0:T(8,128)(2,1)S(1)} %bitcast.21), channel_id=1, source_target_pairs={{0,1},{1,2},{2,3},{3,0},{4,5},{5,6},{6,7},{7,4},{8,9},{9,10},{10,1... | collective-permute-start | bytes 786440 | tf_op jit(solution)/shard_map/ppermute | solution.py:399
  50.3 15.8 %all-to-all-start.1 = ((bf16[64,8,128]{2,1,0:T(8,128)(2,1)}), bf16[64,8,128]{2,1,0:T(8,128)(2,1)S(1)}, u32[]{:S(2)}, u32[]{:S(2)}) async-start(bf16[64,8,128]{2,1,0:T(8,128)(2,1)} %scan.1), calls=%async_computation.1 | async-start | bytes 262144 | tf_op jit(solution)/shard_map/all_to_all | solution.py:384
  55.1 16.7 %copy-start.2 = (f32[1,16,16,256]{3,2,1,0:T(8,128)S(1)}, f32[1,16,16,256]{3,2,1,0:T(8,128)}, u32[]{:S(2)}) copy-start(f32[1,16,16,256]{3,2,1,0:T(8,128)} %param.8) | copy-start | bytes 786436
  56.6 1.0 %copy-start = (bf16[2,256,1024]{2,1,0:T(8,128)(2,1)}, bf16[2,256,1024]{2,1,0:T(8,128)(2,1)S(1)}, u32[]{:S(2)}) copy-start(bf16[2,256,1024]{2,1,0:T(8,128)(2,1)S(1)} %turn.1.refs_0_) | copy-start | bytes 3145732
  66.1 8.0 %copy-start.1 = (bf16[2,256,1024]{2,1,0:T(8,128)(2,1)S(1)}, bf16[2,256,1024]{2,1,0:T(8,128)(2,1)}, u32[]{:S(2)}) copy-start(bf16[2,256,1024]{2,1,0:T(8,128)(2,1)} %copy-done) | copy-start | bytes 3145732
  66.8 6.8 %collective-permute-start.10 = (bf16[2,128,128]{2,1,0:T(8,128)(2,1)S(1)}, bf16[2,128,128]{2,1,0:T(8,128)(2,1)S(1)}, u32[]{:S(2)}, u32[]{:S(2)}) collective-permute-start(bf16[2,128,128]{2,1,0:T(8,128)(2,1)S(1)} %get-tuple-element.48), channel_id=1, source_target_pairs={{0,1},{1,2},{2,3},{3,0},{4,5},{5,6},{6,7},{7,4},{8,9},{9,10},{10,1... | collective-permute-start | bytes 196616 | tf_op jit(solution)/shard_map/ppermute | solution.py:417
  68.1 5.5 %collective-permute-start.8 = (bf16[2,128,128]{2,1,0:T(8,128)(2,1)S(1)}, bf16[2,128,128]{2,1,0:T(8,128)(2,1)S(1)}, u32[]{:S(2)}, u32[]{:S(2)}) collective-permute-start(bf16[2,128,128]{2,1,0:T(8,128)(2,1)S(1)} %get-tuple-element.50), channel_id=1, source_target_pairs={{0,2},{1,3},{2,0},{3,1},{4,6},{5,7},{6,4},{7,5},{8,10},{9,11},{10,... | collective-permute-start | bytes 196616 | tf_op jit(solution)/shard_map/ppermute | solution.py:417
  70.7 3.4 %collective-permute-start.9 = (bf16[2,128,128]{2,1,0:T(8,128)(2,1)S(1)}, bf16[2,128,128]{2,1,0:T(8,128)(2,1)S(1)}, u32[]{:S(2)}, u32[]{:S(2)}) collective-permute-start(bf16[2,128,128]{2,1,0:T(8,128)(2,1)S(1)} %get-tuple-element.49), channel_id=1, source_target_pairs={{0,3},{1,0},{2,1},{3,2},{4,7},{5,4},{6,5},{7,6},{8,11},{9,8},{10,9... | collective-permute-start | bytes 196616 | tf_op jit(solution)/shard_map/ppermute | solution.py:417
  71.8 1.0 %copy-start.4 = (f32[256,256]{1,0:T(8,128)S(1)}, f32[256,256]{1,0:T(8,128)}, u32[]{:S(2)}) copy-start(f32[256,256]{1,0:T(8,128)} %get-tuple-element.42.relax_ref) | copy-start | bytes 786436

commit v7 on v6

--- a/solution.py
+++ b/solution.py
@@ -200,16 +200,29 @@
         relax_copy.wait()
 
 
-def scan_body(given_ref, out_far, out_ref, sem):
+def scan_body(given_ref, out_far, out_ref, carry_ref, sems):
     count = given_ref.shape[0]
-    error = jnp.zeros((8, 128), F32)
-    for at in range(count - 1, -1, -1):
-        out_ref[at] = error.astype(BF)
-        term = given_ref[at].astype(F32)
-        error = error - term[8:] * error + term[:8]
-    copy = pltpu.make_async_copy(out_ref, out_far, sem)
-    copy.start()
-    copy.wait()
+    half = count // 2
+    parts = [pl.ds(0, half), pl.ds(half, count - half)]
+    copies = [pltpu.make_async_copy(out_ref.at[part], out_far.at[part], sems.at[k]) for k, part in enumerate(parts)]
+
+    def sweep_down(first, stop, error):
+        for at in range(first - 1, stop - 1, -1):
+            out_ref[at] = error.astype(BF)
+            term = given_ref[at].astype(F32)
+            error = error - term[8:] * error + term[:8]
+        return error
+
+    carry_ref[...] = sweep_down(count, half, jnp.zeros((8, 128), F32))
+    copies[1].start()
+
+    @stage
+    def _():
+        sweep_down(half, 0, carry_ref[...])
+        copies[0].start()
+
+    for copy in copies:
+        copy.wait()
 
 
 def final_body(width, points_ref, error_ref, slope_ref, turned_ref, inner_ref, error_out_ref, signal_ref):
@@ -391,7 +404,11 @@
         name="scan",
         moved=0,
         far_out=(0,),
-        scratch=(pltpu.VMEM((slabs, 8, 128), BF), pltpu.SemaphoreType.DMA),
+        scratch=(
+            pltpu.VMEM((slabs, 8, 128), BF),
+            pltpu.VMEM((8, 128), F32),
+            pltpu.SemaphoreType.DMA((2,)),
+        ),
     )
     error = spread(errors)
     all_states = [own_states]

time: 76.7 us -> 76.7 us (level)
  no operation moved by 1% of the time
where the time goes in v7:
time: 76.7 us; the launch traced here: 76.4 us
  starting transfers between devices  36.3 us (47%)
  waiting for transfers between devices  23.4 us (31%)
  Pallas kernels  13.7 us (18%)
  local copies, waits for them, and re-layouts  1.96 us (3%)
  between operations  1.04 us (1%)
    all_to_all x2, waiting for transfers between devices, spread(): return lax.all_to_all(parts, 'layer', 0, 0, tiled=True)  17.2 us
    all_to_all x2, starting transfers between devices, spread(): return lax.all_to_all(parts, 'layer', 0, 0, tiled=True)  15.2 us
    pallas_call x11, Pallas kernels, call(): pl.pallas_call(body, out_shape=placed[0] if single else placed, in_specs=...  13.7 us
    ppermute x3, starting transfers between devices, shifted(): lax.ppermute(part, 'layer', [((i + 1) % slabs, i) for i in range(slabs)])  8.08 us
    ppermute x3, starting transfers between devices, on_device(): lax.ppermute(part, 'dp', [(i, (i + k) % images) for i in range(images)])  5.07 us
    ppermute x3, starting transfers between devices, on_device(): lax.ppermute(own_states, 'dp', [(i, (i + k) % images) for i in range(imag...  4.47 us
    ppermute x3, waiting for transfers between devices, shifted(): lax.ppermute(part, 'layer', [((i + 1) % slabs, i) for i in range(slabs)])  4.25 us
    ppermute x2, starting transfers between devices, swapped(): return lax.ppermute(part, 'layer', [(i ^ 1, i) for i in range(slabs)])  3.49 us
  transfers between devices with their start and end apart: 13, of which 7 were waited for; matrix products, arithmetic and copies ran while one was open for 0% of the time, Pallas kernels for 7%

profile of v7, /device:TPU:1, one launch (start us, length us, event | category | flops | bytes accessed | tf_op | source)
XLA Modules:
  0.0 76.4 jit_solution(3006602141960939729)
XLA Ops:
  0.6 1.8 %load.1 = (bf16[256,256]{1,0:T(8,128)(2,1)S(1)}, f32[256,256]{1,0:T(8,128)S(1)}, bf16[2,1,16,16,256]{4,3,2,1,0:T(8,128)(2,1)S(1)}, bf16[2,3,3,256,256]{4,3,2,1,0:T(8,128)(2,1)S(1)}) custom-call(f32[256,256]{1,0:T(8,128)} %bitcast.28, f32[256,256]{1,0:T(8,128)} %bitcast.23, bf16[2,1,16,16,256]{4,3,2,1,0:T(8,128)(2,1)} %states_far.1, ...), custom_call_target="tpu_custom_call" | custom-call | flops 603979776 | bytes 2000000 | tf_op jit(solution)/shard_map/load/pallas_call | solution.py:31
  2.4 3.4 %collective-permute-start.1 = (bf16[256,256]{1,0:T(8,128)(2,1)S(1)}, bf16[256,256]{1,0:T(8,128)(2,1)S(1)}, u32[]{:S(2)}, u32[]{:S(2)}) collective-permute-start(bf16[256,256]{1,0:T(8,128)(2,1)S(1)} %get-tuple-element.24), channel_id=1, source_target_pairs={{4,0},{0,4},{12,8},{8,12},{20,16},{16,20},{28,24},{24,28},{36,32},... | collective-permute-start | bytes 393224 | tf_op jit(solution)/shard_map/ppermute | solution.py:308
  5.8 0.1 collective-permute-start
  5.9 0.8 %slopes.1 = (bf16[2,256,256]{2,1,0:T(8,128)(2,1)S(1)}, bf16[2,2304,256]{2,1,0:T(8,128)(2,1)S(1)}) custom-call(bf16[2,1,16,16,256]{4,3,2,1,0:T(8,128)(2,1)S(1)} %get-tuple-element.25.states_ref, bf16[2,3,3,256,256]{4,3,2,1,0:T(8,128)(2,1)S(1)} %get-tuple-element.26.kernels_ref), custom_call_target="tpu_custom_call" | custom-call | flops 603979776 | bytes 2000000 | tf_op jit(solution)/shard_map/slopes/pallas_call | solution.py:31
  6.8 0.1 collective-permute-done.1.swapped_ref
  6.9 7.8 %collective-permute-start.3 = (bf16[256,256]{1,0:T(8,128)(2,1)S(1)}, bf16[256,256]{1,0:T(8,128)(2,1)S(1)}, u32[]{:S(2)}, u32[]{:S(2)}) collective-permute-start(bf16[256,256]{1,0:T(8,128)(2,1)S(1)} %get-tuple-element.32), channel_id=1, source_target_pairs={{4,0},{8,4},{12,8},{16,12},{20,16},{24,20},{28,24},{32,28},{36,32}... | collective-permute-start | bytes 393224 | tf_op jit(solution)/shard_map/ppermute | solution.py:311
  14.6 0.0 collective-permute-done.shifted_ref
  14.6 1.5 %odd.1 = (f32[256,256]{1,0:T(8,128)S(1)}, bf16[256,256]{1,0:T(8,128)(2,1)S(1)}) custom-call(bf16[256,256]{1,0:T(8,128)(2,1)S(1)} %collective-permute-done.shifted_ref, bf16[2,256,256]{2,1,0:T(8,128)(2,1)S(1)} %get-tuple-element.27.slope_ref, bf16[2,2304,256]{2,1,0:T(8,128)(2,1)S(1)} %get-tuple-element.28.turned_ref, ...), custom_call_target="tpu_custom_call", output_to_operand_aliasing={{0}: (3, {})} | custom-call | flops 603979776 | bytes 2000000 | tf_op jit(solution)/shard_map/odd/pallas_call | solution.py:31
  16.1 0.1 collective-permute-start.2
  16.2 0.0 collective-permute-done.3
  16.2 1.3 %collective-permute-done.2.swapped_ref = bf16[256,256]{1,0:T(8,128)(2,1)S(1)} collective-permute-done((bf16[256,256]{1,0:T(8,128)(2,1)S(1)}, bf16[256,256]{1,0:T(8,128)(2,1)S(1)}, u32[]{:S(2)}, u32[]{:S(2)}) %collective-permute-start.2) | collective-permute-done | bytes 131104 | tf_op jit(solution)/shard_map/ppermute | solution.py:308
  17.5 1.5 %sweep.1 = (f32[256,256]{1,0:T(8,128)S(1)}, bf16[256,256]{1,0:T(8,128)(2,1)S(1)}) custom-call(bf16[256,256]{1,0:T(8,128)(2,1)S(1)} %collective-permute-done.2.swapped_ref, bf16[256,256]{1,0:T(8,128)(2,1)S(1)} %broadcast_select_fusion.shifted_ref, f32[256,256]{1,0:T(8,128)} %bitcast.25, ...), custom_call_target="tpu_custom_call", output_to_operand_aliasing={{0}: (5, {})} | custom-call | flops 603979776 | bytes 2000000 | tf_op jit(solution)/shard_map/sweep/pallas_call | solution.py:31
  19.0 0.0 copy-start.3
  19.0 0.2 collective-permute-start.4
  19.3 4.2 %collective-permute-done.4.shifted_ref = bf16[256,256]{1,0:T(8,128)(2,1)S(1)} collective-permute-done((bf16[256,256]{1,0:T(8,128)(2,1)S(1)}, bf16[256,256]{1,0:T(8,128)(2,1)S(1)}, u32[]{:S(2)}, u32[]{:S(2)}) %collective-permute-start.4) | collective-permute-done | bytes 131104 | tf_op jit(solution)/shard_map/ppermute | solution.py:311
  23.5 2.3 %residual.1 = (f32[256,256]{1,0:T(8,128)}, bf16[32,2,16,128]{3,2,1,0:T(8,128)(2,1)}, f32[256,256]{1,0:T(8,128)S(1)}) custom-call(bf16[256,256]{1,0:T(8,128)(2,1)S(1)} %collective-permute-done.4.shifted_ref, bf16[2,256,256]{2,1,0:T(8,128)(2,1)S(1)} %get-tuple-element.27.slope_ref, ...), custom_call_target="tpu_custom_call", output_to_operand_aliasing={{2}: (3, {})} | custom-call | flops 603979776 | bytes 2000000 | tf_op jit(solution)/shard_map/residual/pallas_call | solution.py:31
  25.8 10.5 %all-to-all-start = ((bf16[64,16,128]{2,1,0:T(8,128)(2,1)}), bf16[64,16,128]{2,1,0:T(8,128)(2,1)S(1)}, u32[]{:S(2)}, u32[]{:S(2)}) async-start(bf16[64,16,128]{2,1,0:T(8,128)(2,1)} %bitcast.29), calls=%async_computation | async-start | bytes 524288 | tf_op jit(solution)/shard_map/all_to_all | solution.py:397
  36.3 0.0 copy-done.3
  36.3 3.0 %collective-permute-start.5 = (bf16[2,256,256]{2,1,0:T(8,128)(2,1)S(1)}, bf16[2,256,256]{2,1,0:T(8,128)(2,1)}, u32[]{:S(2)}, u32[]{:S(2)}) collective-permute-start(bf16[2,256,256]{2,1,0:T(8,128)(2,1)S(1)} %bitcast.19), channel_id=1, source_target_pairs={{0,2},{1,3},{2,0},{3,1},{4,6},{5,7},{6,4},{7,5},{8,10},{9,11},{10,... | collective-permute-start | bytes 786440 | tf_op jit(solution)/shard_map/ppermute | solution.py:416
  39.3 0.8 %collective-permute-start.6 = (bf16[2,256,256]{2,1,0:T(8,128)(2,1)S(1)}, bf16[2,256,256]{2,1,0:T(8,128)(2,1)}, u32[]{:S(2)}, u32[]{:S(2)}) collective-permute-start(bf16[2,256,256]{2,1,0:T(8,128)(2,1)S(1)} %bitcast.20), channel_id=1, source_target_pairs={{0,3},{1,0},{2,1},{3,2},{4,7},{5,4},{6,5},{7,6},{8,11},{9,8},{10,9... | collective-permute-start | bytes 786440 | tf_op jit(solution)/shard_map/ppermute | solution.py:416
  40.1 0.7 collective-permute-start.7
  40.8 8.7 %all-to-all-done.given_ref = bf16[64,16,128]{2,1,0:T(8,128)(2,1)S(1)} async-done(((bf16[64,16,128]{2,1,0:T(8,128)(2,1)}), bf16[64,16,128]{2,1,0:T(8,128)(2,1)S(1)}, u32[]{:S(2)}, u32[]{:S(2)}) %all-to-all-start) | async-done | bytes 262176 | tf_op jit(solution)/shard_map/all_to_all | solution.py:397
  49.4 0.8 %scan.1 = bf16[64,8,128]{2,1,0:T(8,128)(2,1)} custom-call(bf16[64,16,128]{2,1,0:T(8,128)(2,1)S(1)} %all-to-all-done.given_ref), custom_call_target="tpu_custom_call" | custom-call | tf_op jit(solution)/shard_map/scan/pallas_call | solution.py:31
  50.3 4.7 %all-to-all-start.1 = ((bf16[64,8,128]{2,1,0:T(8,128)(2,1)}), bf16[64,8,128]{2,1,0:T(8,128)(2,1)S(1)}, u32[]{:S(2)}, u32[]{:S(2)}) async-start(bf16[64,8,128]{2,1,0:T(8,128)(2,1)} %scan.1), calls=%async_computation.1 | async-start | bytes 262144 | tf_op jit(solution)/shard_map/all_to_all | solution.py:397
  55.1 0.0 copy-start.2
  55.1 0.0 collective-permute-done.5.refs_1_
  55.1 0.0 collective-permute-done.6.refs_2_
  55.1 0.0 collective-permute-done.7.refs_3_
  55.1 1.5 %turn.1.refs_0_ = bf16[2,256,1024]{2,1,0:T(8,128)(2,1)S(1)} custom-call(bf16[2,256,256]{2,1,0:T(8,128)(2,1)S(1)} %bitcast.22, bf16[2,256,256]{2,1,0:T(8,128)(2,1)} %collective-permute-done.5.refs_1_, bf16[2,256,256]{2,1,0:T(8,128)(2,1)} %collective-permute-done.6.refs_2_, bf16[2,256,256]{2,1,0:T(8,128)(2,1)} %collective-permute-done.7.refs_3_), custom_call_target="tpu_custom_call" | custom-call | bytes 2000000 | tf_op jit(solution)/shard_map/turn/pallas_call | solution.py:31
  56.6 0.0 copy-start
  56.6 1.0 %copy-done = bf16[2,256,1024]{2,1,0:T(8,128)(2,1)} copy-done((bf16[2,256,1024]{2,1,0:T(8,128)(2,1)}, bf16[2,256,1024]{2,1,0:T(8,128)(2,1)S(1)}, u32[]{:S(2)}) %copy-start) | copy-done | bytes 1048600
  57.6 8.6 %all-to-all-done.1.error_ref = bf16[64,8,128]{2,1,0:T(8,128)(2,1)S(1)} async-done(((bf16[64,8,128]{2,1,0:T(8,128)(2,1)}), bf16[64,8,128]{2,1,0:T(8,128)(2,1)S(1)}, u32[]{:S(2)}, u32[]{:S(2)}) %all-to-all-start.1) | async-done | bytes 131104 | tf_op jit(solution)/shard_map/all_to_all | solution.py:397
  66.1 0.0 copy-start.1
  66.1 0.6 final.1
  66.7 1.4 %collective-permute-start.10 = (bf16[2,128,128]{2,1,0:T(8,128)(2,1)S(1)}, bf16[2,128,128]{2,1,0:T(8,128)(2,1)S(1)}, u32[]{:S(2)}, u32[]{:S(2)}) collective-permute-start(bf16[2,128,128]{2,1,0:T(8,128)(2,1)S(1)} %get-tuple-element.48), channel_id=1, source_target_pairs={{0,1},{1,2},{2,3},{3,0},{4,5},{5,6},{6,7},{7,4},{8,9},{9,10},{10,1... | collective-permute-start | bytes 196616 | tf_op jit(solution)/shard_map/ppermute | solution.py:434
  68.1 2.6 %collective-permute-start.8 = (bf16[2,128,128]{2,1,0:T(8,128)(2,1)S(1)}, bf16[2,128,128]{2,1,0:T(8,128)(2,1)S(1)}, u32[]{:S(2)}, u32[]{:S(2)}) collective-permute-start(bf16[2,128,128]{2,1,0:T(8,128)(2,1)S(1)} %get-tuple-element.50), channel_id=1, source_target_pairs={{0,2},{1,3},{2,0},{3,1},{4,6},{5,7},{6,4},{7,5},{8,10},{9,11},{10,... | collective-permute-start | bytes 196616 | tf_op jit(solution)/shard_map/ppermute | solution.py:434
  70.7 1.1 %collective-permute-start.9 = (bf16[2,128,128]{2,1,0:T(8,128)(2,1)S(1)}, bf16[2,128,128]{2,1,0:T(8,128)(2,1)S(1)}, u32[]{:S(2)}, u32[]{:S(2)}) collective-permute-start(bf16[2,128,128]{2,1,0:T(8,128)(2,1)S(1)} %get-tuple-element.49), channel_id=1, source_target_pairs={{0,3},{1,0},{2,1},{3,2},{4,7},{5,4},{6,5},{7,6},{8,11},{9,8},{10,9... | collective-permute-start | bytes 196616 | tf_op jit(solution)/shard_map/ppermute | solution.py:434
  71.8 0.0 copy-done.2
  71.8 0.0 copy-start.4
  71.8 0.9 %copy-done.4 = f32[256,256]{1,0:T(8,128)S(1)} copy-done((f32[256,256]{1,0:T(8,128)S(1)}, f32[256,256]{1,0:T(8,128)}, u32[]{:S(2)}) %copy-start.4) | copy-done | bytes 262168
  72.8 0.8 %corrected.1 = f32[2,256,256]{2,1,0:T(8,128)} custom-call(f32[256,256]{1,0:T(8,128)S(1)} %get-tuple-element.41.error_ref, f32[256,256]{1,0:T(8,128)S(1)} %bitcast.18, f32[256,256]{1,0:T(8,128)S(1)} %copy-done.4, f32[256,256]{1,0:T(8,128)S(1)} %get-tuple-element.43.inner_ref), custom_call_target="tpu_custom_call" | custom-call | bytes 2000000 | tf_op jit(solution)/shard_map/corrected/pallas_call | solution.py:31
  73.6 0.0 collective-permute-done.10.refs_4_
  73.6 0.1 collective-permute-done.8.refs_2_
  73.7 0.5 collective-permute-done.9.refs_3_
  74.2 0.0 copy-done.1
  74.2 2.1 %taps.1 = f32[2,3,3,64,256]{4,3,2,1,0:T(8,128)} custom-call(bf16[2,256,1024]{2,1,0:T(8,128)(2,1)S(1)} %copy-done.1, bf16[2,128,128]{2,1,0:T(8,128)(2,1)S(1)} %get-tuple-element.51.refs_1_, bf16[2,128,128]{2,1,0:T(8,128)(2,1)S(1)} %collective-permute-done.8.refs_2_, bf16[2,128,128]{2,1,0:T(8,128)(2,1)S(1)} %collective-permute-done.9.refs_3_, ...), custom_call_target="tpu_custom_call" | custom-call | flops 603979776 | bytes 2000000 | tf_op jit(solution)/shard_map/taps/pallas_call | solution.py:31
  (3 shorter events, 0.1 us)
Async XLA Ops:
  2.4 4.4 %collective-permute-start.1 = (bf16[256,256]{1,0:T(8,128)(2,1)S(1)}, bf16[256,256]{1,0:T(8,128)(2,1)S(1)}, u32[]{:S(2)}, u32[]{:S(2)}) collective-permute-start(bf16[256,256]{1,0:T(8,128)(2,1)S(1)} %get-tuple-element.24), channel_id=1, source_target_pairs={{4,0},{0,4},{12,8},{8,12},{20,16},{16,20},{28,24},{24,28},{36,32},... | collective-permute-start | bytes 393224 | tf_op jit(solution)/shard_map/ppermute | solution.py:308
  5.8 8.8 %collective-permute-start = (bf16[256,256]{1,0:T(8,128)(2,1)S(1)}, bf16[256,256]{1,0:T(8,128)(2,1)S(1)}, u32[]{:S(2)}, u32[]{:S(2)}) collective-permute-start(bf16[256,256]{1,0:T(8,128)(2,1)S(1)} %get-tuple-element.24), channel_id=1, source_target_pairs={{4,0},{8,4},{12,8},{16,12},{20,16},{24,20},{28,24},{32,28},{36,32}... | collective-permute-start | bytes 393224 | tf_op jit(solution)/shard_map/ppermute | solution.py:311
  6.9 9.3 %collective-permute-start.3 = (bf16[256,256]{1,0:T(8,128)(2,1)S(1)}, bf16[256,256]{1,0:T(8,128)(2,1)S(1)}, u32[]{:S(2)}, u32[]{:S(2)}) collective-permute-start(bf16[256,256]{1,0:T(8,128)(2,1)S(1)} %get-tuple-element.32), channel_id=1, source_target_pairs={{4,0},{8,4},{12,8},{16,12},{20,16},{24,20},{28,24},{32,28},{36,32}... | collective-permute-start | bytes 393224 | tf_op jit(solution)/shard_map/ppermute | solution.py:311
  16.1 1.4 %collective-permute-start.2 = (bf16[256,256]{1,0:T(8,128)(2,1)S(1)}, bf16[256,256]{1,0:T(8,128)(2,1)S(1)}, u32[]{:S(2)}, u32[]{:S(2)}) collective-permute-start(bf16[256,256]{1,0:T(8,128)(2,1)S(1)} %get-tuple-element.31), channel_id=1, source_target_pairs={{4,0},{0,4},{12,8},{8,12},{20,16},{16,20},{28,24},{24,28},{36,32},... | collective-permute-start | bytes 393224 | tf_op jit(solution)/shard_map/ppermute | solution.py:308
  19.0 17.3 %copy-start.3 = (bf16[2,1,16,16,256]{4,3,2,1,0:T(8,128)(2,1)S(1)}, bf16[2,1,16,16,256]{4,3,2,1,0:T(8,128)(2,1)}, u32[]{:S(2)}) copy-start(bf16[2,1,16,16,256]{4,3,2,1,0:T(8,128)(2,1)} %states_far.1) | copy-start | bytes 786436
  19.0 4.5 %collective-permute-start.4 = (bf16[256,256]{1,0:T(8,128)(2,1)S(1)}, bf16[256,256]{1,0:T(8,128)(2,1)S(1)}, u32[]{:S(2)}, u32[]{:S(2)}) collective-permute-start(bf16[256,256]{1,0:T(8,128)(2,1)S(1)} %get-tuple-element.34), channel_id=1, source_target_pairs={{4,0},{8,4},{12,8},{16,12},{20,16},{24,20},{28,24},{32,28},{36,32}... | collective-permute-start | bytes 393224 | tf_op jit(solution)/shard_map/ppermute | solution.py:311
  25.8 23.6 %all-to-all-start = ((bf16[64,16,128]{2,1,0:T(8,128)(2,1)}), bf16[64,16,128]{2,1,0:T(8,128)(2,1)S(1)}, u32[]{:S(2)}, u32[]{:S(2)}) async-start(bf16[64,16,128]{2,1,0:T(8,128)(2,1)} %bitcast.29), calls=%async_computation | async-start | bytes 524288 | tf_op jit(solution)/shard_map/all_to_all | solution.py:397
  36.3 18.8 %collective-permute-start.5 = (bf16[2,256,256]{2,1,0:T(8,128)(2,1)S(1)}, bf16[2,256,256]{2,1,0:T(8,128)(2,1)}, u32[]{:S(2)}, u32[]{:S(2)}) collective-permute-start(bf16[2,256,256]{2,1,0:T(8,128)(2,1)S(1)} %bitcast.19), channel_id=1, source_target_pairs={{0,2},{1,3},{2,0},{3,1},{4,6},{5,7},{6,4},{7,5},{8,10},{9,11},{10,... | collective-permute-start | bytes 786440 | tf_op jit(solution)/shard_map/ppermute | solution.py:416
  39.3 15.8 %collective-permute-start.6 = (bf16[2,256,256]{2,1,0:T(8,128)(2,1)S(1)}, bf16[2,256,256]{2,1,0:T(8,128)(2,1)}, u32[]{:S(2)}, u32[]{:S(2)}) collective-permute-start(bf16[2,256,256]{2,1,0:T(8,128)(2,1)S(1)} %bitcast.20), channel_id=1, source_target_pairs={{0,3},{1,0},{2,1},{3,2},{4,7},{5,4},{6,5},{7,6},{8,11},{9,8},{10,9... | collective-permute-start | bytes 786440 | tf_op jit(solution)/shard_map/ppermute | solution.py:416
  40.1 15.0 %collective-permute-start.7 = (bf16[2,256,256]{2,1,0:T(8,128)(2,1)S(1)}, bf16[2,256,256]{2,1,0:T(8,128)(2,1)}, u32[]{:S(2)}, u32[]{:S(2)}) collective-permute-start(bf16[2,256,256]{2,1,0:T(8,128)(2,1)S(1)} %bitcast.21), channel_id=1, source_target_pairs={{0,1},{1,2},{2,3},{3,0},{4,5},{5,6},{6,7},{7,4},{8,9},{9,10},{10,1... | collective-permute-start | bytes 786440 | tf_op jit(solution)/shard_map/ppermute | solution.py:416
  50.3 15.8 %all-to-all-start.1 = ((bf16[64,8,128]{2,1,0:T(8,128)(2,1)}), bf16[64,8,128]{2,1,0:T(8,128)(2,1)S(1)}, u32[]{:S(2)}, u32[]{:S(2)}) async-start(bf16[64,8,128]{2,1,0:T(8,128)(2,1)} %scan.1), calls=%async_computation.1 | async-start | bytes 262144 | tf_op jit(solution)/shard_map/all_to_all | solution.py:397
  55.1 16.7 %copy-start.2 = (f32[1,16,16,256]{3,2,1,0:T(8,128)S(1)}, f32[1,16,16,256]{3,2,1,0:T(8,128)}, u32[]{:S(2)}) copy-start(f32[1,16,16,256]{3,2,1,0:T(8,128)} %param.8) | copy-start | bytes 786436
  56.6 1.0 %copy-start = (bf16[2,256,1024]{2,1,0:T(8,128)(2,1)}, bf16[2,256,1024]{2,1,0:T(8,128)(2,1)S(1)}, u32[]{:S(2)}) copy-start(bf16[2,256,1024]{2,1,0:T(8,128)(2,1)S(1)} %turn.1.refs_0_) | copy-start | bytes 3145732
  66.1 8.0 %copy-start.1 = (bf16[2,256,1024]{2,1,0:T(8,128)(2,1)S(1)}, bf16[2,256,1024]{2,1,0:T(8,128)(2,1)}, u32[]{:S(2)}) copy-start(bf16[2,256,1024]{2,1,0:T(8,128)(2,1)} %copy-done) | copy-start | bytes 3145732
  66.7 6.8 %collective-permute-start.10 = (bf16[2,128,128]{2,1,0:T(8,128)(2,1)S(1)}, bf16[2,128,128]{2,1,0:T(8,128)(2,1)S(1)}, u32[]{:S(2)}, u32[]{:S(2)}) collective-permute-start(bf16[2,128,128]{2,1,0:T(8,128)(2,1)S(1)} %get-tuple-element.48), channel_id=1, source_target_pairs={{0,1},{1,2},{2,3},{3,0},{4,5},{5,6},{6,7},{7,4},{8,9},{9,10},{10,1... | collective-permute-start | bytes 196616 | tf_op jit(solution)/shard_map/ppermute | solution.py:434
  68.1 5.5 %collective-permute-start.8 = (bf16[2,128,128]{2,1,0:T(8,128)(2,1)S(1)}, bf16[2,128,128]{2,1,0:T(8,128)(2,1)S(1)}, u32[]{:S(2)}, u32[]{:S(2)}) collective-permute-start(bf16[2,128,128]{2,1,0:T(8,128)(2,1)S(1)} %get-tuple-element.50), channel_id=1, source_target_pairs={{0,2},{1,3},{2,0},{3,1},{4,6},{5,7},{6,4},{7,5},{8,10},{9,11},{10,... | collective-permute-start | bytes 196616 | tf_op jit(solution)/shard_map/ppermute | solution.py:434
  70.7 3.4 %collective-permute-start.9 = (bf16[2,128,128]{2,1,0:T(8,128)(2,1)S(1)}, bf16[2,128,128]{2,1,0:T(8,128)(2,1)S(1)}, u32[]{:S(2)}, u32[]{:S(2)}) collective-permute-start(bf16[2,128,128]{2,1,0:T(8,128)(2,1)S(1)} %get-tuple-element.49), channel_id=1, source_target_pairs={{0,3},{1,0},{2,1},{3,2},{4,7},{5,4},{6,5},{7,6},{8,11},{9,8},{10,9... | collective-permute-start | bytes 196616 | tf_op jit(solution)/shard_map/ppermute | solution.py:434
  71.8 1.0 %copy-start.4 = (f32[256,256]{1,0:T(8,128)S(1)}, f32[256,256]{1,0:T(8,128)}, u32[]{:S(2)}) copy-start(f32[256,256]{1,0:T(8,128)} %get-tuple-element.42.relax_ref) | copy-start | bytes 786436
